TPU v7x, 128 devices: a whole 4x4x4 slice. The times are simulated.
128 devices in a mesh: inst: 16 (over z, y_hi, core), tp: 8 (over x, y_lo).
Axes of the slice: x: 4, y: 4 (y_hi: 2, y_lo: 2; y = y_hi * 2 + y_lo), z: 4, core: 2. Of those that a mesh axis runs over, the one named last changes fastest.
Arguments:
- queries: bfloat16 [4, 64, 8192], P(None, 'inst', 'tp'), may hold values from -240 to 240
- new_kv: bfloat16 [4, 64, 8, 256], P(None, 'inst', 'tp'), may hold values from -6 to 6
- kv_pool: bfloat16 [1536, 128, 8, 256], P('inst', None, 'tp'), may hold values from -6 to 6
- out_weight: bfloat16 [8192, 8192], P('tp'), may hold values from -0.0625 to 0.0625
- send_block: int32 [256], P('inst'), may hold values from 0 to 95, as said below
- send_dest: int32 [256], P('inst'), may hold values from 0 to 15, as said below
- block_table: int32 [64, 16], P('inst'), may hold values from 0 to 127, as said below
- cache_len: int32 [64], P('inst'), may hold values from 1 to 2048, as said below
Outputs:
- projected: bfloat16 [4, 64, 8192], P(None, 'inst', 'tp')
Inputs may be any that keep to these rules, and one draw needn't show every extreme that they name: `send_dest`: no entry of one instance's list names an instance more than 2 times; one instance is named exactly 2 times in every instance's list. `send_block`: the blocks of one instance's list are distinct. `block_table`: ids below 96 are own blocks that the instance did not send; an id 96 + s * 2 + r names only a block that instance s really sends to it; ids of one instance are distinct, and every arrived block is named. `cache_len`: on every instance one request holds 2048 tokens.
All inputs are finite; a program needn't handle non-finite values.
Results may differ from a plain program's by a relative error of at most 0.0049.
Values may be sent and summed in bfloat16 or wider, within the bound.
No kernel may reach another device: no remote copies, remote signals or barrier semaphores. Data moves between devices by JAX's collectives and lax.ppermute only.
A program may use at most 128 MiB of HBM per device.

v0:
```python
import jax
import jax.numpy as jnp
from jax import lax
from jax.sharding import PartitionSpec as P

CAP = 2


def partial_terms(query_heads, keys_values, is_valid, score_scale):
    head_size = keys_values.shape[-1] // 2
    scores = (
        jnp.einsum(
            "tkgd,lkd->tkgl",
            query_heads,
            keys_values[..., :head_size],
            preferred_element_type=jnp.float32,
        )
        * score_scale
    )
    scores = jnp.where(is_valid, scores, -1e30)
    peak_value = jnp.max(scores, axis=-1)
    weights = jnp.where(is_valid, jnp.exp(scores - peak_value[..., None]), 0.0)
    weight_sum = jnp.sum(weights, axis=-1)
    value_sum = jnp.einsum(
        "tkgl,lkd->tkgd",
        weights,
        keys_values[..., head_size:].astype(jnp.float32),
        precision=lax.Precision.HIGHEST,
    )
    return (peak_value, weight_sum, value_sum)


def shards(queries, new_kv, kv_pool, out_weight, send_block, send_dest, block_table, cache_len):
    n_inst = lax.axis_size("inst")
    num_steps, num_slots, head_width = queries.shape
    pool_size, block_len, kv_dev, pair_width = kv_pool.shape
    head_size = pair_width // 2
    head_group = head_width // (kv_dev * head_size)
    blk_count = block_table.shape[1]
    arrivals = n_inst * CAP
    score_scale = head_size ** (-0.5)
    grouped = queries.reshape(num_steps, num_slots, kv_dev, head_group, head_size)
    owners = jnp.arange(n_inst, dtype=jnp.int32)
    is_target = send_dest[None, :] == owners[:, None]
    target_rank = jnp.cumsum(is_target.astype(jnp.int32), axis=1) - 1
    rank_match = is_target[:, :, None] & (
        target_rank[:, :, None] == jnp.arange(CAP, dtype=jnp.int32)[None, None, :]
    )
    picked = jnp.sum(jnp.where(rank_match, send_block[None, :, None], 0), axis=1).reshape(-1)
    outgoing = kv_pool[picked]
    arrival_ids = pool_size + jnp.arange(arrivals, dtype=jnp.int32)
    refers = block_table[:, :, None] == arrival_ids[None, None, :]
    block_starts = jnp.arange(blk_count, dtype=jnp.int32) * block_len
    block_room = jnp.clip(cache_len[:, None] - block_starts[None, :], 0, block_len)
    arrival_count = jnp.sum(jnp.where(refers, block_room[:, :, None], 0), axis=(0, 1))
    slot_ids = jnp.arange(num_slots, dtype=jnp.int32)
    owner_slot = jnp.sum(jnp.where(refers, slot_ids[:, None, None], 0), axis=(0, 1))
    slot_uses = jnp.any(refers, axis=1)
    is_used = jnp.any(slot_uses, axis=0)
    arrive_query = jnp.transpose(grouped[:, owner_slot], (1, 0, 2, 3, 4))

    def block_terms(query_heads, keys_values, live_count):
        return partial_terms(
            query_heads,
            keys_values,
            jnp.arange(block_len, dtype=jnp.int32) < live_count,
            score_scale,
        )

    moved = lax.all_to_all(
        outgoing.reshape(n_inst, CAP, block_len, kv_dev, pair_width),
        "inst",
        split_axis=0,
        concat_axis=0,
        tiled=True,
    )
    moved = moved.reshape(arrivals, block_len, kv_dev, pair_width)
    arrive_peak, arrive_sum, arrive_values = jax.vmap(block_terms)(
        arrive_query, moved, arrival_count
    )

    def resident(inputs):
        query_heads, table_row, row_length = inputs
        safe_ids = jnp.clip(table_row, 0, pool_size - 1)
        gathered = kv_pool[safe_ids].reshape(blk_count * block_len, kv_dev, pair_width)
        positions = jnp.arange(blk_count * block_len, dtype=jnp.int32)
        is_valid = (positions < row_length) & jnp.repeat(table_row < pool_size, block_len)
        return partial_terms(query_heads, gathered, is_valid, score_scale)

    slot_query = jnp.transpose(grouped, (1, 0, 2, 3, 4))
    own_peak, own_sum, own_values = lax.map(resident, (slot_query, block_table, cache_len))
    new_scores = (
        jnp.einsum(
            "tskgd,uskd->stkgu",
            grouped,
            new_kv[..., :head_size],
            preferred_element_type=jnp.float32,
        )
        * score_scale
    )
    causal = (
        jnp.arange(num_steps, dtype=jnp.int32)[:, None]
        >= jnp.arange(num_steps, dtype=jnp.int32)[None, :]
    )
    causal = causal[None, :, None, None, :]
    new_scores = jnp.where(causal, new_scores, -1e30)
    new_peak = jnp.max(new_scores, axis=-1)
    new_weights = jnp.where(causal, jnp.exp(new_scores - new_peak[..., None]), 0.0)
    new_sum = jnp.sum(new_weights, axis=-1)
    new_values = jnp.einsum(
        "stkgu,uskd->stkgd",
        new_weights,
        new_kv[..., head_size:].astype(jnp.float32),
        precision=lax.Precision.HIGHEST,
    )
    slot_mask = slot_uses[:, :, None, None, None]
    arrive_best = jnp.max(jnp.where(slot_mask, arrive_peak[None], -1e30), axis=1)
    overall = jnp.maximum(jnp.maximum(own_peak, new_peak), arrive_best)
    arrive_factor = jnp.where(
        is_used[:, None, None, None], jnp.exp(arrive_peak - overall[owner_slot]), 0.0
    )
    own_factor = jnp.exp(own_peak - overall)
    new_factor = jnp.exp(new_peak - overall)
    weight_total = own_sum * own_factor + new_sum * new_factor
    weight_total = weight_total + jnp.sum(
        jnp.where(slot_mask, (arrive_sum * arrive_factor)[None], 0.0), axis=1
    )
    value_total = own_values * own_factor[..., None] + new_values * new_factor[..., None]
    value_total = value_total + jnp.sum(
        jnp.where(slot_mask[..., None], (arrive_values * arrive_factor[..., None])[None], 0.0),
        axis=1,
    )
    attended = value_total / weight_total[..., None]
    attended = (
        jnp.transpose(attended, (1, 0, 2, 3, 4))
        .reshape(num_steps * num_slots, head_width)
        .astype(jnp.bfloat16)
    )
    partial_out = jnp.dot(attended, out_weight, preferred_element_type=jnp.float32).reshape(
        num_steps, num_slots, -1
    )
    return lax.psum_scatter(partial_out, "tp", scatter_dimension=2, tiled=True).astype(jnp.bfloat16)


def solution(mesh):
    return jax.shard_map(
        shards,
        mesh=mesh,
        in_specs=(
            P(None, "inst", "tp"),
            P(None, "inst", "tp", None),
            P("inst", None, "tp", None),
            P("tp", None),
            P("inst"),
            P("inst"),
            P("inst", None),
            P("inst"),
        ),
        out_specs=P(None, "inst", "tp"),
        check_vma=False,
    )
```

profile of v0, /device:TPU:0, one launch (start us, length us, event | category | flops | bytes accessed | tf_op | source)
XLA Modules:
  0.0 185.4 jit_solution(7886098905103628144)
XLA Ops:
  6.5 0.7 iota_compare_fusion.3
  7.2 0.2 reduce_window_sum.11
  7.4 0.8 select_reduce_fusion.3
  8.1 0.1 copy.40
  8.2 0.1 reshape.328
  8.3 4.8 %gather_fusion.1 = bf16[32,128,256]{2,1,0:T(8,128)(2,1)} fusion(bf16[96,128,256]{2,1,0:T(8,128)(2,1)} %bitcast.243, s32[1024]{0:T(1024)S(1)} %pad_clamp_fusion.2), kind=kCustom, calls=%fused_computation.1 | custom fusion | bytes 4194432 | tf_op jit(solution)/shard_map/gather | solution.py:50
  13.2 8.3 %all-to-all-start = ((bf16[16,2,128,1,256]{4,2,1,3,0:T(8,128)(2,1)}), bf16[16,2,128,1,256]{4,2,1,3,0:T(8,128)(2,1)S(1)}, u32[]{:S(2)}, u32[]{:S(2)}) async-start(bf16[16,2,128,1,256]{4,2,1,3,0:T(8,128)(2,1)} %bitcast.32), calls=%async_computation | async-start | bytes 4194304 | tf_op jit(solution)/shard_map/all_to_all | solution.py:70
  21.4 0.0 reduce-scatter.4.cloned.1.call-start
  21.5 0.0 copy-done
  21.6 0.0 copy-done.2
  21.6 0.0 copy-done.3
  21.6 0.0 copy-start.1
  21.6 23.0 %while.14 = (s32[]{:T(128)}, f32[4,4,1,8]{3,1,2,0:T(4,128)S(1)}, f32[4,4,1,8]{3,1,2,0:T(4,128)S(1)}, f32[4,4,1,8,128]{4,3,1,2,0:T(8,128)S(1)}, s32[4]{0:T(128)S(...) while((s32[]{:T(128)}, f32[4,4,1,8]{3,1,2,0:T(4,128)S(1)}, ...), condition=%wide.region_3.4_spmd, body=%wide.region_0.3_spmd.sunk | while | flops 117969936 | bytes 3980137 | solution.py:91
  21.6 0.6 dynamic_slice.30
  22.2 0.7 fusion.71
  22.9 3.4 %gather_fusion = bf16[16,128,256]{2,1,0:T(8,128)(2,1)S(1)} fusion(bf16[96,128,256]{2,1,0:T(8,128)(2,1)} %bitcast.244, s32[1024]{0:T(1024)S(1)} %pad_clamp_fusion.4), kind=kCustom, calls=%fused_computation.clone.1 | custom fusion | bytes 2097216 | tf_op jit(solution)/shard_map/while/body/eval_jaxpr/gather | solution.py:85
  26.3 0.4 fusion.72
  26.7 0.4 fusion.74
  27.1 0.2 fusion.73
  27.4 0.6 dynamic_slice.30
  28.0 0.7 fusion.71
  28.7 3.4 %gather_fusion = bf16[16,128,256]{2,1,0:T(8,128)(2,1)S(1)} fusion(bf16[96,128,256]{2,1,0:T(8,128)(2,1)} %bitcast.244, s32[1024]{0:T(1024)S(1)} %pad_clamp_fusion.4), kind=kCustom, calls=%fused_computation.clone.1 | custom fusion | bytes 2097216 | tf_op jit(solution)/shard_map/while/body/eval_jaxpr/gather | solution.py:85
  32.1 0.4 fusion.72
  32.4 0.4 fusion.74
  32.9 0.2 fusion.73
  33.1 0.6 dynamic_slice.30
  33.7 0.7 fusion.71
  34.4 3.4 %gather_fusion = bf16[16,128,256]{2,1,0:T(8,128)(2,1)S(1)} fusion(bf16[96,128,256]{2,1,0:T(8,128)(2,1)} %bitcast.244, s32[1024]{0:T(1024)S(1)} %pad_clamp_fusion.4), kind=kCustom, calls=%fused_computation.clone.1 | custom fusion | bytes 2097216 | tf_op jit(solution)/shard_map/while/body/eval_jaxpr/gather | solution.py:85
  37.8 0.4 fusion.72
  38.2 0.4 fusion.74
  38.6 0.2 fusion.73
  38.8 0.6 dynamic_slice.30
  39.4 0.7 fusion.71
  40.1 3.4 %gather_fusion = bf16[16,128,256]{2,1,0:T(8,128)(2,1)S(1)} fusion(bf16[96,128,256]{2,1,0:T(8,128)(2,1)} %bitcast.244, s32[1024]{0:T(1024)S(1)} %pad_clamp_fusion.4), kind=kCustom, calls=%fused_computation.clone.1 | custom fusion | bytes 2097216 | tf_op jit(solution)/shard_map/while/body/eval_jaxpr/gather | solution.py:85
  43.6 0.4 fusion.72
  43.9 0.4 fusion.74
  44.3 0.2 fusion.73
  44.6 0.1 subtract_clamp_fusion
  44.7 0.1 fusion.36
  44.8 0.6 gather_fusion.2
  45.4 0.1 compare_reduce_fusion
  45.5 0.0 copy-done.1
  45.6 0.3 fusion.61
  45.8 0.1 fusion.41
  45.9 0.1 iota_compare_fusion.2
  46.0 4.7 %all-to-all-done = bf16[16,2,128,1,256]{4,2,1,3,0:T(8,128)(2,1)S(1)} async-done(((bf16[16,2,128,1,256]{4,2,1,3,0:T(8,128)(2,1)}), bf16[16,2,128,1,256]{4,2,1,3,0:T(8,128)(2,1)S(1)}, u32[]{:S(2)}, u32[]{:S(2)}) %all-to-all-start) | async-done | bytes 2097184 | tf_op jit(solution)/shard_map/all_to_all | solution.py:70
  50.7 0.8 fusion.60
  51.5 0.1 copy.41
  51.6 0.1 select_reduce_fusion.2
  51.7 0.6 gather_fusion.3
  52.3 0.4 fusion.32
  52.8 0.1 fusion.57
  52.9 1.0 fusion.19
  53.9 0.2 select_reduce_fusion
  54.2 0.1 copy.46
  54.2 0.1 select_reduce_fusion.1
  54.4 0.3 fusion.28
  54.7 8.2 %fusion.15 = f32[4,4,8192]{2,1,0:T(4,128)S(1)} fusion(bf16[1024,8192]{1,0:T(8,128)(2,1)} %param.13, bf16[4,4,1024]{2,0,1:T(4,128)(2,1)S(1)} %convert_element_type.26), kind=kOutput, calls=%fused_computation.31 | convolution fusion | flops 268435456 | bytes 17334272 | tf_op jit(solution)/shard_map/dot_general | solution.py:139
  62.9 10.8 %copy.53 = f32[4,4,8192]{1,0,2:T(4,128)} copy(f32[4,4,8192]{2,1,0:T(4,128)S(1)} %fusion.15) | data formatting | bytes 1048576
  73.7 13.5 %reshape.389 = f32[8192,16]{1,0:T(8,128)} reshape(f32[8192,4,4]{2,1,0:T(4,128)} %bitcast.240) | data formatting | bytes 1048576
  87.2 0.0 reduce-scatter.4.cloned.1.call-update
  87.2 88.0 %reduce-scatter.4.cloned.1.call-done = f32[1024,16]{1,0:T(8,128)} async-done(((f32[8192,16]{1,0:T(8,128)}), f32[1024,16]{1,0:T(8,128)}) %reduce-scatter.4.cloned.1.call-update) | async-done | bytes 65552
  175.2 2.1 %reshape.390 = bf16[1024,4,4]{2,1,0:T(4,128)(2,1)S(1)} reshape(f32[1024,16]{1,0:T(8,128)} %reduce-scatter.4.cloned.1.call-done) | data formatting | bytes 98304
  177.3 1.3 copy.54
  (37 shorter events, 0.3 us)
Async XLA Ops:
  13.2 8.4 %copy-start = (bf16[4,4,1024]{2,1,0:T(4,128)(2,1)S(1)}, bf16[4,4,1024]{2,1,0:T(4,128)(2,1)}, u32[]{:S(2)}) copy-start(bf16[4,4,1024]{2,1,0:T(4,128)(2,1)} %param.10) | copy-start | bytes 98308
  13.2 8.4 %copy-start.2 = (s32[4,16]{1,0:T(4,128)S(1)}, s32[4,16]{1,0:T(4,128)}, u32[]{:S(2)}) copy-start(s32[4,16]{1,0:T(4,128)} %param.16) | copy-start | bytes 772
  13.2 8.4 %copy-start.3 = (s32[4]{0:T(128)S(1)}, s32[4]{0:T(128)}, u32[]{:S(2)}) copy-start(s32[4]{0:T(128)} %param.17) | copy-start | bytes 52
  13.2 37.6 %all-to-all-start = ((bf16[16,2,128,1,256]{4,2,1,3,0:T(8,128)(2,1)}), bf16[16,2,128,1,256]{4,2,1,3,0:T(8,128)(2,1)S(1)}, u32[]{:S(2)}, u32[]{:S(2)}) async-start(bf16[16,2,128,1,256]{4,2,1,3,0:T(8,128)(2,1)} %bitcast.32), calls=%async_computation | async-start | bytes 4194304 | tf_op jit(solution)/shard_map/all_to_all | solution.py:70
  21.4 153.7 %reduce-scatter.4.cloned.1.call-start = ((), (), s32[]{:S(2)}) async-start(), calls=%async_computation.2 | async-start | bytes 4718592
  21.6 24.0 %copy-start.1 = (bf16[4,4,1,256]{3,1,2,0:T(4,128)(2,1)S(1)}, bf16[4,4,1,256]{3,1,2,0:T(4,128)(2,1)}, u32[]{:S(2)}) copy-start(bf16[4,4,1,256]{3,1,2,0:T(4,128)(2,1)} %param.11) | copy-start | bytes 24580
Sparse Core Ops, SparseCore 0:
  87.3 87.8 reduce-scatter.3
where the time goes:
time: 187 us; the launch traced here: 185 us
  waiting for transfers between devices  92.7 us (50%)
  local copies, waits for them, and re-layouts  50.1 us (27%)
  matrix products  13.7 us (7%)
  between operations  13.6 us (7%)
  starting transfers between devices  8.3 us (4%)
  other arithmetic  6.8 us (4%)
    unnamed x2, waiting for transfers between devices  88 us
    unnamed x12, local copies, waits for them, and re-layouts  27.6 us
    gather x4, local copies, waits for them, and re-layouts, resident(): kv_pool[safe_ids].reshape(blk_count * block_len, kv_dev, pair_width)  13.6 us
    all_to_all x1, starting transfers between devices, shards(): lax.all_to_all(outgoing.reshape(n_inst, CAP, block_len, kv_dev, pair_widt...  8.26 us
    dot_general x1, matrix products, shards(): jnp.dot(attended, out_weight, preferred_element_type=jnp.float32)  8.19 us
    gather x1, local copies, waits for them, and re-layouts, shards(): outgoing = kv_pool[picked]  4.82 us
    all_to_all x1, waiting for transfers between devices, shards(): lax.all_to_all(outgoing.reshape(n_inst, CAP, block_len, kv_dev, pair_widt...  4.72 us
  transfers between devices with their start and end apart: 2, of which 2 were waited for; matrix products, arithmetic and copies ran while one was open for 13% of the time, Pallas kernels for 0%

commit v1 on v0

v1 whole, which is shorter than its diff:
```python
import functools

import jax
import jax.numpy as jnp
from jax import lax
from jax.experimental import pallas as pl
from jax.experimental.pallas import tpu as pltpu
from jax.sharding import PartitionSpec as P

CAP = 2
INFO = 16
MASKED = -1e30
VMEM_BYTES = 40 * 1024 * 1024

SMEM = pl.BlockSpec(memory_space=pltpu.SMEM)
VMEM = pl.BlockSpec(memory_space=pltpu.VMEM)
HBM = pl.BlockSpec(memory_space=pl.ANY)

nt_dims = (((1,), (1,)), ((), ()))


def split_dot(weights, values):
    rows = weights.shape[0]
    high = weights.astype(jnp.bfloat16)
    low = (weights - high.astype(jnp.float32)).astype(jnp.bfloat16)
    both = jnp.dot(
        jnp.concatenate([high, low], axis=0), values, preferred_element_type=jnp.float32
    )
    return both[:rows] + both[rows:]


def ask_kernel(pool_size, block_len, table_ref, len_ref, q_ref, out_ref, slot_ref, live_ref):
    slots, blocks = table_ref.shape
    rows = q_ref.shape[1]
    n_inst = out_ref.shape[0]

    def clear(a, carry):
        slot_ref[a] = -1
        live_ref[a] = 0
        return carry

    lax.fori_loop(0, n_inst * CAP, clear, 0)
    for slot in range(slots):
        query = q_ref[slot]

        def entry(b, carry):
            block_id = table_ref[slot, b]

            @pl.when(block_id >= pool_size)
            def _():
                arrival = block_id - pool_size
                source = arrival // CAP
                start = pl.multiple_of((arrival % CAP) * rows, rows)
                out_ref[source, pl.ds(start, rows), :] = query
                slot_ref[arrival] = slot
                live_ref[arrival] = jnp.clip(len_ref[slot] - b * block_len, 0, block_len)

            return carry

        lax.fori_loop(0, blocks, entry, 0)
    row = lax.broadcasted_iota(jnp.int32, (INFO, 128), 0)

    def info(source, carry):
        live = jnp.where(row < INFO // 2, live_ref[source * CAP], live_ref[source * CAP + 1])
        out_ref[source, CAP * rows :, :] = live.astype(jnp.float32).astype(jnp.bfloat16)
        return carry

    lax.fori_loop(0, n_inst, info, 0)


def own_kernel(
    scale, head_group, table_ref, len_ref, q_ref, new_ref, pool_ref,
    peak_ref, sum_ref, acc_ref, kv_ref, sems,
):
    slots, blocks = table_ref.shape
    pool_size, block_len, _ = pool_ref.shape
    rows = q_ref.shape[1]
    steps = new_ref.shape[0]
    head = q_ref.shape[2]
    span = blocks * block_len

    def copy(slot, b):
        block_id = jnp.minimum(table_ref[slot, b], pool_size - 1)
        return pltpu.make_async_copy(
            pool_ref.at[block_id],
            kv_ref.at[slot, pl.ds(b * block_len, block_len), :],
            sems.at[slot, b],
        )

    for slot in range(slots):
        for b in range(blocks):
            copy(slot, b).start()
    lane = lax.broadcasted_iota(jnp.int32, (rows, block_len), 1)
    step = lax.broadcasted_iota(jnp.int32, (rows, block_len), 0) // head_group
    for slot in range(slots):
        fresh = jnp.concatenate(
            [new_ref[u, slot : slot + 1, :].astype(jnp.float32) for u in range(steps)]
            + [jnp.zeros((block_len - steps, 2 * head), jnp.float32)],
            axis=0,
        )
        kv_ref[slot, span:, :] = fresh.astype(jnp.bfloat16)
    for slot in range(slots):
        for b in range(blocks):
            copy(slot, b).wait()
        scores = lax.dot_general(
            q_ref[slot], kv_ref[slot, :, :head], nt_dims, preferred_element_type=jnp.float32
        ) * scale
        parts = []
        for b in range(blocks):
            live = jnp.clip(len_ref[slot] - b * block_len, 0, block_len)
            live = jnp.where(table_ref[slot, b] < pool_size, live, 0)
            part = scores[:, b * block_len : (b + 1) * block_len]
            parts.append(jnp.where(lane < live, part, MASKED))
        parts.append(jnp.where((lane <= step) & (lane < steps), scores[:, span:], MASKED))
        peaks = functools.reduce(jnp.maximum, parts)
        peak = jnp.max(peaks, axis=1, keepdims=True)
        weights = [jnp.exp(part - peak) for part in parts]
        total = jnp.sum(functools.reduce(jnp.add, weights), axis=1, keepdims=True)
        acc_ref[slot] = split_dot(jnp.concatenate(weights, axis=1), kv_ref[slot, :, head:])
        peak_ref[slot] = jnp.broadcast_to(peak, (rows, head))
        sum_ref[slot] = jnp.broadcast_to(total, (rows, head))


def split_rows(row, values):
    high = values.astype(jnp.bfloat16).astype(jnp.float32)
    rest = values - high
    middle = rest.astype(jnp.bfloat16).astype(jnp.float32)
    return high, middle, rest - middle


def answer_kernel(
    scale, block_ref, dest_ref, asked_ref, pool_ref, out_ref, kv_ref, peak_ref, sum_ref, seen_ref, sems
):
    pool_size, block_len, width = pool_ref.shape
    head = width // 2
    n_inst = out_ref.shape[0]
    rows = (out_ref.shape[1] - INFO) // CAP
    entries = block_ref.shape[0]

    def copy(e):
        block_id = jnp.clip(block_ref[e], 0, pool_size - 1)
        return pltpu.make_async_copy(pool_ref.at[block_id], kv_ref.at[e], sems.at[e])

    for e in range(entries):
        copy(e).start()
    for i in range(n_inst):
        seen_ref[i] = 0
    peak_ref[...] = jnp.zeros_like(peak_ref)
    sum_ref[...] = jnp.zeros_like(sum_ref)
    lane = lax.broadcasted_iota(jnp.int32, (rows, block_len), 1)
    row = lax.broadcasted_iota(jnp.int32, (rows, block_len), 0)
    for e in range(entries):
        dest = jnp.clip(dest_ref[e], 0, n_inst - 1)
        rank = jnp.minimum(seen_ref[dest], CAP - 1)
        seen_ref[dest] = seen_ref[dest] + 1
        start = pl.multiple_of(rank * rows, rows)
        copy(e).wait()
        query = asked_ref[dest, pl.ds(start, rows), :]
        info = asked_ref[dest, CAP * rows :, :].astype(jnp.float32)
        live = jnp.where(rank == 0, info[0:1], info[INFO // 2 : INFO // 2 + 1])
        scores = lax.dot_general(
            query, kv_ref[e, :, :head], nt_dims, preferred_element_type=jnp.float32
        ) * scale
        scores = jnp.where(lane.astype(jnp.float32) < live, scores, MASKED)
        peak = jnp.max(scores, axis=1, keepdims=True)
        weights = jnp.where(lane.astype(jnp.float32) < live, jnp.exp(scores - peak), 0.0)
        total = jnp.sum(weights, axis=1, keepdims=True)
        values = split_dot(weights, kv_ref[e, :, head:])
        values = values / jnp.where(total > 0.0, total, 1.0)
        out_ref[dest, pl.ds(start, rows), :] = values.astype(jnp.bfloat16)
        here = lane == row + start
        peak_ref[pl.ds(dest, 1), :] += jnp.sum(jnp.where(here, peak, 0.0), axis=0, keepdims=True)
        sum_ref[pl.ds(dest, 1), :] += jnp.sum(jnp.where(here, total, 0.0), axis=0, keepdims=True)
    row = lax.broadcasted_iota(jnp.int32, (INFO, block_len), 0)
    peaks = split_rows(row, peak_ref[...])
    sums = split_rows(row, sum_ref[...])
    for i in range(n_inst):
        info = jnp.zeros((INFO, block_len), jnp.float32)
        for k, term in enumerate(peaks + sums):
            info = jnp.where(row == k, term[i : i + 1], info)
        out_ref[i, CAP * rows :, :] = info.astype(jnp.bfloat16)


def project_kernel(
    slot_ref, back_ref, peak_ref, sum_ref, acc_ref, weight_ref, out_ref,
    m_ref, l_ref, a_ref, att_ref, w_ref, sems,
):
    slots, rows, head = acc_ref.shape
    n_inst = back_ref.shape[0]
    parts, out_rows, part_cols = out_ref.shape
    steps = out_rows // slots
    group = rows // steps

    def copy(c):
        return pltpu.make_async_copy(
            weight_ref.at[:, pl.ds(c * part_cols, part_cols)], w_ref.at[c], sems.at[c]
        )

    for c in range(parts):
        copy(c).start()
    m_ref[...] = peak_ref[...]
    l_ref[...] = sum_ref[...]
    a_ref[...] = acc_ref[...]
    lane = lax.broadcasted_iota(jnp.int32, (rows, head), 1)
    row = lax.broadcasted_iota(jnp.int32, (rows, head), 0)

    def source(s, carry):
        info = back_ref[s, CAP * rows :, :].astype(jnp.float32)
        peaks = info[0:1] + info[1:2] + info[2:3]
        sums = info[3:4] + info[4:5] + info[5:6]
        for r in range(CAP):
            slot = slot_ref[s * CAP + r]

            @pl.when(slot >= 0)
            def _():
                here = lane == row + r * rows
                peak = jnp.sum(jnp.where(here, peaks, 0.0), axis=1, keepdims=True)
                total = jnp.sum(jnp.where(here, sums, 0.0), axis=1, keepdims=True)
                values = back_ref[s, r * rows : (r + 1) * rows, :].astype(jnp.float32)
                old = m_ref[slot]
                new = jnp.maximum(old, peak)
                keep = jnp.exp(old - new)
                gain = jnp.exp(peak - new) * total
                m_ref[slot] = new
                l_ref[slot] = l_ref[slot] * keep + gain
                a_ref[slot] = a_ref[slot] * keep + gain * values

        return carry

    lax.fori_loop(0, n_inst, source, 0)
    for slot in range(slots):
        done = a_ref[slot] / l_ref[slot]
        for step in range(steps):
            for g in range(group):
                at = step * group + g
                att_ref[step * slots + slot : step * slots + slot + 1, g * head : (g + 1) * head] = (
                    done[at : at + 1]
                )
    attended = att_ref[...].astype(jnp.bfloat16)
    for c in range(parts):
        copy(c).wait()
        out_ref[c] = jnp.dot(
            attended, w_ref[c], preferred_element_type=jnp.float32
        ).astype(jnp.bfloat16)


def params():
    return pltpu.CompilerParams(vmem_limit_bytes=VMEM_BYTES)


def shards(queries, new_kv, kv_pool, out_weight, send_block, send_dest, block_table, cache_len):
    n_inst = lax.axis_size("inst")
    n_tp = lax.axis_size("tp")
    steps, slots, head_width = queries.shape
    pool_size, block_len, _, width = kv_pool.shape
    head = width // 2
    group = head_width // head
    rows = steps * group
    blocks = block_table.shape[1]
    entries = send_block.shape[0]
    columns = out_weight.shape[1]
    scale = head ** (-0.5)
    f32, bf16 = jnp.float32, jnp.bfloat16
    pool = kv_pool.reshape(pool_size, block_len, width)
    fresh = new_kv.reshape(steps, slots, width)
    slot_query = jnp.transpose(
        queries.reshape(steps, slots, group, head), (1, 0, 2, 3)
    ).reshape(slots, rows, head)

    packet = jax.ShapeDtypeStruct((n_inst, CAP * rows + INFO, head), bf16)
    ask, slot_of = pl.pallas_call(
        functools.partial(ask_kernel, pool_size, block_len),
        out_shape=(packet, jax.ShapeDtypeStruct((n_inst * CAP,), jnp.int32)),
        in_specs=[SMEM, SMEM, VMEM],
        out_specs=(VMEM, SMEM),
        scratch_shapes=[pltpu.SMEM((n_inst * CAP,), jnp.int32)],
        compiler_params=params(),
        name="ask",
    )(block_table, cache_len, slot_query)
    asked = lax.all_to_all(ask, "inst", 0, 0, tiled=True)

    own = jax.ShapeDtypeStruct((slots, rows, head), f32)
    own_peak, own_sum, own_acc = pl.pallas_call(
        functools.partial(own_kernel, scale, group),
        out_shape=(own, own, own),
        in_specs=[SMEM, SMEM, VMEM, VMEM, HBM],
        out_specs=(VMEM, VMEM, VMEM),
        scratch_shapes=[
            pltpu.VMEM((slots, (blocks + 1) * block_len, width), bf16),
            pltpu.SemaphoreType.DMA((slots, blocks)),
        ],
        compiler_params=params(),
        cost_estimate=pl.CostEstimate(
            flops=4 * slots * rows * blocks * block_len * width,
            bytes_accessed=slots * blocks * block_len * width * 2,
            transcendentals=slots * rows * blocks * block_len,
        ),
        name="own",
    )(block_table, cache_len, slot_query, fresh, pool)

    answer = pl.pallas_call(
        functools.partial(answer_kernel, scale),
        out_shape=packet,
        in_specs=[SMEM, SMEM, VMEM, HBM],
        out_specs=VMEM,
        scratch_shapes=[
            pltpu.VMEM((entries, block_len, width), bf16),
            pltpu.VMEM((n_inst, head), f32),
            pltpu.VMEM((n_inst, head), f32),
            pltpu.SMEM((n_inst,), jnp.int32),
            pltpu.SemaphoreType.DMA((entries,)),
        ],
        compiler_params=params(),
        name="answer",
    )(send_block, send_dest, asked, pool)
    back = lax.all_to_all(answer, "inst", 0, 0, tiled=True)

    out_rows = steps * slots
    partial_out = pl.pallas_call(
        project_kernel,
        out_shape=jax.ShapeDtypeStruct((n_tp, out_rows, columns // n_tp), bf16),
        in_specs=[SMEM, VMEM, VMEM, VMEM, VMEM, HBM],
        out_specs=VMEM,
        scratch_shapes=[
            pltpu.VMEM((slots, rows, head), f32),
            pltpu.VMEM((slots, rows, head), f32),
            pltpu.VMEM((slots, rows, head), f32),
            pltpu.VMEM((out_rows, head_width), f32),
            pltpu.VMEM((n_tp, head_width, columns // n_tp), bf16),
            pltpu.SemaphoreType.DMA((n_tp,)),
        ],
        compiler_params=params(),
        name="project",
    )(slot_of, back, own_peak, own_sum, own_acc, out_weight)
    shares = lax.all_to_all(partial_out, "tp", 0, 0, tiled=True)
    total = jnp.sum(shares.astype(f32), axis=0).astype(bf16)
    return total.reshape(steps, slots, columns // n_tp)


def solution(mesh):
    return jax.shard_map(
        shards,
        mesh=mesh,
        in_specs=(
            P(None, "inst", "tp"),
            P(None, "inst", "tp", None),
            P("inst", None, "tp", None),
            P("tp", None),
            P("inst"),
            P("inst"),
            P("inst", None),
            P("inst"),
        ),
        out_specs=P(None, "inst", "tp"),
        check_vma=False,
    )
```

time: 187 us -> 73.8 us (0.39)
  waiting for transfers between devices: 92.7 us -> 0.01 us
  local copies, waits for them, and re-layouts: 50.1 us -> 11.7 us
  blocking collectives: 0 us -> 29.8 us
  Pallas kernels: 0 us -> 27.6 us
  matrix products: 13.7 us -> 0 us
  between operations: 13.6 us -> 0.08 us
  other arithmetic: 6.8 us -> 0.04 us
  starting transfers between devices: 8.3 us -> 3.55 us
    unnamed x2 -> x0, waiting for transfers between devices: 88 us -> none
    all_to_all x0 -> x2, blocking collectives: none -> 29.8 us  [the longest x1 18.2 us: shards(): asked = lax.all_to_all(ask, 'inst', 0, 0, tiled=True)]
    pallas_call x0 -> x4, Pallas kernels: none -> 27.6 us  [the longest x1 9.51 us: shards(): pl.pallas_call(functools.partial(own_kernel, scale, group), out_shape=(ow...]
    gather x7 -> x0, local copies, waits for them, and re-layouts: 19.7 us -> none  [the longest x4 13.6 us: resident(): kv_pool[safe_ids].reshape(blk_count * block_len, kv_dev, pair_width)]
    unnamed x12 -> x18, local copies, waits for them, and re-layouts: 27.6 us -> 10.2 us
    dot_general x13 -> x0, matrix products: 13.7 us -> none  [the longest x1 8.19 us: shards(): jnp.dot(attended, out_weight, preferred_element_type=jnp.float32)]
    all_to_all x1, waiting for transfers between devices: 4.72 us -> 0.01 us  [shards(): back = lax.all_to_all(answer, 'inst', 0, 0, tiled=True)]
    all_to_all x1, starting transfers between devices: 8.26 us -> 3.55 us  [shards(): back = lax.all_to_all(answer, 'inst', 0, 0, tiled=True)]
  transfers between devices with their start and end apart: 2 -> 1, of which waited for: 2 -> 0; matrix products, arithmetic and copies ran while one was open for 13% -> 0% of each run, Pallas kernels for 0% -> 13%
where the time goes in v1:
time: 73.8 us; the launch traced here: 72.8 us
  blocking collectives  29.8 us (40%)
  Pallas kernels  27.6 us (37%)
  local copies, waits for them, and re-layouts  11.7 us (16%)
  starting transfers between devices  3.55 us (5%)
    all_to_all x1, blocking collectives, shards(): asked = lax.all_to_all(ask, 'inst', 0, 0, tiled=True)  18.2 us
    all_to_all x1, blocking collectives, shards(): shares = lax.all_to_all(partial_out, 'tp', 0, 0, tiled=True)  11.6 us
    unnamed x18, local copies, waits for them, and re-layouts  10.2 us
    pallas_call x1, Pallas kernels, shards(): pl.pallas_call(functools.partial(own_kernel, scale, group), out_shape=(ow...  9.51 us
    pallas_call x1, Pallas kernels, shards(): pl.pallas_call(functools.partial(answer_kernel, scale), out_shape=packet,...  8.65 us
    pallas_call x1, Pallas kernels, shards(): pl.pallas_call(project_kernel, out_shape=jax.ShapeDtypeStruct((n_tp, out_...  6.91 us
    all_to_all x1, starting transfers between devices, shards(): back = lax.all_to_all(answer, 'inst', 0, 0, tiled=True)  3.55 us
    pallas_call x1, Pallas kernels, shards(): pl.pallas_call(functools.partial(ask_kernel, pool_size, block_len), out_s...  2.54 us
  transfers between devices with their start and end apart: 1, of which 0 were waited for; matrix products, arithmetic and copies ran while one was open for 0% of the time, Pallas kernels for 13%

profile of v1, /device:TPU:0, one launch (start us, length us, event | category | flops | bytes accessed | tf_op | source)
XLA Modules:
  0.0 72.8 jit_solution(3701507662174630307)
XLA Ops:
  0.0 0.8 %reshape.15 = bf16[4,4,8,128]{3,2,1,0:T(8,128)(2,1)S(1)} reshape(bf16[4,4,1024]{2,1,0:T(4,128)(2,1)} %param.8) | data formatting | bytes 65536 | tf_op jit(solution)/shard_map/reshape | solution.py:267
  0.8 0.0 copy-start.3
  0.8 0.7 copy-done.3
  1.5 0.0 copy-start.5
  1.5 0.7 copy-done.5
  2.1 2.5 %ask.1 = (bf16[16,80,128]{2,1,0:T(8,128)(2,1)S(1)}, s32[32]{0:T(128)S(1)}) custom-call(s32[4,16]{1,0:T(4,128)S(1)} %copy-done.3, s32[4]{0:T(128)S(1)} %copy-done.5, bf16[4,32,128]{2,1,0:T(8,128)(2,1)S(1)} %bitcast.9), custom_call_target="tpu_custom_call" | custom-call | tf_op jit(solution)/shard_map/ask/pallas_call | solution.py:271
  4.7 18.2 %all_to_all.15.asked_ref = bf16[16,80,128]{2,1,0:T(8,128)(2,1)S(1)} all-to-all(bf16[16,80,128]{2,1,0:T(8,128)(2,1)S(1)} %get-tuple-element.11), channel_id=1, replica_groups=mesh['inst'=16,'tp'=8] {'inst'}, dimensions={0} | all-to-all | bytes 655360 | tf_op jit(solution)/shard_map/all_to_all | solution.py:280
  22.9 0.0 copy-start
  22.9 2.8 %copy-done = bf16[96,128,1,256]{3,1,2,0:T(8,128)(2,1)S(1)} copy-done((bf16[96,128,1,256]{3,1,2,0:T(8,128)(2,1)S(1)}, bf16[96,128,1,256]{3,1,2,0:T(8,128)(2,1)}, u32[]{:S(2)}) %copy-start) | copy-done | bytes 6291480
  25.7 0.0 copy-start.7
  25.7 0.7 copy-done.7
  26.3 0.0 copy-start.8
  26.4 0.7 copy-done.8
  27.0 8.7 %answer.1 = bf16[16,80,128]{2,1,0:T(8,128)(2,1)} custom-call(s32[16]{0:T(128)S(1)} %copy-done.7, s32[16]{0:T(128)S(1)} %copy-done.8, bf16[16,80,128]{2,1,0:T(8,128)(2,1)S(1)} %all_to_all.15.asked_ref, bf16[96,128,256]{2,1,0:T(8,128)(2,1)S(1)} %bitcast.7), custom_call_target="tpu_custom_call" | custom-call | tf_op jit(solution)/shard_map/answer/pallas_call | solution.py:301
  35.7 3.6 %all-to-all-start.1 = ((bf16[16,80,128]{2,1,0:T(8,128)(2,1)}), bf16[16,80,128]{2,1,0:T(8,128)(2,1)S(1)}, u32[]{:S(2)}, u32[]{:S(2)}) async-start(bf16[16,80,128]{2,1,0:T(8,128)(2,1)} %answer.1), calls=%async_computation.1 | async-start | bytes 655360 | tf_op jit(solution)/shard_map/all_to_all | solution.py:316
  39.2 0.0 copy-start.1
  39.2 2.8 %copy-done.1 = bf16[96,128,1,256]{3,1,2,0:T(8,128)(2,1)S(1)} copy-done((bf16[96,128,1,256]{3,1,2,0:T(8,128)(2,1)S(1)}, bf16[96,128,1,256]{3,1,2,0:T(8,128)(2,1)}, u32[]{:S(2)}) %copy-start.1) | copy-done | bytes 6291480
  42.0 0.0 copy-start.2
  42.0 0.7 copy-done.2
  42.7 0.0 copy-start.4
  42.7 0.7 copy-done.4
  43.4 0.0 copy-start.6
  43.4 0.7 copy-done.6
  44.0 9.5 %own.1 = (f32[4,32,128]{2,1,0:T(8,128)S(1)}, f32[4,32,128]{2,1,0:T(8,128)S(1)}, f32[4,32,128]{2,1,0:T(8,128)S(1)}) custom-call(s32[4,16]{1,0:T(4,128)S(1)} %copy-done.4, s32[4]{0:T(128)S(1)} %copy-done.6, bf16[4,32,128]{2,1,0:T(8,128)(2,1)S(1)} %bitcast.10, bf16[4,4,256]{2,1,0:T(4,128)(2,1)S(1)} %bitcast.11, bf16[96,128,256]{2,1,0:T(8,128)(2,1)S(1)} %bitcast.8), custom_call_target="tpu_custom_call" | custom-call | flops 268435456 | bytes 4194304 | tf_op jit(solution)/shard_map/own/pallas_call | solution.py:283
  53.6 0.0 all-to-all-done.1.back_ref
  53.6 6.9 %project.1 = bf16[8,16,1024]{2,1,0:T(8,128)(2,1)S(1)} custom-call(s32[32]{0:T(128)S(1)} %get-tuple-element.10.slot_ref, bf16[16,80,128]{2,1,0:T(8,128)(2,1)S(1)} %all-to-all-done.1.back_ref, f32[4,32,128]{2,1,0:T(8,128)S(1)} %get-tuple-element.12.peak_ref, f32[4,32,128]{2,1,0:T(8,128)S(1)} %get-tuple-element.13.sum_ref, ...), custom_call_target="tpu_custom_call" | custom-call | tf_op jit(solution)/shard_map/project/pallas_call | solution.py:319
  60.5 11.6 %all_to_all.16 = bf16[8,16,1024]{2,1,0:T(8,128)(2,1)S(1)} all-to-all(bf16[8,16,1024]{2,1,0:T(8,128)(2,1)S(1)} %project.1), channel_id=1, replica_groups=mesh['inst'=16,'tp'=8] {'tp'}, dimensions={0} | all-to-all | bytes 524288 | tf_op jit(solution)/shard_map/all_to_all | solution.py:335
  72.1 0.6 reshape.19
  (2 shorter events, 0.0 us)
Async XLA Ops:
  0.8 0.7 copy-start.3
  1.5 0.7 copy-start.5
  22.9 2.8 %copy-start = (bf16[96,128,1,256]{3,1,2,0:T(8,128)(2,1)S(1)}, bf16[96,128,1,256]{3,1,2,0:T(8,128)(2,1)}, u32[]{:S(2)}) copy-start(bf16[96,128,1,256]{3,1,2,0:T(8,128)(2,1)} %param.10) | copy-start | bytes 18874372
  25.7 0.7 copy-start.7
  26.3 0.7 copy-start.8
  35.7 17.9 %all-to-all-start.1 = ((bf16[16,80,128]{2,1,0:T(8,128)(2,1)}), bf16[16,80,128]{2,1,0:T(8,128)(2,1)S(1)}, u32[]{:S(2)}, u32[]{:S(2)}) async-start(bf16[16,80,128]{2,1,0:T(8,128)(2,1)} %answer.1), calls=%async_computation.1 | async-start | bytes 655360 | tf_op jit(solution)/shard_map/all_to_all | solution.py:316
  39.2 2.8 %copy-start.1 = (bf16[96,128,1,256]{3,1,2,0:T(8,128)(2,1)S(1)}, bf16[96,128,1,256]{3,1,2,0:T(8,128)(2,1)}, u32[]{:S(2)}) copy-start(bf16[96,128,1,256]{3,1,2,0:T(8,128)(2,1)} %param.10) | copy-start | bytes 18874372
  42.0 0.7 copy-start.2
  42.7 0.7 copy-start.4
  43.4 0.7 copy-start.6

commit v2 on v1

v2 whole, which is shorter than its diff:
```python
import functools

import jax
import jax.numpy as jnp
from jax import lax
from jax.experimental import pallas as pl
from jax.experimental.pallas import tpu as pltpu
from jax.sharding import PartitionSpec as P

CAP = 2
INFO = 16
MASKED = -1e30

SMEM = pl.BlockSpec(memory_space=pltpu.SMEM)
VMEM = pl.BlockSpec(memory_space=pltpu.VMEM)
HBM = pl.BlockSpec(memory_space=pltpu.HBM)

nt_dims = (((1,), (1,)), ((), ()))


def split_dot(weights, values):
    rows = weights.shape[0]
    high = weights.astype(jnp.bfloat16)
    low = (weights - high.astype(jnp.float32)).astype(jnp.bfloat16)
    both = jnp.dot(
        jnp.concatenate([high, low], axis=0), values, preferred_element_type=jnp.float32
    )
    return both[:rows] + both[rows:]


def ask_kernel(
    pool_size, block_len, table_hbm, len_hbm, block_hbm, dest_hbm, q_hbm,
    out_ref, query_ref, plan_ref,
    table_ref, len_ref, block_ref, dest_ref, code_ref, live_ref, q_ref, rows_ref, sems,
):
    slots, blocks = table_ref.shape
    steps = q_ref.shape[0]
    rows, head = query_ref.shape[1:]
    group = rows // steps
    arrivals = out_ref.shape[0] * CAP
    copies = [
        pltpu.make_async_copy(source, target, sems.at[k])
        for k, (source, target) in enumerate(
            (
                (q_hbm, q_ref),
                (table_hbm, table_ref),
                (len_hbm, len_ref),
                (block_hbm, block_ref),
                (dest_hbm, dest_ref),
            )
        )
    ]
    for copy in copies:
        copy.start()
    for a in range(arrivals):
        code_ref[a] = 0
        live_ref[a] = 0
    for copy in copies:
        copy.wait()
    for step in range(steps):
        query = q_ref[step].astype(jnp.float32)
        for slot in range(slots):
            for g in range(group):
                at = step * group + g
                rows_ref[slot, at : at + 1, :] = query[slot : slot + 1, g * head : (g + 1) * head]
    for slot in range(slots):
        length = len_ref[slot]
        for b in range(blocks):
            block_id = table_ref[slot, b]
            arrival = jnp.where(block_id >= pool_size, block_id - pool_size, arrivals)
            code_ref[arrival] = slot
            live_ref[arrival] = jnp.clip(length - b * block_len, 0, block_len)
            plan_ref[slot * blocks + b] = block_id
    for slot in range(slots):
        query_ref[slot] = rows_ref[slot].astype(jnp.bfloat16)
    row = lax.broadcasted_iota(jnp.int32, (INFO, head), 0)
    for a in range(arrivals):
        source, rank = a // CAP, a % CAP
        out_ref[source, rank * rows : (rank + 1) * rows, :] = query_ref[code_ref[a]]
    for source in range(arrivals // CAP):
        live = jnp.where(row < INFO // 2, live_ref[source * CAP], live_ref[source * CAP + 1])
        out_ref[source, CAP * rows :, :] = live.astype(jnp.float32).astype(jnp.bfloat16)
    base = slots * blocks
    for ref in (len_ref, block_ref, dest_ref):
        for k in range(ref.shape[0]):
            plan_ref[base + k] = ref[k]
        base += ref.shape[0]


def own_kernel(
    scale, head_group, blocks,
    plan_ref, q_ref, new_ref, pool_ref,
    peak_ref, sum_ref, acc_ref, sent_ref, place_ref,
    seen_ref, kv_ref, sems, sent_sems,
):
    pool_size, block_len, _ = pool_ref.shape
    slots, rows, head = q_ref.shape
    steps = new_ref.shape[0]
    span = blocks * block_len
    entries = sent_ref.shape[0]
    n_inst = seen_ref.shape[0]
    arrivals = n_inst * CAP
    len_at = slots * blocks
    block_at = len_at + slots
    dest_at = block_at + entries

    def own_copy(slot, b):
        block_id = jnp.clip(plan_ref[slot * blocks + b], 0, pool_size - 1)
        return pltpu.make_async_copy(
            pool_ref.at[block_id],
            kv_ref.at[slot, pl.ds(b * block_len, block_len), :],
            sems.at[slot, b],
        )

    def sent_copy(e):
        block_id = jnp.clip(plan_ref[block_at + e], 0, pool_size - 1)
        return pltpu.make_async_copy(pool_ref.at[block_id], sent_ref.at[e], sent_sems.at[e])

    for slot in range(slots):
        for b in range(blocks):
            own_copy(slot, b).start()
    for e in range(entries):
        sent_copy(e).start()
    for i in range(n_inst):
        seen_ref[i] = 0
    for e in range(entries):
        dest = jnp.clip(plan_ref[dest_at + e], 0, n_inst - 1)
        rank = seen_ref[dest]
        seen_ref[dest] = rank + 1
        place_ref[e] = jnp.minimum(rank, CAP - 1) * n_inst + dest
    for a in range(arrivals):
        place_ref[entries + a] = -1
    for slot in range(slots):
        for b in range(blocks):
            block_id = plan_ref[slot * blocks + b]
            arrival = jnp.where(block_id >= pool_size, block_id - pool_size, arrivals)
            place_ref[entries + arrival] = slot
    lane = lax.broadcasted_iota(jnp.int32, (rows, block_len), 1)
    step = lax.broadcasted_iota(jnp.int32, (rows, block_len), 0) // head_group
    for slot in range(slots):
        fresh = jnp.concatenate(
            [new_ref[u, slot : slot + 1, :].astype(jnp.float32) for u in range(steps)]
            + [jnp.zeros((block_len - steps, 2 * head), jnp.float32)],
            axis=0,
        )
        kv_ref[slot, span:, :] = fresh.astype(jnp.bfloat16)
    for slot in range(slots):
        for b in range(blocks):
            own_copy(slot, b).wait()
        scores = lax.dot_general(
            q_ref[slot], kv_ref[slot, :, :head], nt_dims, preferred_element_type=jnp.float32
        ) * scale
        parts_s = []
        for b in range(blocks):
            live = jnp.clip(plan_ref[len_at + slot] - b * block_len, 0, block_len)
            live = jnp.where(plan_ref[slot * blocks + b] < pool_size, live, 0)
            part = scores[:, b * block_len : (b + 1) * block_len]
            parts_s.append(jnp.where(lane < live, part, MASKED))
        parts_s.append(jnp.where((lane <= step) & (lane < steps), scores[:, span:], MASKED))
        peak = jnp.max(functools.reduce(jnp.maximum, parts_s), axis=1, keepdims=True)
        weights = [jnp.exp(part - peak) for part in parts_s]
        total = jnp.sum(functools.reduce(jnp.add, weights), axis=1, keepdims=True)
        acc_ref[slot] = split_dot(jnp.concatenate(weights, axis=1), kv_ref[slot, :, head:])
        peak_ref[slot] = jnp.broadcast_to(peak, (rows, head))
        sum_ref[slot] = jnp.broadcast_to(total, (rows, head))
    for e in range(entries):
        sent_copy(e).wait()


def three_terms(values):
    high = values.astype(jnp.bfloat16).astype(jnp.float32)
    rest = values - high
    middle = rest.astype(jnp.bfloat16).astype(jnp.float32)
    return high, middle, rest - middle


def answer_kernel(
    scale, place_ref, asked_ref, sent_ref, out_ref, peak_ref, sum_ref
):
    entries, block_len, width = sent_ref.shape
    head = width // 2
    n_inst = out_ref.shape[0]
    rows = (out_ref.shape[1] - INFO) // CAP
    peak_ref[...] = jnp.zeros_like(peak_ref)
    sum_ref[...] = jnp.zeros_like(sum_ref)
    lane = lax.broadcasted_iota(jnp.int32, (rows, block_len), 1)
    row = lax.broadcasted_iota(jnp.int32, (rows, block_len), 0)
    key = lane.astype(jnp.float32)
    places, starts, masks, scores = [], [], [], []
    for e in range(entries):
        place = place_ref[e]
        dest = lax.rem(place, n_inst)
        rank = lax.div(place, n_inst)
        start = pl.multiple_of(rank * rows, rows)
        query = asked_ref[dest, pl.ds(start, rows), :]
        info = asked_ref[dest, CAP * rows :, :].astype(jnp.float32)
        live = jnp.where(rank == 0, info[0:1], info[INFO // 2 : INFO // 2 + 1])
        places.append((place, dest))
        starts.append(start)
        masks.append(key < live)
        scores.append(
            lax.dot_general(
                query, sent_ref[e, :, :head], nt_dims, preferred_element_type=jnp.float32
            )
        )
    peaks, totals, results = [], [], []
    for e in range(entries):
        masked = jnp.where(masks[e], scores[e] * scale, MASKED)
        peak = jnp.max(masked, axis=1, keepdims=True)
        weights = jnp.where(masks[e], jnp.exp(masked - peak), 0.0)
        total = jnp.sum(weights, axis=1, keepdims=True)
        values = split_dot(weights, sent_ref[e, :, head:])
        peaks.append(peak)
        totals.append(total)
        results.append((values / jnp.where(total > 0.0, total, 1.0)).astype(jnp.bfloat16))
    for e in range(entries):
        place, dest = places[e]
        out_ref[dest, pl.ds(starts[e], rows), :] = results[e]
        here = lane == row + starts[e]
        peak_ref[pl.ds(place, 1), :] = jnp.sum(
            jnp.where(here, peaks[e], 0.0), axis=0, keepdims=True
        )
        sum_ref[pl.ds(place, 1), :] = jnp.sum(
            jnp.where(here, totals[e], 0.0), axis=0, keepdims=True
        )
    row = lax.broadcasted_iota(jnp.int32, (INFO, block_len), 0)
    terms = three_terms(peak_ref[:n_inst] + peak_ref[n_inst:])
    terms += three_terms(sum_ref[:n_inst] + sum_ref[n_inst:])
    for i in range(n_inst):
        info = jnp.zeros((INFO, block_len), jnp.float32)
        for k, term in enumerate(terms):
            info = jnp.where(row == k, term[i : i + 1], info)
        out_ref[i, CAP * rows :, :] = info.astype(jnp.bfloat16)


def project_kernel(
    first_slot, slot_ref, back_ref, peak_ref, sum_ref, acc_ref, weight_ref, out_ref,
    m_ref, l_ref, a_ref, att_ref, w_ref, sems,
):
    slots, rows, head = acc_ref.shape
    n_inst = back_ref.shape[0]
    parts, out_rows, part_cols = out_ref.shape
    steps = out_rows // slots
    group = rows // steps
    copies = [
        pltpu.make_async_copy(
            weight_ref.at[:, pl.ds(c * part_cols, part_cols)], w_ref.at[c], sems.at[c]
        )
        for c in range(parts)
    ]
    for copy in copies:
        copy.start()
    lane = lax.broadcasted_iota(jnp.int32, (rows, head), 1)
    row = lax.broadcasted_iota(jnp.int32, (rows, head), 0)
    arrivals = []
    best = [peak_ref[slot] for slot in range(slots)]
    for s in range(n_inst):
        info = back_ref[s, CAP * rows :, :].astype(jnp.float32)
        peaks = info[0:1] + info[1:2] + info[2:3]
        sums = info[3:4] + info[4:5] + info[5:6]
        for r in range(CAP):
            slot = slot_ref[first_slot + s * CAP + r]
            here = lane == row + r * rows
            peak = jnp.sum(jnp.where(here, peaks, 0.0), axis=1, keepdims=True)
            total = jnp.sum(jnp.where(here, sums, 0.0), axis=1, keepdims=True)
            arrivals.append((slot, peak, total))
            for k in range(slots):
                best[k] = jnp.maximum(best[k], jnp.where(slot == k, peak, MASKED))
    for k in range(slots):
        keep = jnp.exp(peak_ref[k] - best[k])
        m_ref[k] = best[k]
        l_ref[k] = sum_ref[k] * keep
        a_ref[k] = acc_ref[k] * keep
    for a, (slot, peak, total) in enumerate(arrivals):
        s, r = a // CAP, a % CAP
        at = jnp.maximum(slot, 0)
        gain = jnp.where(slot >= 0, total * jnp.exp(peak - m_ref[at]), 0.0)
        values = back_ref[s, r * rows : (r + 1) * rows, :].astype(jnp.float32)
        l_ref[at] += gain
        a_ref[at] += jnp.where(slot >= 0, gain * values, 0.0)
    for slot in range(slots):
        done = a_ref[slot] / l_ref[slot]
        for step in range(steps):
            for g in range(group):
                at = step * group + g
                to = step * slots + slot
                att_ref[to : to + 1, g * head : (g + 1) * head] = done[at : at + 1]
    attended = att_ref[...].astype(jnp.bfloat16)
    for c in range(parts):
        copies[c].wait()
        out_ref[c] = jnp.dot(
            attended, w_ref[c], preferred_element_type=jnp.float32
        ).astype(jnp.bfloat16)


def params(mib):
    return pltpu.CompilerParams(vmem_limit_bytes=mib * 1024 * 1024)


def shards(queries, new_kv, kv_pool, out_weight, send_block, send_dest, block_table, cache_len):
    n_inst = lax.axis_size("inst")
    n_tp = lax.axis_size("tp")
    steps, slots, head_width = queries.shape
    pool_size, block_len, _, width = kv_pool.shape
    head = width // 2
    group = head_width // head
    rows = steps * group
    blocks = block_table.shape[1]
    entries = send_block.shape[0]
    columns = out_weight.shape[1]
    arrivals = n_inst * CAP
    scale = head ** (-0.5)
    f32, bf16, i32 = jnp.float32, jnp.bfloat16, jnp.int32
    shape = jax.ShapeDtypeStruct
    pool = kv_pool.reshape(pool_size, block_len, width)
    fresh = new_kv.reshape(steps, slots, width)

    packet = shape((n_inst, CAP * rows + INFO, head), bf16)
    ask, slot_query, plan = pl.pallas_call(
        functools.partial(ask_kernel, pool_size, block_len),
        out_shape=(
            packet,
            shape((slots, rows, head), bf16),
            shape((slots * blocks + slots + 2 * entries,), i32),
        ),
        in_specs=[HBM] * 5,
        out_specs=(VMEM, VMEM, SMEM),
        scratch_shapes=[
            pltpu.SMEM((slots, blocks), i32),
            pltpu.SMEM((slots,), i32),
            pltpu.SMEM((entries,), i32),
            pltpu.SMEM((entries,), i32),
            pltpu.SMEM((arrivals + 1,), i32),
            pltpu.SMEM((arrivals + 1,), i32),
            pltpu.VMEM(queries.shape, bf16),
            pltpu.VMEM((slots, rows, head), f32),
            pltpu.SemaphoreType.DMA((5,)),
        ],
        compiler_params=params(64),
        name="ask",
    )(block_table, cache_len, send_block, send_dest, queries)
    asked = lax.all_to_all(ask, "inst", 0, 0, tiled=True)

    own = shape((slots, rows, head), f32)
    own_peak, own_sum, own_acc, sent, place = pl.pallas_call(
        functools.partial(own_kernel, scale, group, blocks),
        out_shape=(
            own, own, own,
            shape((entries, block_len, width), bf16),
            shape((entries + arrivals + 1,), i32),
        ),
        in_specs=[SMEM, VMEM, VMEM, HBM],
        out_specs=(VMEM, VMEM, VMEM, VMEM, SMEM),
        scratch_shapes=[
            pltpu.SMEM((n_inst,), i32),
            pltpu.VMEM((slots, (blocks + 1) * block_len, width), bf16),
            pltpu.SemaphoreType.DMA((slots, blocks)),
            pltpu.SemaphoreType.DMA((entries,)),
        ],
        compiler_params=params(50),
        cost_estimate=pl.CostEstimate(
            flops=4 * slots * rows * blocks * block_len * width,
            bytes_accessed=8 * slots * blocks * block_len * width,
            transcendentals=slots * rows * blocks * block_len,
        ),
        name="own",
    )(plan, slot_query, fresh, pool)

    part_cols = columns // n_tp
    answer = pl.pallas_call(
        functools.partial(answer_kernel, scale),
        out_shape=packet,
        in_specs=[SMEM, VMEM, VMEM],
        out_specs=VMEM,
        scratch_shapes=[
            pltpu.VMEM((arrivals, head), f32),
            pltpu.VMEM((arrivals, head), f32),
        ],
        compiler_params=params(16),
        name="answer",
    )(place, asked, sent)
    back = lax.all_to_all(answer, "inst", 0, 0, tiled=True)

    out_rows = steps * slots
    partial_out = pl.pallas_call(
        functools.partial(project_kernel, entries),
        out_shape=shape((n_tp, out_rows, part_cols), bf16),
        in_specs=[SMEM, VMEM, VMEM, VMEM, VMEM, HBM],
        out_specs=VMEM,
        scratch_shapes=[
            pltpu.VMEM((slots, rows, head), f32),
            pltpu.VMEM((slots, rows, head), f32),
            pltpu.VMEM((slots, rows, head), f32),
            pltpu.VMEM((out_rows, head_width), f32),
            pltpu.VMEM((n_tp, head_width, part_cols), bf16),
            pltpu.SemaphoreType.DMA((n_tp,)),
        ],
        compiler_params=params(44),
        name="project",
    )(place, back, own_peak, own_sum, own_acc, out_weight)
    shares = lax.all_to_all(partial_out, "tp", 0, 0, tiled=True)
    total = jnp.sum(shares.astype(f32), axis=0).astype(bf16)
    return total.reshape(steps, slots, columns // n_tp)


def solution(mesh):
    return jax.shard_map(
        shards,
        mesh=mesh,
        in_specs=(
            P(None, "inst", "tp"),
            P(None, "inst", "tp", None),
            P("inst", None, "tp", None),
            P("tp", None),
            P("inst"),
            P("inst"),
            P("inst", None),
            P("inst"),
        ),
        out_specs=P(None, "inst", "tp"),
        check_vma=False,
    )
```

time: 73.8 us -> 56.5 us (0.77)
  Pallas kernels: 27.6 us -> 16.7 us
  local copies, waits for them, and re-layouts: 11.7 us -> 2.69 us
  starting transfers between devices: 3.55 us -> 8.14 us
  blocking collectives: 29.8 us -> 26.3 us
  waiting for transfers between devices: 0.01 us -> 1.95 us
    unnamed x18 -> x6, local copies, waits for them, and re-layouts: 10.2 us -> 2.06 us
    pallas_call x1, Pallas kernels: 8.65 us -> 1.18 us  [shards(): pl.pallas_call(functools.partial(answer_kernel, scale), out_shape=packet,...]
    all_to_all x1, starting transfers between devices: 3.55 us -> 8.14 us  [shards(): asked = lax.all_to_all(ask, 'inst', 0, 0, tiled=True)]
    all_to_all x1, blocking collectives: 18.2 us -> 15.2 us  [shards(): back = lax.all_to_all(answer, 'inst', 0, 0, tiled=True)]
    pallas_call x2, Pallas kernels: 16.4 us -> 13.6 us  [the longest x1 7.38 us: shards(): pl.pallas_call(functools.partial(project_kernel, entries), out_shape=shap...]
    all_to_all x1, waiting for transfers between devices: 0.01 us -> 1.95 us  [shards(): asked = lax.all_to_all(ask, 'inst', 0, 0, tiled=True)]
    reshape x2 -> x0, local copies, waits for them, and re-layouts: 0.78 us -> none  [shards(): queries.reshape(steps, slots, group, head)]
  transfers between devices with their start and end apart: 1 -> 1, of which waited for: 0 -> 1; matrix products, arithmetic and copies ran while one was open for 0% -> 0% of each run, Pallas kernels for 13% -> 11%
where the time goes in v2:
time: 56.5 us; the launch traced here: 55.9 us
  blocking collectives  26.3 us (47%)
  Pallas kernels  16.7 us (30%)
  starting transfers between devices  8.14 us (14%)
  local copies, waits for them, and re-layouts  2.69 us (5%)
  waiting for transfers between devices  1.95 us (3%)
    all_to_all x1, blocking collectives, shards(): back = lax.all_to_all(answer, 'inst', 0, 0, tiled=True)  15.2 us
    all_to_all x1, blocking collectives, shards(): shares = lax.all_to_all(partial_out, 'tp', 0, 0, tiled=True)  11.1 us
    all_to_all x1, starting transfers between devices, shards(): asked = lax.all_to_all(ask, 'inst', 0, 0, tiled=True)  8.14 us
    pallas_call x1, Pallas kernels, shards(): pl.pallas_call(functools.partial(project_kernel, entries), out_shape=shap...  7.38 us
    pallas_call x1, Pallas kernels, shards(): pl.pallas_call(functools.partial(own_kernel, scale, group, blocks), out_s...  6.24 us
    unnamed x6, local copies, waits for them, and re-layouts  2.06 us
    all_to_all x1, waiting for transfers between devices, shards(): asked = lax.all_to_all(ask, 'inst', 0, 0, tiled=True)  1.95 us
    pallas_call x1, Pallas kernels, shards(): pl.pallas_call(functools.partial(ask_kernel, pool_size, block_len), out_s...  1.92 us
  transfers between devices with their start and end apart: 1, of which 1 were waited for; matrix products, arithmetic and copies ran while one was open for 0% of the time, Pallas kernels for 11%

profile of v2, /device:TPU:0, one launch (start us, length us, event | category | flops | bytes accessed | tf_op | source)
XLA Modules:
  0.0 55.9 jit_solution(6206508638648364949)
XLA Ops:
  0.0 1.9 %ask.1 = (bf16[16,80,128]{2,1,0:T(8,128)(2,1)}, bf16[4,32,128]{2,1,0:T(8,128)(2,1)}, s32[100]{0:T(128)}) custom-call(s32[4,16]{1,0:T(4,128)} %table_hbm.1, s32[4]{0:T(128)} %len_hbm.1, s32[16]{0:T(128)} %block_hbm.1, s32[16]{0:T(128)} %dest_hbm.1, bf16[4,4,1024]{2,1,0:T(4,128)(2,1)} %q_hbm.1), custom_call_target="tpu_custom_call" | custom-call | tf_op jit(solution)/shard_map/ask/pallas_call | solution.py:319
  1.9 8.1 %all-to-all-start = ((bf16[16,80,128]{2,1,0:T(8,128)(2,1)}), bf16[16,80,128]{2,1,0:T(8,128)(2,1)S(1)}, u32[]{:S(2)}, u32[]{:S(2)}) async-start(bf16[16,80,128]{2,1,0:T(8,128)(2,1)} %get-tuple-element.16), calls=%async_computation | async-start | bytes 655360 | tf_op jit(solution)/shard_map/all_to_all | solution.py:342
  10.1 0.0 copy-start
  10.1 0.7 %copy-done = bf16[4,32,128]{2,1,0:T(8,128)(2,1)S(1)} copy-done((bf16[4,32,128]{2,1,0:T(8,128)(2,1)S(1)}, bf16[4,32,128]{2,1,0:T(8,128)(2,1)}, u32[]{:S(2)}) %copy-start) | copy-done | bytes 32792
  10.8 0.0 copy-start.1
  10.8 0.7 %copy-done.1 = bf16[4,4,1,256]{3,1,2,0:T(4,128)(2,1)S(1)} copy-done((bf16[4,4,1,256]{3,1,2,0:T(4,128)(2,1)S(1)}, bf16[4,4,1,256]{3,1,2,0:T(4,128)(2,1)}, u32[]{:S(2)}) %copy-start.1) | copy-done | bytes 8216
  11.5 0.0 copy-start.2
  11.5 0.6 %copy-done.2 = s32[100]{0:T(128)S(1)} copy-done((s32[100]{0:T(128)S(1)}, s32[100]{0:T(128)}, u32[]{:S(2)}) %copy-start.2) | copy-done | bytes 424
  12.1 6.2 %own.1 = (f32[4,32,128]{2,1,0:T(8,128)S(1)}, f32[4,32,128]{2,1,0:T(8,128)S(1)}, f32[4,32,128]{2,1,0:T(8,128)S(1)}, bf16[16,128,256]{2,1,0:T(8,128)(2,1)S(1)}, s32[49]{0:T(128)S(1)}) custom-call(s32[100]{0:T(128)S(1)} %copy-done.2, bf16[4,32,128]{2,1,0:T(8,128)(2,1)S(1)} %copy-done, bf16[4,4,256]{2,1,0:T(4,128)(2,1)S(1)} %bitcast.2, bf16[96,128,256]{2,1,0:T(8,128)(2,1)} %bitcast.3), custom_call_target="tpu_custom_call" | custom-call | flops 268435456 | bytes 16777216 | tf_op jit(solution)/shard_map/own/pallas_call | solution.py:345
  18.4 1.9 %all-to-all-done.asked_ref = bf16[16,80,128]{2,1,0:T(8,128)(2,1)S(1)} async-done(((bf16[16,80,128]{2,1,0:T(8,128)(2,1)}), bf16[16,80,128]{2,1,0:T(8,128)(2,1)S(1)}, u32[]{:S(2)}, u32[]{:S(2)}) %all-to-all-start) | async-done | bytes 327712 | tf_op jit(solution)/shard_map/all_to_all | solution.py:342
  20.3 1.2 %answer.1 = bf16[16,80,128]{2,1,0:T(8,128)(2,1)S(1)} custom-call(s32[49]{0:T(128)S(1)} %get-tuple-element.15.place_ref.slot_ref, bf16[16,80,128]{2,1,0:T(8,128)(2,1)S(1)} %all-to-all-done.asked_ref, bf16[16,128,256]{2,1,0:T(8,128)(2,1)S(1)} %get-tuple-element.17.sent_ref), custom_call_target="tpu_custom_call" | custom-call | tf_op jit(solution)/shard_map/answer/pallas_call | solution.py:370
  21.5 15.2 %all_to_all.15.back_ref = bf16[16,80,128]{2,1,0:T(8,128)(2,1)S(1)} all-to-all(bf16[16,80,128]{2,1,0:T(8,128)(2,1)S(1)} %answer.1), channel_id=1, replica_groups=mesh['inst'=16,'tp'=8] {'inst'}, dimensions={0} | all-to-all | bytes 655360 | tf_op jit(solution)/shard_map/all_to_all | solution.py:382
  36.7 7.4 %project.1 = bf16[8,16,1024]{2,1,0:T(8,128)(2,1)S(1)} custom-call(s32[49]{0:T(128)S(1)} %get-tuple-element.15.place_ref.slot_ref, bf16[16,80,128]{2,1,0:T(8,128)(2,1)S(1)} %all_to_all.15.back_ref, f32[4,32,128]{2,1,0:T(8,128)S(1)} %get-tuple-element.18.peak_ref, f32[4,32,128]{2,1,0:T(8,128)S(1)} %get-tuple-element.19.sum_ref, ...), custom_call_target="tpu_custom_call" | custom-call | tf_op jit(solution)/shard_map/project/pallas_call | solution.py:385
  44.1 11.1 %all_to_all.16 = bf16[8,16,1024]{2,1,0:T(8,128)(2,1)S(1)} all-to-all(bf16[8,16,1024]{2,1,0:T(8,128)(2,1)S(1)} %project.1), channel_id=1, replica_groups=mesh['inst'=16,'tp'=8] {'tp'}, dimensions={0} | all-to-all | bytes 524288 | tf_op jit(solution)/shard_map/all_to_all | solution.py:401
  55.3 0.6 %reshape.11 = bf16[4,4,1024]{2,1,0:T(4,128)(2,1)} reshape(bf16[16,1024]{1,0:T(8,128)(2,1)S(1)} %reduce_sum.12) | data formatting | bytes 65536 | tf_op jit(solution)/shard_map/reshape | solution.py:403
  (1 shorter events, 0.0 us)
Async XLA Ops:
  1.9 18.4 %all-to-all-start = ((bf16[16,80,128]{2,1,0:T(8,128)(2,1)}), bf16[16,80,128]{2,1,0:T(8,128)(2,1)S(1)}, u32[]{:S(2)}, u32[]{:S(2)}) async-start(bf16[16,80,128]{2,1,0:T(8,128)(2,1)} %get-tuple-element.16), calls=%async_computation | async-start | bytes 655360 | tf_op jit(solution)/shard_map/all_to_all | solution.py:342
  10.1 0.8 %copy-start = (bf16[4,32,128]{2,1,0:T(8,128)(2,1)S(1)}, bf16[4,32,128]{2,1,0:T(8,128)(2,1)}, u32[]{:S(2)}) copy-start(bf16[4,32,128]{2,1,0:T(8,128)(2,1)} %get-tuple-element.14.q_ref) | copy-start | bytes 98308
  10.8 0.7 %copy-start.1 = (bf16[4,4,1,256]{3,1,2,0:T(4,128)(2,1)S(1)}, bf16[4,4,1,256]{3,1,2,0:T(4,128)(2,1)}, u32[]{:S(2)}) copy-start(bf16[4,4,1,256]{3,1,2,0:T(4,128)(2,1)} %param.9) | copy-start | bytes 24580
  11.5 0.6 %copy-start.2 = (s32[100]{0:T(128)S(1)}, s32[100]{0:T(128)}, u32[]{:S(2)}) copy-start(s32[100]{0:T(128)} %get-tuple-element.13.plan_ref) | copy-start | bytes 1204

commit v3 on v2

--- a/solution.py
+++ b/solution.py
@@ -8,8 +8,9 @@
 from jax.sharding import PartitionSpec as P
 
 CAP = 2
-INFO = 16
+INFO = 8
 MASKED = -1e30
+TILE = 256
 
 SMEM = pl.BlockSpec(memory_space=pltpu.SMEM)
 VMEM = pl.BlockSpec(memory_space=pltpu.VMEM)
@@ -88,67 +89,43 @@
 
 
 def own_kernel(
-    scale, head_group, blocks,
+    scale, head_group, blocks, first,
     plan_ref, q_ref, new_ref, pool_ref,
-    peak_ref, sum_ref, acc_ref, sent_ref, place_ref,
-    seen_ref, kv_ref, sems, sent_sems,
+    peak_ref, sum_ref, acc_ref, kv_ref, sems, bring,
 ):
     pool_size, block_len, _ = pool_ref.shape
     slots, rows, head = q_ref.shape
     steps = new_ref.shape[0]
     span = blocks * block_len
-    entries = sent_ref.shape[0]
-    n_inst = seen_ref.shape[0]
-    arrivals = n_inst * CAP
     len_at = slots * blocks
-    block_at = len_at + slots
-    dest_at = block_at + entries
+    mine = range(first, first + peak_ref.shape[0])
 
     def own_copy(slot, b):
         block_id = jnp.clip(plan_ref[slot * blocks + b], 0, pool_size - 1)
         return pltpu.make_async_copy(
             pool_ref.at[block_id],
-            kv_ref.at[slot, pl.ds(b * block_len, block_len), :],
-            sems.at[slot, b],
-        )
-
-    def sent_copy(e):
-        block_id = jnp.clip(plan_ref[block_at + e], 0, pool_size - 1)
-        return pltpu.make_async_copy(pool_ref.at[block_id], sent_ref.at[e], sent_sems.at[e])
-
-    for slot in range(slots):
+            kv_ref.at[slot - first, pl.ds(b * block_len, block_len), :],
+            sems.at[slot - first, b],
+        )
+
+    for slot in mine:
         for b in range(blocks):
             own_copy(slot, b).start()
-    for e in range(entries):
-        sent_copy(e).start()
-    for i in range(n_inst):
-        seen_ref[i] = 0
-    for e in range(entries):
-        dest = jnp.clip(plan_ref[dest_at + e], 0, n_inst - 1)
-        rank = seen_ref[dest]
-        seen_ref[dest] = rank + 1
-        place_ref[e] = jnp.minimum(rank, CAP - 1) * n_inst + dest
-    for a in range(arrivals):
-        place_ref[entries + a] = -1
-    for slot in range(slots):
-        for b in range(blocks):
-            block_id = plan_ref[slot * blocks + b]
-            arrival = jnp.where(block_id >= pool_size, block_id - pool_size, arrivals)
-            place_ref[entries + arrival] = slot
+    brought = bring()
     lane = lax.broadcasted_iota(jnp.int32, (rows, block_len), 1)
     step = lax.broadcasted_iota(jnp.int32, (rows, block_len), 0) // head_group
-    for slot in range(slots):
+    for slot in mine:
         fresh = jnp.concatenate(
             [new_ref[u, slot : slot + 1, :].astype(jnp.float32) for u in range(steps)]
             + [jnp.zeros((block_len - steps, 2 * head), jnp.float32)],
             axis=0,
         )
-        kv_ref[slot, span:, :] = fresh.astype(jnp.bfloat16)
-    for slot in range(slots):
+        kv_ref[slot - first, span:, :] = fresh.astype(jnp.bfloat16)
+    for slot in mine:
         for b in range(blocks):
             own_copy(slot, b).wait()
         scores = lax.dot_general(
-            q_ref[slot], kv_ref[slot, :, :head], nt_dims, preferred_element_type=jnp.float32
+            q_ref[slot], kv_ref[slot - first, :, :head], nt_dims, preferred_element_type=jnp.float32
         ) * scale
         parts_s = []
         for b in range(blocks):
@@ -160,11 +137,76 @@
         peak = jnp.max(functools.reduce(jnp.maximum, parts_s), axis=1, keepdims=True)
         weights = [jnp.exp(part - peak) for part in parts_s]
         total = jnp.sum(functools.reduce(jnp.add, weights), axis=1, keepdims=True)
-        acc_ref[slot] = split_dot(jnp.concatenate(weights, axis=1), kv_ref[slot, :, head:])
-        peak_ref[slot] = jnp.broadcast_to(peak, (rows, head))
-        sum_ref[slot] = jnp.broadcast_to(total, (rows, head))
-    for e in range(entries):
-        sent_copy(e).wait()
+        acc_ref[slot - first] = split_dot(jnp.concatenate(weights, axis=1), kv_ref[slot - first, :, head:])
+        peak_ref[slot - first] = jnp.broadcast_to(peak, (rows, head))
+        sum_ref[slot - first] = jnp.broadcast_to(total, (rows, head))
+    for copy in brought:
+        copy.wait()
+
+
+def first_kernel(
+    scale, head_group, blocks,
+    plan_ref, q_ref, new_ref, pool_ref,
+    peak_ref, sum_ref, acc_ref, sent_ref, place_ref,
+    seen_ref, kv_ref, sems, sent_sems,
+):
+    pool_size = pool_ref.shape[0]
+    slots = q_ref.shape[0]
+    entries = sent_ref.shape[0]
+    n_inst = seen_ref.shape[0]
+    arrivals = n_inst * CAP
+    block_at = slots * blocks + slots
+    dest_at = block_at + entries
+
+    def bring():
+        copies = []
+        for e in range(entries):
+            block_id = jnp.clip(plan_ref[block_at + e], 0, pool_size - 1)
+            copies.append(
+                pltpu.make_async_copy(pool_ref.at[block_id], sent_ref.at[e], sent_sems.at[e])
+            )
+            copies[e].start()
+        for i in range(n_inst):
+            seen_ref[i] = 0
+        for e in range(entries):
+            dest = jnp.clip(plan_ref[dest_at + e], 0, n_inst - 1)
+            rank = seen_ref[dest]
+            seen_ref[dest] = rank + 1
+            place_ref[e] = jnp.minimum(rank, CAP - 1) * n_inst + dest
+        for a in range(arrivals):
+            place_ref[entries + a] = -1
+        for slot in range(slots):
+            for b in range(blocks):
+                block_id = plan_ref[slot * blocks + b]
+                arrival = jnp.where(block_id >= pool_size, block_id - pool_size, arrivals)
+                place_ref[entries + arrival] = slot
+        return copies
+
+    own_kernel(
+        scale, head_group, blocks, 0, plan_ref, q_ref, new_ref, pool_ref,
+        peak_ref, sum_ref, acc_ref, kv_ref, sems, bring,
+    )
+
+
+def second_kernel(
+    scale, head_group, blocks, first,
+    plan_ref, q_ref, new_ref, pool_ref, weight_ref, after_ref,
+    peak_ref, sum_ref, acc_ref, held_ref,
+    kv_ref, sems, weight_sem,
+):
+    del after_ref
+
+    def bring():
+        copy = pltpu.make_async_copy(
+            weight_ref.at[:, pl.ds(0, held_ref.shape[1])], held_ref, weight_sem
+        )
+        copy.start()
+        return [copy]
+
+    own_kernel(
+        scale, head_group, blocks, first, plan_ref, q_ref, new_ref, pool_ref,
+        peak_ref, sum_ref, acc_ref, kv_ref, sems, bring,
+    )
 
 
 def three_terms(values):
@@ -234,26 +276,34 @@
 
 
 def project_kernel(
-    first_slot, slot_ref, back_ref, peak_ref, sum_ref, acc_ref, weight_ref, out_ref,
+    first_slot, slot_ref, back_ref, peak_a, sum_a, acc_a, peak_b, sum_b, acc_b,
+    held_ref, weight_ref, out_ref,
     m_ref, l_ref, a_ref, att_ref, w_ref, sems,
 ):
-    slots, rows, head = acc_ref.shape
+    slots, rows, head = a_ref.shape
     n_inst = back_ref.shape[0]
     parts, out_rows, part_cols = out_ref.shape
+    held = held_ref.shape[1]
+    half = acc_a.shape[0]
     steps = out_rows // slots
     group = rows // steps
-    copies = [
-        pltpu.make_async_copy(
-            weight_ref.at[:, pl.ds(c * part_cols, part_cols)], w_ref.at[c], sems.at[c]
-        )
-        for c in range(parts)
-    ]
-    for copy in copies:
-        copy.start()
+    copies = {}
+    for c in range(parts):
+        low, high = max(held, c * part_cols), (c + 1) * part_cols
+        if low < high:
+            copies[c] = pltpu.make_async_copy(
+                weight_ref.at[:, pl.ds(low, high - low)],
+                w_ref.at[:, pl.ds(low - held, high - low)],
+                sems.at[c],
+            )
+            copies[c].start()
     lane = lax.broadcasted_iota(jnp.int32, (rows, head), 1)
     row = lax.broadcasted_iota(jnp.int32, (rows, head), 0)
     arrivals = []
-    best = [peak_ref[slot] for slot in range(slots)]
+    peak_own = [peak_a[k] for k in range(half)] + [peak_b[k] for k in range(slots - half)]
+    sum_own = [sum_a[k] for k in range(half)] + [sum_b[k] for k in range(slots - half)]
+    acc_own = [acc_a[k] for k in range(half)] + [acc_b[k] for k in range(slots - half)]
+    best = list(peak_own)
     for s in range(n_inst):
         info = back_ref[s, CAP * rows :, :].astype(jnp.float32)
         peaks = info[0:1] + info[1:2] + info[2:3]
@@ -267,10 +317,10 @@
             for k in range(slots):
                 best[k] = jnp.maximum(best[k], jnp.where(slot == k, peak, MASKED))
     for k in range(slots):
-        keep = jnp.exp(peak_ref[k] - best[k])
+        keep = jnp.exp(peak_own[k] - best[k])
         m_ref[k] = best[k]
-        l_ref[k] = sum_ref[k] * keep
-        a_ref[k] = acc_ref[k] * keep
+        l_ref[k] = sum_own[k] * keep
+        a_ref[k] = acc_own[k] * keep
     for a, (slot, peak, total) in enumerate(arrivals):
         s, r = a // CAP, a % CAP
         at = jnp.maximum(slot, 0)
@@ -287,10 +337,17 @@
                 att_ref[to : to + 1, g * head : (g + 1) * head] = done[at : at + 1]
     attended = att_ref[...].astype(jnp.bfloat16)
     for c in range(parts):
-        copies[c].wait()
-        out_ref[c] = jnp.dot(
-            attended, w_ref[c], preferred_element_type=jnp.float32
-        ).astype(jnp.bfloat16)
+        if c in copies:
+            copies[c].wait()
+        for low in range(c * part_cols, (c + 1) * part_cols, TILE):
+            if low < held:
+                weight = held_ref[:, low : low + TILE]
+            else:
+                weight = w_ref[:, low - held : low - held + TILE]
+            at = low - c * part_cols
+            out_ref[c, :, at : at + TILE] = jnp.dot(
+                attended, weight, preferred_element_type=jnp.float32
+            ).astype(jnp.bfloat16)
 
 
 def params(mib):
@@ -341,9 +398,16 @@
     )(block_table, cache_len, send_block, send_dest, queries)
     asked = lax.all_to_all(ask, "inst", 0, 0, tiled=True)
 
-    own = shape((slots, rows, head), f32)
-    own_peak, own_sum, own_acc, sent, place = pl.pallas_call(
-        functools.partial(own_kernel, scale, group, blocks),
+    half = slots // 2
+    own = shape((half, rows, head), f32)
+    kv_scratch = pltpu.VMEM((half, (blocks + 1) * block_len, width), bf16)
+    own_cost = pl.CostEstimate(
+        flops=2 * slots * rows * blocks * block_len * width,
+        bytes_accessed=4 * slots * blocks * block_len * width,
+        transcendentals=half * rows * blocks * block_len,
+    )
+    peak_a, sum_a, acc_a, sent, place = pl.pallas_call(
+        functools.partial(first_kernel, scale, group, blocks),
         out_shape=(
             own, own, own,
             shape((entries, block_len, width), bf16),
@@ -353,17 +417,13 @@
         out_specs=(VMEM, VMEM, VMEM, VMEM, SMEM),
         scratch_shapes=[
             pltpu.SMEM((n_inst,), i32),
-            pltpu.VMEM((slots, (blocks + 1) * block_len, width), bf16),
-            pltpu.SemaphoreType.DMA((slots, blocks)),
+            kv_scratch,
+            pltpu.SemaphoreType.DMA((half, blocks)),
             pltpu.SemaphoreType.DMA((entries,)),
         ],
         compiler_params=params(50),
-        cost_estimate=pl.CostEstimate(
-            flops=4 * slots * rows * blocks * block_len * width,
-            bytes_accessed=8 * slots * blocks * block_len * width,
-            transcendentals=slots * rows * blocks * block_len,
-        ),
-        name="own",
+        cost_estimate=own_cost,
+        name="own_first",
     )(plan, slot_query, fresh, pool)
 
     part_cols = columns // n_tp
@@ -381,23 +441,39 @@
     )(place, asked, sent)
     back = lax.all_to_all(answer, "inst", 0, 0, tiled=True)
 
+    ahead = 5 * TILE
+    peak_b, sum_b, acc_b, held = pl.pallas_call(
+        functools.partial(second_kernel, scale, group, blocks, half),
+        out_shape=(own, own, own, shape((head_width, ahead), bf16)),
+        in_specs=[SMEM, VMEM, VMEM, HBM, HBM, pl.BlockSpec(memory_space=pl.ANY)],
+        out_specs=(VMEM, VMEM, VMEM, VMEM),
+        scratch_shapes=[
+            kv_scratch,
+            pltpu.SemaphoreType.DMA((half, blocks)),
+            pltpu.SemaphoreType.DMA,
+        ],
+        compiler_params=params(50),
+        cost_estimate=own_cost,
+        name="own_second",
+    )(plan, slot_query, fresh, pool, out_weight, answer)
+
     out_rows = steps * slots
     partial_out = pl.pallas_call(
         functools.partial(project_kernel, entries),
         out_shape=shape((n_tp, out_rows, part_cols), bf16),
-        in_specs=[SMEM, VMEM, VMEM, VMEM, VMEM, HBM],
+        in_specs=[SMEM] + [VMEM] * 8 + [HBM],
         out_specs=VMEM,
         scratch_shapes=[
             pltpu.VMEM((slots, rows, head), f32),
             pltpu.VMEM((slots, rows, head), f32),
             pltpu.VMEM((slots, rows, head), f32),
             pltpu.VMEM((out_rows, head_width), f32),
-            pltpu.VMEM((n_tp, head_width, part_cols), bf16),
+            pltpu.VMEM((head_width, columns - ahead), bf16),
             pltpu.SemaphoreType.DMA((n_tp,)),
         ],
         compiler_params=params(44),
         name="project",
-    )(place, back, own_peak, own_sum, own_acc, out_weight)
+    )(place, back, peak_a, sum_a, acc_a, peak_b, sum_b, acc_b, held, out_weight)
     shares = lax.all_to_all(partial_out, "tp", 0, 0, tiled=True)
     total = jnp.sum(shares.astype(f32), axis=0).astype(bf16)
     return total.reshape(steps, slots, columns // n_tp)

time: 56.5 us -> 54.8 us (0.970)
  blocking collectives: 26.3 us -> 11.1 us
  waiting for transfers between devices: 1.95 us -> 9.91 us
  starting transfers between devices: 8.14 us -> 12.1 us
  Pallas kernels: 16.7 us -> 18.2 us
    all_to_all x1 -> x0, blocking collectives: 15.2 us -> none  [shards(): back = lax.all_to_all(answer, 'inst', 0, 0, tiled=True)]
    all_to_all x0 -> x1, waiting for transfers between devices: none -> 6.29 us  [shards(): back = lax.all_to_all(answer, 'inst', 0, 0, tiled=True)]
    all_to_all x0 -> x1, starting transfers between devices: none -> 3.96 us  [shards(): back = lax.all_to_all(answer, 'inst', 0, 0, tiled=True)]
    all_to_all x1, waiting for transfers between devices: 1.95 us -> 3.62 us  [shards(): asked = lax.all_to_all(ask, 'inst', 0, 0, tiled=True)]
    pallas_call x1 -> x2, Pallas kernels: 6.24 us -> 7.72 us  [the longest x1 4.14 us: shards(): pl.pallas_call(functools.partial(first_kernel, scale, group, blocks), out...]
    pallas_call x1, Pallas kernels: 1.18 us -> 1.9 us  [shards(): pl.pallas_call(functools.partial(answer_kernel, scale), out_shape=packet,...]
    pallas_call x1, Pallas kernels: 7.38 us -> 6.67 us  [shards(): pl.pallas_call(functools.partial(project_kernel, entries), out_shape=shap...]
    unnamed x6 -> x12, local copies, waits for them, and re-layouts: 2.06 us -> 2.15 us
  transfers between devices with their start and end apart: 1 -> 2, of which waited for: 1 -> 2; matrix products, arithmetic and copies ran while one was open for 0% -> 0% of each run, Pallas kernels for 11% -> 14%
where the time goes in v3:
time: 54.8 us; the launch traced here: 54.3 us
  Pallas kernels  18.2 us (33%)
  starting transfers between devices  12.1 us (22%)
  blocking collectives  11.1 us (20%)
  waiting for transfers between devices  9.91 us (18%)
  local copies, waits for them, and re-layouts  2.78 us (5%)
    all_to_all x1, blocking collectives, shards(): shares = lax.all_to_all(partial_out, 'tp', 0, 0, tiled=True)  11.1 us
    all_to_all x1, starting transfers between devices, shards(): asked = lax.all_to_all(ask, 'inst', 0, 0, tiled=True)  8.14 us
    pallas_call x1, Pallas kernels, shards(): pl.pallas_call(functools.partial(project_kernel, entries), out_shape=shap...  6.67 us
    all_to_all x1, waiting for transfers between devices, shards(): back = lax.all_to_all(answer, 'inst', 0, 0, tiled=True)  6.29 us
    pallas_call x1, Pallas kernels, shards(): pl.pallas_call(functools.partial(first_kernel, scale, group, blocks), out...  4.14 us
    all_to_all x1, starting transfers between devices, shards(): back = lax.all_to_all(answer, 'inst', 0, 0, tiled=True)  3.96 us
    all_to_all x1, waiting for transfers between devices, shards(): asked = lax.all_to_all(ask, 'inst', 0, 0, tiled=True)  3.62 us
    pallas_call x1, Pallas kernels, shards(): pl.pallas_call(functools.partial(second_kernel, scale, group, blocks, hal...  3.58 us
  transfers between devices with their start and end apart: 2, of which 2 were waited for; matrix products, arithmetic and copies ran while one was open for 0% of the time, Pallas kernels for 14%

profile of v3, /device:TPU:0, one launch (start us, length us, event | category | flops | bytes accessed | tf_op | source)
XLA Modules:
  0.0 54.3 jit_solution(7120492076472200680)
XLA Ops:
  0.0 1.9 %ask.1 = (bf16[16,72,128]{2,1,0:T(8,128)(2,1)}, bf16[4,32,128]{2,1,0:T(8,128)(2,1)}, s32[100]{0:T(128)}) custom-call(s32[4,16]{1,0:T(4,128)} %table_hbm.1, s32[4]{0:T(128)} %len_hbm.1, s32[16]{0:T(128)} %block_hbm.1, s32[16]{0:T(128)} %dest_hbm.1, bf16[4,4,1024]{2,1,0:T(4,128)(2,1)} %q_hbm.1), custom_call_target="tpu_custom_call" | custom-call | tf_op jit(solution)/shard_map/ask/pallas_call | solution.py:376
  1.9 0.0 copy-start.1
  1.9 0.0 copy-start.3
  1.9 0.0 copy-start.5
  2.0 8.1 %all-to-all-start = ((bf16[16,72,128]{2,1,0:T(8,128)(2,1)}), bf16[16,72,128]{2,1,0:T(8,128)(2,1)S(1)}, u32[]{:S(2)}, u32[]{:S(2)}) async-start(bf16[16,72,128]{2,1,0:T(8,128)(2,1)} %get-tuple-element.20), calls=%async_computation | async-start | bytes 589824 | tf_op jit(solution)/shard_map/all_to_all | solution.py:399
  10.1 0.0 copy-start
  10.1 0.7 %copy-done = bf16[4,32,128]{2,1,0:T(8,128)(2,1)S(1)} copy-done((bf16[4,32,128]{2,1,0:T(8,128)(2,1)S(1)}, bf16[4,32,128]{2,1,0:T(8,128)(2,1)}, u32[]{:S(2)}) %copy-start) | copy-done | bytes 32792
  10.9 0.0 copy-start.2
  10.9 0.7 %copy-done.2 = bf16[4,4,1,256]{3,1,2,0:T(4,128)(2,1)S(1)} copy-done((bf16[4,4,1,256]{3,1,2,0:T(4,128)(2,1)S(1)}, bf16[4,4,1,256]{3,1,2,0:T(4,128)(2,1)}, u32[]{:S(2)}) %copy-start.2) | copy-done | bytes 8216
  11.6 0.0 copy-start.4
  11.6 0.7 %copy-done.4 = s32[100]{0:T(128)S(1)} copy-done((s32[100]{0:T(128)S(1)}, s32[100]{0:T(128)}, u32[]{:S(2)}) %copy-start.4) | copy-done | bytes 424
  12.2 4.1 %own_first.1 = (f32[2,32,128]{2,1,0:T(8,128)S(1)}, f32[2,32,128]{2,1,0:T(8,128)S(1)}, f32[2,32,128]{2,1,0:T(8,128)S(1)}, bf16[16,128,256]{2,1,0:T(8,128)(2,1)S(1)}, s32[49]{0:T(128)S(1)}) custom-call(s32[100]{0:T(128)S(1)} %copy-done.4, bf16[4,32,128]{2,1,0:T(8,128)(2,1)S(1)} %copy-done, bf16[4,4,256]{2,1,0:T(4,128)(2,1)S(1)} %bitcast.2, ...), custom_call_target="tpu_custom_call" | custom-call | flops 134217728 | bytes 8388608 | tf_op jit(solution)/shard_map/own_first/pallas_call | solution.py:409
  16.4 3.6 %all-to-all-done.asked_ref = bf16[16,72,128]{2,1,0:T(8,128)(2,1)S(1)} async-done(((bf16[16,72,128]{2,1,0:T(8,128)(2,1)}), bf16[16,72,128]{2,1,0:T(8,128)(2,1)S(1)}, u32[]{:S(2)}, u32[]{:S(2)}) %all-to-all-start) | async-done | bytes 294944 | tf_op jit(solution)/shard_map/all_to_all | solution.py:399
  20.0 1.9 %answer.1.after_ref = bf16[16,72,128]{2,1,0:T(8,128)(2,1)} custom-call(s32[49]{0:T(128)S(1)} %get-tuple-element.19.place_ref.slot_ref, bf16[16,72,128]{2,1,0:T(8,128)(2,1)S(1)} %all-to-all-done.asked_ref, bf16[16,128,256]{2,1,0:T(8,128)(2,1)S(1)} %get-tuple-element.21.sent_ref), custom_call_target="tpu_custom_call" | custom-call | tf_op jit(solution)/shard_map/answer/pallas_call | solution.py:430
  21.9 4.0 %all-to-all-start.1 = ((bf16[16,72,128]{2,1,0:T(8,128)(2,1)}), bf16[16,72,128]{2,1,0:T(8,128)(2,1)S(1)}, u32[]{:S(2)}, u32[]{:S(2)}) async-start(bf16[16,72,128]{2,1,0:T(8,128)(2,1)} %answer.1.after_ref), calls=%async_computation.1 | async-start | bytes 589824 | tf_op jit(solution)/shard_map/all_to_all | solution.py:442
  25.9 0.0 copy-done.1
  25.9 0.0 copy-done.3
  25.9 0.0 copy-done.5
  25.9 3.6 %own_second.1 = (f32[2,32,128]{2,1,0:T(8,128)S(1)}, f32[2,32,128]{2,1,0:T(8,128)S(1)}, f32[2,32,128]{2,1,0:T(8,128)S(1)}, bf16[1024,1280]{1,0:T(8,128)(2,1)S(1)}) custom-call(s32[100]{0:T(128)S(1)} %copy-done.5, bf16[4,32,128]{2,1,0:T(8,128)(2,1)S(1)} %copy-done.1, bf16[4,4,256]{2,1,0:T(4,128)(2,1)S(1)} %bitcast.3, bf16[96,128,256]{2,1,0:T(8,128)(2,1)} %bitcast.5, ...), custom_call_target="tpu_custom_call" | custom-call | flops 134217728 | bytes 8388608 | tf_op jit(solution)/shard_map/own_second/pallas_call | solution.py:445
  29.5 6.3 %all-to-all-done.1.back_ref = bf16[16,72,128]{2,1,0:T(8,128)(2,1)S(1)} async-done(((bf16[16,72,128]{2,1,0:T(8,128)(2,1)}), bf16[16,72,128]{2,1,0:T(8,128)(2,1)S(1)}, u32[]{:S(2)}, u32[]{:S(2)}) %all-to-all-start.1) | async-done | bytes 294944 | tf_op jit(solution)/shard_map/all_to_all | solution.py:442
  35.8 6.7 %project.1 = bf16[8,16,1024]{2,1,0:T(8,128)(2,1)S(1)} custom-call(s32[49]{0:T(128)S(1)} %get-tuple-element.19.place_ref.slot_ref, bf16[16,72,128]{2,1,0:T(8,128)(2,1)S(1)} %all-to-all-done.1.back_ref, f32[2,32,128]{2,1,0:T(8,128)S(1)} %get-tuple-element.22.peak_a, f32[2,32,128]{2,1,0:T(8,128)S(1)} %get-tuple-element.23.sum_a, ...), custom_call_target="tpu_custom_call" | custom-call | tf_op jit(solution)/shard_map/project/pallas_call | solution.py:461
  42.5 11.1 %all_to_all.15 = bf16[8,16,1024]{2,1,0:T(8,128)(2,1)S(1)} all-to-all(bf16[8,16,1024]{2,1,0:T(8,128)(2,1)S(1)} %project.1), channel_id=1, replica_groups=mesh['inst'=16,'tp'=8] {'tp'}, dimensions={0} | all-to-all | bytes 524288 | tf_op jit(solution)/shard_map/all_to_all | solution.py:477
  53.6 0.6 %reshape.11 = bf16[4,4,1024]{2,1,0:T(4,128)(2,1)} reshape(bf16[16,1024]{1,0:T(8,128)(2,1)S(1)} %reduce_sum.12) | data formatting | bytes 65536 | tf_op jit(solution)/shard_map/reshape | solution.py:479
  (1 shorter events, 0.0 us)
Async XLA Ops:
  1.9 24.0 %copy-start.1 = (bf16[4,32,128]{2,1,0:T(8,128)(2,1)S(1)}, bf16[4,32,128]{2,1,0:T(8,128)(2,1)}, u32[]{:S(2)}) copy-start(bf16[4,32,128]{2,1,0:T(8,128)(2,1)} %get-tuple-element.18.q_ref) | copy-start | bytes 98308
  1.9 24.0 %copy-start.3 = (bf16[4,4,1,256]{3,1,2,0:T(4,128)(2,1)S(1)}, bf16[4,4,1,256]{3,1,2,0:T(4,128)(2,1)}, u32[]{:S(2)}) copy-start(bf16[4,4,1,256]{3,1,2,0:T(4,128)(2,1)} %param.9) | copy-start | bytes 24580
  1.9 24.0 %copy-start.5 = (s32[100]{0:T(128)S(1)}, s32[100]{0:T(128)}, u32[]{:S(2)}) copy-start(s32[100]{0:T(128)} %get-tuple-element.17.plan_ref) | copy-start | bytes 1204
  2.0 18.1 %all-to-all-start = ((bf16[16,72,128]{2,1,0:T(8,128)(2,1)}), bf16[16,72,128]{2,1,0:T(8,128)(2,1)S(1)}, u32[]{:S(2)}, u32[]{:S(2)}) async-start(bf16[16,72,128]{2,1,0:T(8,128)(2,1)} %get-tuple-element.20), calls=%async_computation | async-start | bytes 589824 | tf_op jit(solution)/shard_map/all_to_all | solution.py:399
  10.1 0.8 %copy-start = (bf16[4,32,128]{2,1,0:T(8,128)(2,1)S(1)}, bf16[4,32,128]{2,1,0:T(8,128)(2,1)}, u32[]{:S(2)}) copy-start(bf16[4,32,128]{2,1,0:T(8,128)(2,1)} %get-tuple-element.18.q_ref) | copy-start | bytes 98308
  10.9 0.7 %copy-start.2 = (bf16[4,4,1,256]{3,1,2,0:T(4,128)(2,1)S(1)}, bf16[4,4,1,256]{3,1,2,0:T(4,128)(2,1)}, u32[]{:S(2)}) copy-start(bf16[4,4,1,256]{3,1,2,0:T(4,128)(2,1)} %param.9) | copy-start | bytes 24580
  11.6 0.7 %copy-start.4 = (s32[100]{0:T(128)S(1)}, s32[100]{0:T(128)}, u32[]{:S(2)}) copy-start(s32[100]{0:T(128)} %get-tuple-element.17.plan_ref) | copy-start | bytes 1204
  21.9 13.9 %all-to-all-start.1 = ((bf16[16,72,128]{2,1,0:T(8,128)(2,1)}), bf16[16,72,128]{2,1,0:T(8,128)(2,1)S(1)}, u32[]{:S(2)}, u32[]{:S(2)}) async-start(bf16[16,72,128]{2,1,0:T(8,128)(2,1)} %answer.1.after_ref), calls=%async_computation.1 | async-start | bytes 589824 | tf_op jit(solution)/shard_map/all_to_all | solution.py:442

commit v4 on v3

--- a/solution.py
+++ b/solution.py
@@ -11,6 +11,7 @@
 INFO = 8
 MASKED = -1e30
 TILE = 256
+FRESH = 8
 
 SMEM = pl.BlockSpec(memory_space=pltpu.SMEM)
 VMEM = pl.BlockSpec(memory_space=pltpu.VMEM)
@@ -30,13 +31,13 @@
 
 
 def ask_kernel(
-    pool_size, block_len, table_hbm, len_hbm, block_hbm, dest_hbm, q_hbm,
+    pool_size, block_len, table_hbm, len_hbm, block_hbm, dest_hbm, q_hbm, new_hbm,
     out_ref, query_ref, plan_ref,
-    table_ref, len_ref, block_ref, dest_ref, code_ref, live_ref, q_ref, rows_ref, sems,
+    table_ref, len_ref, block_ref, dest_ref, code_ref, live_ref, q_ref, new_ref, rows_ref, sems,
 ):
     slots, blocks = table_ref.shape
     steps = q_ref.shape[0]
-    rows, head = query_ref.shape[1:]
+    rows, head = query_ref.shape[1] - 2 * FRESH, query_ref.shape[2]
     group = rows // steps
     arrivals = out_ref.shape[0] * CAP
     copies = [
@@ -44,6 +45,7 @@
         for k, (source, target) in enumerate(
             (
                 (q_hbm, q_ref),
+                (new_hbm, new_ref),
                 (table_hbm, table_ref),
                 (len_hbm, len_ref),
                 (block_hbm, block_ref),
@@ -53,6 +55,7 @@
     ]
     for copy in copies:
         copy.start()
+    rows_ref[:, rows:, :] = jnp.zeros((slots, 2 * FRESH, head), jnp.float32)
     for a in range(arrivals):
         code_ref[a] = 0
         live_ref[a] = 0
@@ -64,6 +67,11 @@
             for g in range(group):
                 at = step * group + g
                 rows_ref[slot, at : at + 1, :] = query[slot : slot + 1, g * head : (g + 1) * head]
+        fresh = new_ref[step].astype(jnp.float32)
+        for slot in range(slots):
+            for k in range(2):
+                at = rows + k * FRESH + step
+                rows_ref[slot, at : at + 1, :] = fresh[slot : slot + 1, k * head : (k + 1) * head]
     for slot in range(slots):
         length = len_ref[slot]
         for b in range(blocks):
@@ -77,7 +85,7 @@
     row = lax.broadcasted_iota(jnp.int32, (INFO, head), 0)
     for a in range(arrivals):
         source, rank = a // CAP, a % CAP
-        out_ref[source, rank * rows : (rank + 1) * rows, :] = query_ref[code_ref[a]]
+        out_ref[source, rank * rows : (rank + 1) * rows, :] = query_ref[code_ref[a], :rows, :]
     for source in range(arrivals // CAP):
         live = jnp.where(row < INFO // 2, live_ref[source * CAP], live_ref[source * CAP + 1])
         out_ref[source, CAP * rows :, :] = live.astype(jnp.float32).astype(jnp.bfloat16)
@@ -90,12 +98,11 @@
 
 def own_kernel(
     scale, head_group, blocks, first,
-    plan_ref, q_ref, new_ref, pool_ref,
+    steps, plan_ref, q_ref, pool_ref,
     peak_ref, sum_ref, acc_ref, kv_ref, sems, bring,
 ):
     pool_size, block_len, _ = pool_ref.shape
-    slots, rows, head = q_ref.shape
-    steps = new_ref.shape[0]
+    slots, rows, head = q_ref.shape[0], q_ref.shape[1] - 2 * FRESH, q_ref.shape[2]
     span = blocks * block_len
     len_at = slots * blocks
     mine = range(first, first + peak_ref.shape[0])
@@ -115,17 +122,16 @@
     lane = lax.broadcasted_iota(jnp.int32, (rows, block_len), 1)
     step = lax.broadcasted_iota(jnp.int32, (rows, block_len), 0) // head_group
     for slot in mine:
-        fresh = jnp.concatenate(
-            [new_ref[u, slot : slot + 1, :].astype(jnp.float32) for u in range(steps)]
-            + [jnp.zeros((block_len - steps, 2 * head), jnp.float32)],
-            axis=0,
-        )
-        kv_ref[slot - first, span:, :] = fresh.astype(jnp.bfloat16)
+        fresh = q_ref[slot, rows:, :].astype(jnp.float32)
+        rest = jnp.zeros((block_len - FRESH, head), jnp.float32)
+        for k in range(2):
+            part = jnp.concatenate([fresh[k * FRESH : (k + 1) * FRESH], rest], axis=0)
+            kv_ref[slot - first, span:, k * head : (k + 1) * head] = part.astype(jnp.bfloat16)
     for slot in mine:
         for b in range(blocks):
             own_copy(slot, b).wait()
         scores = lax.dot_general(
-            q_ref[slot], kv_ref[slot - first, :, :head], nt_dims, preferred_element_type=jnp.float32
+            q_ref[slot, :rows, :], kv_ref[slot - first, :, :head], nt_dims, preferred_element_type=jnp.float32
         ) * scale
         parts_s = []
         for b in range(blocks):
@@ -138,15 +144,17 @@
         weights = [jnp.exp(part - peak) for part in parts_s]
         total = jnp.sum(functools.reduce(jnp.add, weights), axis=1, keepdims=True)
         acc_ref[slot - first] = split_dot(jnp.concatenate(weights, axis=1), kv_ref[slot - first, :, head:])
-        peak_ref[slot - first] = jnp.broadcast_to(peak, (rows, head))
-        sum_ref[slot - first] = jnp.broadcast_to(total, (rows, head))
+        same = lane % rows == lax.broadcasted_iota(jnp.int32, (rows, block_len), 0)
+        for ref, column in ((peak_ref, peak), (sum_ref, total)):
+            across = jnp.sum(jnp.where(same, column, 0.0), axis=0, keepdims=True)
+            ref[slot - first] = jnp.broadcast_to(across, ref.shape[1:])
     for copy in brought:
         copy.wait()
 
 
 def first_kernel(
-    scale, head_group, blocks,
-    plan_ref, q_ref, new_ref, pool_ref,
+    scale, head_group, blocks, steps,
+    plan_ref, q_ref, pool_ref,
     peak_ref, sum_ref, acc_ref, sent_ref, place_ref,
     seen_ref, kv_ref, sems, sent_sems,
 ):
@@ -183,14 +191,14 @@
         return copies
 
     own_kernel(
-        scale, head_group, blocks, 0, plan_ref, q_ref, new_ref, pool_ref,
+        scale, head_group, blocks, 0, steps, plan_ref, q_ref, pool_ref,
         peak_ref, sum_ref, acc_ref, kv_ref, sems, bring,
     )
 
 
 def second_kernel(
-    scale, head_group, blocks, first,
-    plan_ref, q_ref, new_ref, pool_ref, weight_ref, after_ref,
+    scale, head_group, blocks, steps, first,
+    plan_ref, q_ref, pool_ref, weight_ref, after_ref,
     peak_ref, sum_ref, acc_ref, held_ref,
     kv_ref, sems, weight_sem,
 ):
@@ -204,7 +212,7 @@
         return [copy]
 
     own_kernel(
-        scale, head_group, blocks, first, plan_ref, q_ref, new_ref, pool_ref,
+        scale, head_group, blocks, first, steps, plan_ref, q_ref, pool_ref,
         peak_ref, sum_ref, acc_ref, kv_ref, sems, bring,
     )
 
@@ -223,6 +231,7 @@
     head = width // 2
     n_inst = out_ref.shape[0]
     rows = (out_ref.shape[1] - INFO) // CAP
+    out_ref[...] = jnp.zeros_like(out_ref)
     peak_ref[...] = jnp.zeros_like(peak_ref)
     sum_ref[...] = jnp.zeros_like(sum_ref)
     lane = lax.broadcasted_iota(jnp.int32, (rows, block_len), 1)
@@ -275,16 +284,23 @@
         out_ref[i, CAP * rows :, :] = info.astype(jnp.bfloat16)
 
 
+def over_groups(combine, row, size):
+    shift = row.shape[1] // 2
+    while shift >= size:
+        row = combine(row, pltpu.roll(row, shift, axis=1))
+        shift //= 2
+    return row
+
+
 def project_kernel(
     first_slot, slot_ref, back_ref, peak_a, sum_a, acc_a, peak_b, sum_b, acc_b,
-    held_ref, weight_ref, out_ref,
-    m_ref, l_ref, a_ref, att_ref, w_ref, sems,
+    held_ref, weight_ref, out_ref, att_ref, w_ref, sems,
 ):
-    slots, rows, head = a_ref.shape
+    half, rows, head = acc_a.shape
+    slots = half + acc_b.shape[0]
     n_inst = back_ref.shape[0]
     parts, out_rows, part_cols = out_ref.shape
     held = held_ref.shape[1]
-    half = acc_a.shape[0]
     steps = out_rows // slots
     group = rows // steps
     copies = {}
@@ -297,39 +313,65 @@
                 sems.at[c],
             )
             copies[c].start()
-    lane = lax.broadcasted_iota(jnp.int32, (rows, head), 1)
-    row = lax.broadcasted_iota(jnp.int32, (rows, head), 0)
-    arrivals = []
+    across = head // rows
+    lines = n_inst * CAP // across
+    line = lax.broadcasted_iota(jnp.int32, (lines, head), 0)
+    lane_group = lax.broadcasted_iota(jnp.int32, (lines, head), 1) // rows
+    slot_of = jnp.full((lines, head), -1, jnp.int32)
+    for j in range(lines):
+        for i in range(across):
+            here = (line == j) & (lane_group == i)
+            slot_of = jnp.where(here, slot_ref[first_slot + j * across + i], slot_of)
+    apart = across // CAP
+    peak_rows, sum_rows = [], []
+    for s in range(n_inst):
+        info = back_ref[s, CAP * rows :, :].astype(jnp.float32)
+        peak_rows.append(info[0:1] + info[1:2] + info[2:3])
+        sum_rows.append(info[3:4] + info[4:5] + info[5:6])
+
+    def together(per_source):
+        total = None
+        for k in range(apart):
+            part = jnp.concatenate(per_source[k::apart], axis=0)
+            if k:
+                part = pltpu.roll(part, k * CAP * rows, axis=1)
+            total = part if total is None else total + part
+        return total
+
+    peaks, sums = together(peak_rows), together(sum_rows)
     peak_own = [peak_a[k] for k in range(half)] + [peak_b[k] for k in range(slots - half)]
     sum_own = [sum_a[k] for k in range(half)] + [sum_b[k] for k in range(slots - half)]
     acc_own = [acc_a[k] for k in range(half)] + [acc_b[k] for k in range(slots - half)]
-    best = list(peak_own)
-    for s in range(n_inst):
-        info = back_ref[s, CAP * rows :, :].astype(jnp.float32)
-        peaks = info[0:1] + info[1:2] + info[2:3]
-        sums = info[3:4] + info[4:5] + info[5:6]
-        for r in range(CAP):
-            slot = slot_ref[first_slot + s * CAP + r]
-            here = lane == row + r * rows
-            peak = jnp.sum(jnp.where(here, peaks, 0.0), axis=1, keepdims=True)
-            total = jnp.sum(jnp.where(here, sums, 0.0), axis=1, keepdims=True)
-            arrivals.append((slot, peak, total))
-            for k in range(slots):
-                best[k] = jnp.maximum(best[k], jnp.where(slot == k, peak, MASKED))
+    best, best_of = [], jnp.zeros((lines, head), jnp.float32)
     for k in range(slots):
+        top = jnp.max(jnp.where(slot_of == k, peaks, MASKED), axis=0, keepdims=True)
+        best.append(jnp.maximum(over_groups(jnp.maximum, top, rows), peak_own[k]))
+        best_of = jnp.where(slot_of == k, best[k], best_of)
+    gains = jnp.where(slot_of >= 0, sums * jnp.exp(peaks - best_of), 0.0)
+    keeps, matrix = [], []
+    same = lax.broadcasted_iota(jnp.int32, (rows, head), 1) % rows == lax.broadcasted_iota(
+        jnp.int32, (rows, head), 0
+    )
+    first_group = lax.broadcasted_iota(jnp.int32, (rows, head), 1) < rows
+    for k in range(slots):
+        mine = jnp.where(slot_of == k, gains, 0.0)
         keep = jnp.exp(peak_own[k] - best[k])
-        m_ref[k] = best[k]
-        l_ref[k] = sum_own[k] * keep
-        a_ref[k] = acc_own[k] * keep
-    for a, (slot, peak, total) in enumerate(arrivals):
-        s, r = a // CAP, a % CAP
-        at = jnp.maximum(slot, 0)
-        gain = jnp.where(slot >= 0, total * jnp.exp(peak - m_ref[at]), 0.0)
-        values = back_ref[s, r * rows : (r + 1) * rows, :].astype(jnp.float32)
-        l_ref[at] += gain
-        a_ref[at] += jnp.where(slot >= 0, gain * values, 0.0)
+        total = over_groups(jnp.add, jnp.sum(mine, axis=0, keepdims=True), rows)
+        inverse = 1.0 / (total + sum_own[k] * keep)
+        keep = (keep * inverse)[0:1]
+        keeps.append(
+            jnp.sum(jnp.where(same & first_group, keep, 0.0), axis=1, keepdims=True)
+        )
+        mine = mine * inverse
+        matrix.append(
+            jnp.concatenate(
+                [jnp.where(same, mine[j : j + 1], 0.0) for j in range(lines)], axis=1
+            )
+        )
+    values = back_ref[:, : CAP * rows, :].reshape(n_inst * CAP * rows, head)
+    arrived = split_dot(jnp.concatenate(matrix, axis=0), values)
     for slot in range(slots):
-        done = a_ref[slot] / l_ref[slot]
+        done = keeps[slot] * acc_own[slot] + arrived[slot * rows : (slot + 1) * rows]
         for step in range(steps):
             for g in range(group):
                 at = step * group + g
@@ -377,10 +419,10 @@
         functools.partial(ask_kernel, pool_size, block_len),
         out_shape=(
             packet,
-            shape((slots, rows, head), bf16),
+            shape((slots, rows + 2 * FRESH, head), bf16),
             shape((slots * blocks + slots + 2 * entries,), i32),
         ),
-        in_specs=[HBM] * 5,
+        in_specs=[HBM] * 6,
         out_specs=(VMEM, VMEM, SMEM),
         scratch_shapes=[
             pltpu.SMEM((slots, blocks), i32),
@@ -390,16 +432,18 @@
             pltpu.SMEM((arrivals + 1,), i32),
             pltpu.SMEM((arrivals + 1,), i32),
             pltpu.VMEM(queries.shape, bf16),
-            pltpu.VMEM((slots, rows, head), f32),
-            pltpu.SemaphoreType.DMA((5,)),
+            pltpu.VMEM(fresh.shape, bf16),
+            pltpu.VMEM((slots, rows + 2 * FRESH, head), f32),
+            pltpu.SemaphoreType.DMA((6,)),
         ],
         compiler_params=params(64),
         name="ask",
-    )(block_table, cache_len, send_block, send_dest, queries)
+    )(block_table, cache_len, send_block, send_dest, queries, fresh)
     asked = lax.all_to_all(ask, "inst", 0, 0, tiled=True)
 
     half = slots // 2
     own = shape((half, rows, head), f32)
+    stat = shape((half, 8, head), f32)
     kv_scratch = pltpu.VMEM((half, (blocks + 1) * block_len, width), bf16)
     own_cost = pl.CostEstimate(
         flops=2 * slots * rows * blocks * block_len * width,
@@ -407,13 +451,13 @@
         transcendentals=half * rows * blocks * block_len,
     )
     peak_a, sum_a, acc_a, sent, place = pl.pallas_call(
-        functools.partial(first_kernel, scale, group, blocks),
+        functools.partial(first_kernel, scale, group, blocks, steps),
         out_shape=(
-            own, own, own,
+            stat, stat, own,
             shape((entries, block_len, width), bf16),
             shape((entries + arrivals + 1,), i32),
         ),
-        in_specs=[SMEM, VMEM, VMEM, HBM],
+        in_specs=[SMEM, VMEM, HBM],
         out_specs=(VMEM, VMEM, VMEM, VMEM, SMEM),
         scratch_shapes=[
             pltpu.SMEM((n_inst,), i32),
@@ -424,7 +468,7 @@
         compiler_params=params(50),
         cost_estimate=own_cost,
         name="own_first",
-    )(plan, slot_query, fresh, pool)
+    )(plan, slot_query, pool)
 
     part_cols = columns // n_tp
     answer = pl.pallas_call(
@@ -443,9 +487,9 @@
 
     ahead = 5 * TILE
     peak_b, sum_b, acc_b, held = pl.pallas_call(
-        functools.partial(second_kernel, scale, group, blocks, half),
-        out_shape=(own, own, own, shape((head_width, ahead), bf16)),
-        in_specs=[SMEM, VMEM, VMEM, HBM, HBM, pl.BlockSpec(memory_space=pl.ANY)],
+        functools.partial(second_kernel, scale, group, blocks, steps, half),
+        out_shape=(stat, stat, own, shape((head_width, ahead), bf16)),
+        in_specs=[SMEM, VMEM, HBM, HBM, pl.BlockSpec(memory_space=pl.ANY)],
         out_specs=(VMEM, VMEM, VMEM, VMEM),
         scratch_shapes=[
             kv_scratch,
@@ -455,7 +499,7 @@
         compiler_params=params(50),
         cost_estimate=own_cost,
         name="own_second",
-    )(plan, slot_query, fresh, pool, out_weight, answer)
+    )(plan, slot_query, pool, out_weight, answer)
 
     out_rows = steps * slots
     partial_out = pl.pallas_call(
@@ -464,9 +508,6 @@
         in_specs=[SMEM] + [VMEM] * 8 + [HBM],
         out_specs=VMEM,
         scratch_shapes=[
-            pltpu.VMEM((slots, rows, head), f32),
-            pltpu.VMEM((slots, rows, head), f32),
-            pltpu.VMEM((slots, rows, head), f32),
             pltpu.VMEM((out_rows, head_width), f32),
             pltpu.VMEM((head_width, columns - ahead), bf16),
             pltpu.SemaphoreType.DMA((n_tp,)),

time: 54.8 us -> 54.5 us (level)
  local copies, waits for them, and re-layouts: 2.78 us -> 2.09 us
    unnamed x12 -> x8, local copies, waits for them, and re-layouts: 2.15 us -> 1.46 us
  transfers between devices with their start and end apart: 2 -> 2, of which waited for: 2 -> 2; matrix products, arithmetic and copies ran while one was open for 0% -> 0% of each run, Pallas kernels for 14% -> 15%
where the time goes in v4:
time: 54.5 us; the launch traced here: 54 us
  Pallas kernels  18.6 us (34%)
  starting transfers between devices  11.8 us (22%)
  blocking collectives  11.1 us (20%)
  waiting for transfers between devices  10.1 us (19%)
  local copies, waits for them, and re-layouts  2.09 us (4%)
    all_to_all x1, blocking collectives, shards(): shares = lax.all_to_all(partial_out, 'tp', 0, 0, tiled=True)  11.1 us
    all_to_all x1, starting transfers between devices, shards(): asked = lax.all_to_all(ask, 'inst', 0, 0, tiled=True)  8.28 us
    pallas_call x1, Pallas kernels, shards(): pl.pallas_call(functools.partial(project_kernel, entries), out_shape=shap...  6.63 us
    all_to_all x1, waiting for transfers between devices, shards(): back = lax.all_to_all(answer, 'inst', 0, 0, tiled=True)  6.01 us
    pallas_call x1, Pallas kernels, shards(): pl.pallas_call(functools.partial(first_kernel, scale, group, blocks, step...  4.33 us
    all_to_all x1, waiting for transfers between devices, shards(): asked = lax.all_to_all(ask, 'inst', 0, 0, tiled=True)  4.11 us
    pallas_call x1, Pallas kernels, shards(): pl.pallas_call(functools.partial(second_kernel, scale, group, blocks, ste...  3.83 us
    all_to_all x1, starting transfers between devices, shards(): back = lax.all_to_all(answer, 'inst', 0, 0, tiled=True)  3.54 us
  transfers between devices with their start and end apart: 2, of which 2 were waited for; matrix products, arithmetic and copies ran while one was open for 0% of the time, Pallas kernels for 15%

profile of v4, /device:TPU:0, one launch (start us, length us, event | category | flops | bytes accessed | tf_op | source)
XLA Modules:
  0.0 54.0 jit_solution(9606072534816278459)
XLA Ops:
  0.0 1.9 %ask.1 = (bf16[16,72,128]{2,1,0:T(8,128)(2,1)}, bf16[4,48,128]{2,1,0:T(8,128)(2,1)}, s32[100]{0:T(128)}) custom-call(s32[4,16]{1,0:T(4,128)} %table_hbm.1, s32[4]{0:T(128)} %len_hbm.1, s32[16]{0:T(128)} %block_hbm.1, s32[16]{0:T(128)} %dest_hbm.1, bf16[4,4,1024]{2,1,0:T(4,128)(2,1)} %q_hbm.1, bf16[4,4,256]{2,1,0:T(4,128)(2,1)} %bitcast.4), custom_call_target="tpu_custom_call" | custom-call | tf_op jit(solution)/shard_map/ask/pallas_call | solution.py:418
  1.9 0.0 copy-start.1
  2.0 0.0 copy-start.3
  2.0 8.3 %all-to-all-start = ((bf16[16,72,128]{2,1,0:T(8,128)(2,1)}), bf16[16,72,128]{2,1,0:T(8,128)(2,1)S(1)}, u32[]{:S(2)}, u32[]{:S(2)}) async-start(bf16[16,72,128]{2,1,0:T(8,128)(2,1)} %get-tuple-element.20), calls=%async_computation | async-start | bytes 589824 | tf_op jit(solution)/shard_map/all_to_all | solution.py:442
  10.2 0.0 copy-start
  10.3 0.8 %copy-done = bf16[4,48,128]{2,1,0:T(8,128)(2,1)S(1)} copy-done((bf16[4,48,128]{2,1,0:T(8,128)(2,1)S(1)}, bf16[4,48,128]{2,1,0:T(8,128)(2,1)}, u32[]{:S(2)}) %copy-start) | copy-done | bytes 49176
  11.0 0.0 copy-start.2
  11.0 0.7 %copy-done.2 = s32[100]{0:T(128)S(1)} copy-done((s32[100]{0:T(128)S(1)}, s32[100]{0:T(128)}, u32[]{:S(2)}) %copy-start.2) | copy-done | bytes 424
  11.7 4.3 %own_first.1 = (f32[2,8,128]{2,1,0:T(8,128)S(1)}, f32[2,8,128]{2,1,0:T(8,128)S(1)}, f32[2,32,128]{2,1,0:T(8,128)S(1)}, bf16[16,128,256]{2,1,0:T(8,128)(2,1)S(1)}, s32[49]{0:T(128)S(1)}) custom-call(s32[100]{0:T(128)S(1)} %copy-done.2, bf16[4,48,128]{2,1,0:T(8,128)(2,1)S(1)} %copy-done, bf16[96,128,256]{2,1,0:T(8,128)(2,1)} %bitcast.2), custom_call_target="tpu_custom_call" | custom-call | flops 134217728 | bytes 8388608 | tf_op jit(solution)/shard_map/own_first/pallas_call | solution.py:453
  16.0 4.1 %all-to-all-done.asked_ref = bf16[16,72,128]{2,1,0:T(8,128)(2,1)S(1)} async-done(((bf16[16,72,128]{2,1,0:T(8,128)(2,1)}), bf16[16,72,128]{2,1,0:T(8,128)(2,1)S(1)}, u32[]{:S(2)}, u32[]{:S(2)}) %all-to-all-start) | async-done | bytes 294944 | tf_op jit(solution)/shard_map/all_to_all | solution.py:442
  20.2 1.9 %answer.1.after_ref = bf16[16,72,128]{2,1,0:T(8,128)(2,1)} custom-call(s32[49]{0:T(128)S(1)} %get-tuple-element.19.place_ref.slot_ref, bf16[16,72,128]{2,1,0:T(8,128)(2,1)S(1)} %all-to-all-done.asked_ref, bf16[16,128,256]{2,1,0:T(8,128)(2,1)S(1)} %get-tuple-element.21.sent_ref), custom_call_target="tpu_custom_call" | custom-call | tf_op jit(solution)/shard_map/answer/pallas_call | solution.py:474
  22.1 3.5 %all-to-all-start.1 = ((bf16[16,72,128]{2,1,0:T(8,128)(2,1)}), bf16[16,72,128]{2,1,0:T(8,128)(2,1)S(1)}, u32[]{:S(2)}, u32[]{:S(2)}) async-start(bf16[16,72,128]{2,1,0:T(8,128)(2,1)} %answer.1.after_ref), calls=%async_computation.1 | async-start | bytes 589824 | tf_op jit(solution)/shard_map/all_to_all | solution.py:486
  25.6 0.0 copy-done.1
  25.6 0.0 copy-done.3
  25.6 3.8 %own_second.1 = (f32[2,8,128]{2,1,0:T(8,128)S(1)}, f32[2,8,128]{2,1,0:T(8,128)S(1)}, f32[2,32,128]{2,1,0:T(8,128)S(1)}, bf16[1024,1280]{1,0:T(8,128)(2,1)S(1)}) custom-call(s32[100]{0:T(128)S(1)} %copy-done.3, bf16[4,48,128]{2,1,0:T(8,128)(2,1)S(1)} %copy-done.1, bf16[96,128,256]{2,1,0:T(8,128)(2,1)} %bitcast.3, bf16[1024,8192]{1,0:T(8,128)(2,1)} %weight_ref.3, ...), custom_call_target="tpu_custom_call" | custom-call | flops 134217728 | bytes 8388608 | tf_op jit(solution)/shard_map/own_second/pallas_call | solution.py:489
  29.5 6.0 %all-to-all-done.1.back_ref = bf16[16,72,128]{2,1,0:T(8,128)(2,1)S(1)} async-done(((bf16[16,72,128]{2,1,0:T(8,128)(2,1)}), bf16[16,72,128]{2,1,0:T(8,128)(2,1)S(1)}, u32[]{:S(2)}, u32[]{:S(2)}) %all-to-all-start.1) | async-done | bytes 294944 | tf_op jit(solution)/shard_map/all_to_all | solution.py:486
  35.5 6.6 %project.1 = bf16[8,16,1024]{2,1,0:T(8,128)(2,1)S(1)} custom-call(s32[49]{0:T(128)S(1)} %get-tuple-element.19.place_ref.slot_ref, bf16[16,72,128]{2,1,0:T(8,128)(2,1)S(1)} %all-to-all-done.1.back_ref, f32[2,8,128]{2,1,0:T(8,128)S(1)} %get-tuple-element.22.peak_a, f32[2,8,128]{2,1,0:T(8,128)S(1)} %get-tuple-element.23.sum_a, ...), custom_call_target="tpu_custom_call" | custom-call | tf_op jit(solution)/shard_map/project/pallas_call | solution.py:505
  42.1 11.1 %all_to_all.15 = bf16[8,16,1024]{2,1,0:T(8,128)(2,1)S(1)} all-to-all(bf16[8,16,1024]{2,1,0:T(8,128)(2,1)S(1)} %project.1), channel_id=1, replica_groups=mesh['inst'=16,'tp'=8] {'tp'}, dimensions={0} | all-to-all | bytes 524288 | tf_op jit(solution)/shard_map/all_to_all | solution.py:518
  53.3 0.6 %reshape.11 = bf16[4,4,1024]{2,1,0:T(4,128)(2,1)} reshape(bf16[16,1024]{1,0:T(8,128)(2,1)S(1)} %reduce_sum.12) | data formatting | bytes 65536 | tf_op jit(solution)/shard_map/reshape | solution.py:520
  (1 shorter events, 0.0 us)
Async XLA Ops:
  1.9 23.7 %copy-start.1 = (bf16[4,48,128]{2,1,0:T(8,128)(2,1)S(1)}, bf16[4,48,128]{2,1,0:T(8,128)(2,1)}, u32[]{:S(2)}) copy-start(bf16[4,48,128]{2,1,0:T(8,128)(2,1)} %get-tuple-element.18.q_ref) | copy-start | bytes 147460
  2.0 23.7 %copy-start.3 = (s32[100]{0:T(128)S(1)}, s32[100]{0:T(128)}, u32[]{:S(2)}) copy-start(s32[100]{0:T(128)} %get-tuple-element.17.plan_ref) | copy-start | bytes 1204
  2.0 18.2 %all-to-all-start = ((bf16[16,72,128]{2,1,0:T(8,128)(2,1)}), bf16[16,72,128]{2,1,0:T(8,128)(2,1)S(1)}, u32[]{:S(2)}, u32[]{:S(2)}) async-start(bf16[16,72,128]{2,1,0:T(8,128)(2,1)} %get-tuple-element.20), calls=%async_computation | async-start | bytes 589824 | tf_op jit(solution)/shard_map/all_to_all | solution.py:442
  10.2 0.8 %copy-start = (bf16[4,48,128]{2,1,0:T(8,128)(2,1)S(1)}, bf16[4,48,128]{2,1,0:T(8,128)(2,1)}, u32[]{:S(2)}) copy-start(bf16[4,48,128]{2,1,0:T(8,128)(2,1)} %get-tuple-element.18.q_ref) | copy-start | bytes 147460
  11.0 0.7 %copy-start.2 = (s32[100]{0:T(128)S(1)}, s32[100]{0:T(128)}, u32[]{:S(2)}) copy-start(s32[100]{0:T(128)} %get-tuple-element.17.plan_ref) | copy-start | bytes 1204
  22.1 13.4 %all-to-all-start.1 = ((bf16[16,72,128]{2,1,0:T(8,128)(2,1)}), bf16[16,72,128]{2,1,0:T(8,128)(2,1)S(1)}, u32[]{:S(2)}, u32[]{:S(2)}) async-start(bf16[16,72,128]{2,1,0:T(8,128)(2,1)} %answer.1.after_ref), calls=%async_computation.1 | async-start | bytes 589824 | tf_op jit(solution)/shard_map/all_to_all | solution.py:486

commit v5 on v4

--- a/solution.py
+++ b/solution.py
@@ -12,10 +12,12 @@
 MASKED = -1e30
 TILE = 256
 FRESH = 8
-
-SMEM = pl.BlockSpec(memory_space=pltpu.SMEM)
+PLAN_ROW = 4
+LENGTH_BASE = 64
+
 VMEM = pl.BlockSpec(memory_space=pltpu.VMEM)
 HBM = pl.BlockSpec(memory_space=pltpu.HBM)
+ANY = pl.BlockSpec(memory_space=pl.ANY)
 
 nt_dims = (((1,), (1,)), ((), ()))
 
@@ -32,7 +34,7 @@
 
 def ask_kernel(
     pool_size, block_len, table_hbm, len_hbm, block_hbm, dest_hbm, q_hbm, new_hbm,
-    out_ref, query_ref, plan_ref,
+    out_ref, query_ref,
     table_ref, len_ref, block_ref, dest_ref, code_ref, live_ref, q_ref, new_ref, rows_ref, sems,
 ):
     slots, blocks = table_ref.shape
@@ -72,6 +74,7 @@
             for k in range(2):
                 at = rows + k * FRESH + step
                 rows_ref[slot, at : at + 1, :] = fresh[slot : slot + 1, k * head : (k + 1) * head]
+    plan = []
     for slot in range(slots):
         length = len_ref[slot]
         for b in range(blocks):
@@ -79,7 +82,16 @@
             arrival = jnp.where(block_id >= pool_size, block_id - pool_size, arrivals)
             code_ref[arrival] = slot
             live_ref[arrival] = jnp.clip(length - b * block_len, 0, block_len)
-            plan_ref[slot * blocks + b] = block_id
+            plan.append(block_id)
+    plan += [len_ref[slot] // LENGTH_BASE for slot in range(slots)]
+    plan += [len_ref[slot] % LENGTH_BASE for slot in range(slots)]
+    plan += [block_ref[e] for e in range(block_ref.shape[0])]
+    plan += [dest_ref[e] for e in range(dest_ref.shape[0])]
+    lane = lax.broadcasted_iota(jnp.int32, (1, head), 1)
+    line = jnp.zeros((1, head), jnp.int32)
+    for k, number in enumerate(plan):
+        line = jnp.where(lane == k, number, line)
+    rows_ref[0, rows + PLAN_ROW : rows + PLAN_ROW + 1, :] = line.astype(jnp.float32)
     for slot in range(slots):
         query_ref[slot] = rows_ref[slot].astype(jnp.bfloat16)
     row = lax.broadcasted_iota(jnp.int32, (INFO, head), 0)
@@ -89,26 +101,34 @@
     for source in range(arrivals // CAP):
         live = jnp.where(row < INFO // 2, live_ref[source * CAP], live_ref[source * CAP + 1])
         out_ref[source, CAP * rows :, :] = live.astype(jnp.float32).astype(jnp.bfloat16)
-    base = slots * blocks
-    for ref in (len_ref, block_ref, dest_ref):
-        for k in range(ref.shape[0]):
-            plan_ref[base + k] = ref[k]
-        base += ref.shape[0]
+
+
+class Plan:
+    def __init__(self, q_ref, blocks, entries):
+        slots, rows = q_ref.shape[0], q_ref.shape[1] - 2 * FRESH
+        row = q_ref[0, rows:, :].astype(jnp.float32)[PLAN_ROW : PLAN_ROW + 1].astype(jnp.int32)
+        numbers = [row[0, k] for k in range(slots * (blocks + 2) + 2 * entries)]
+        at = slots * blocks
+        self.table = [numbers[slot * blocks : (slot + 1) * blocks] for slot in range(slots)]
+        self.length = [
+            numbers[at + slot] * LENGTH_BASE + numbers[at + slots + slot] for slot in range(slots)
+        ]
+        at += 2 * slots
+        self.block, self.dest = numbers[at : at + entries], numbers[at + entries :]
 
 
 def own_kernel(
     scale, head_group, blocks, first,
-    steps, plan_ref, q_ref, pool_ref,
+    steps, plan, q_ref, pool_ref,
     peak_ref, sum_ref, acc_ref, kv_ref, sems, bring,
 ):
     pool_size, block_len, _ = pool_ref.shape
     slots, rows, head = q_ref.shape[0], q_ref.shape[1] - 2 * FRESH, q_ref.shape[2]
     span = blocks * block_len
-    len_at = slots * blocks
     mine = range(first, first + peak_ref.shape[0])
 
     def own_copy(slot, b):
-        block_id = jnp.clip(plan_ref[slot * blocks + b], 0, pool_size - 1)
+        block_id = jnp.clip(plan.table[slot][b], 0, pool_size - 1)
         return pltpu.make_async_copy(
             pool_ref.at[block_id],
             kv_ref.at[slot - first, pl.ds(b * block_len, block_len), :],
@@ -135,8 +155,8 @@
         ) * scale
         parts_s = []
         for b in range(blocks):
-            live = jnp.clip(plan_ref[len_at + slot] - b * block_len, 0, block_len)
-            live = jnp.where(plan_ref[slot * blocks + b] < pool_size, live, 0)
+            live = jnp.clip(plan.length[slot] - b * block_len, 0, block_len)
+            live = jnp.where(plan.table[slot][b] < pool_size, live, 0)
             part = scores[:, b * block_len : (b + 1) * block_len]
             parts_s.append(jnp.where(lane < live, part, MASKED))
         parts_s.append(jnp.where((lane <= step) & (lane < steps), scores[:, span:], MASKED))
@@ -153,52 +173,50 @@
 
 
 def first_kernel(
-    scale, head_group, blocks, steps,
-    plan_ref, q_ref, pool_ref,
-    peak_ref, sum_ref, acc_ref, sent_ref, place_ref,
-    seen_ref, kv_ref, sems, sent_sems,
+    scale, head_group, blocks, steps, n_inst,
+    q_ref, pool_ref,
+    peak_ref, sum_ref, acc_ref, sent_ref, place_ref, slot_ref,
+    kv_ref, sems, sent_sems,
 ):
     pool_size = pool_ref.shape[0]
-    slots = q_ref.shape[0]
+    slots, rows, head = q_ref.shape[0], q_ref.shape[1] - 2 * FRESH, q_ref.shape[2]
     entries = sent_ref.shape[0]
-    n_inst = seen_ref.shape[0]
-    arrivals = n_inst * CAP
-    block_at = slots * blocks + slots
-    dest_at = block_at + entries
+    plan = Plan(q_ref, blocks, entries)
 
     def bring():
         copies = []
         for e in range(entries):
-            block_id = jnp.clip(plan_ref[block_at + e], 0, pool_size - 1)
+            block_id = jnp.clip(plan.block[e], 0, pool_size - 1)
             copies.append(
                 pltpu.make_async_copy(pool_ref.at[block_id], sent_ref.at[e], sent_sems.at[e])
             )
             copies[e].start()
-        for i in range(n_inst):
-            seen_ref[i] = 0
+        lane = lax.broadcasted_iota(jnp.int32, place_ref.shape, 1)
+        places = jnp.zeros(place_ref.shape, jnp.int32)
         for e in range(entries):
-            dest = jnp.clip(plan_ref[dest_at + e], 0, n_inst - 1)
-            rank = seen_ref[dest]
-            seen_ref[dest] = rank + 1
-            place_ref[e] = jnp.minimum(rank, CAP - 1) * n_inst + dest
-        for a in range(arrivals):
-            place_ref[entries + a] = -1
+            dest = jnp.clip(plan.dest[e], 0, n_inst - 1)
+            rank = sum((plan.dest[f] == plan.dest[e]).astype(jnp.int32) for f in range(e))
+            place = jnp.minimum(rank, CAP - 1) * n_inst + dest
+            places = jnp.where(lane == e, place, places)
+        place_ref[...] = places
+        line = lax.broadcasted_iota(jnp.int32, slot_ref.shape, 0)
+        arrival = line * (head // rows) + lax.broadcasted_iota(jnp.int32, slot_ref.shape, 1) // rows
+        slot_of = jnp.full(slot_ref.shape, -1, jnp.int32)
         for slot in range(slots):
             for b in range(blocks):
-                block_id = plan_ref[slot * blocks + b]
-                arrival = jnp.where(block_id >= pool_size, block_id - pool_size, arrivals)
-                place_ref[entries + arrival] = slot
+                slot_of = jnp.where(arrival == plan.table[slot][b] - pool_size, slot, slot_of)
+        slot_ref[...] = slot_of
         return copies
 
     own_kernel(
-        scale, head_group, blocks, 0, steps, plan_ref, q_ref, pool_ref,
+        scale, head_group, blocks, 0, steps, plan, q_ref, pool_ref,
         peak_ref, sum_ref, acc_ref, kv_ref, sems, bring,
     )
 
 
 def second_kernel(
-    scale, head_group, blocks, steps, first,
-    plan_ref, q_ref, pool_ref, weight_ref, after_ref,
+    scale, head_group, blocks, steps, entries, first,
+    q_ref, pool_ref, weight_ref, after_ref,
     peak_ref, sum_ref, acc_ref, held_ref,
     kv_ref, sems, weight_sem,
 ):
@@ -212,7 +230,7 @@
         return [copy]
 
     own_kernel(
-        scale, head_group, blocks, first, steps, plan_ref, q_ref, pool_ref,
+        scale, head_group, blocks, first, steps, Plan(q_ref, blocks, entries), q_ref, pool_ref,
         peak_ref, sum_ref, acc_ref, kv_ref, sems, bring,
     )
 
@@ -238,8 +256,9 @@
     row = lax.broadcasted_iota(jnp.int32, (rows, block_len), 0)
     key = lane.astype(jnp.float32)
     places, starts, masks, scores = [], [], [], []
+    across = place_ref[...]
     for e in range(entries):
-        place = place_ref[e]
+        place = across[0, e]
         dest = lax.rem(place, n_inst)
         rank = lax.div(place, n_inst)
         start = pl.multiple_of(rank * rows, rows)
@@ -293,7 +312,7 @@
 
 
 def project_kernel(
-    first_slot, slot_ref, back_ref, peak_a, sum_a, acc_a, peak_b, sum_b, acc_b,
+    slot_ref, back_ref, peak_a, sum_a, acc_a, peak_b, sum_b, acc_b,
     held_ref, weight_ref, out_ref, att_ref, w_ref, sems,
 ):
     half, rows, head = acc_a.shape
@@ -314,14 +333,8 @@
             )
             copies[c].start()
     across = head // rows
-    lines = n_inst * CAP // across
-    line = lax.broadcasted_iota(jnp.int32, (lines, head), 0)
-    lane_group = lax.broadcasted_iota(jnp.int32, (lines, head), 1) // rows
-    slot_of = jnp.full((lines, head), -1, jnp.int32)
-    for j in range(lines):
-        for i in range(across):
-            here = (line == j) & (lane_group == i)
-            slot_of = jnp.where(here, slot_ref[first_slot + j * across + i], slot_of)
+    slot_of = slot_ref[...]
+    lines = slot_of.shape[0]
     apart = across // CAP
     peak_rows, sum_rows = [], []
     for s in range(n_inst):
@@ -415,15 +428,14 @@
     fresh = new_kv.reshape(steps, slots, width)
 
     packet = shape((n_inst, CAP * rows + INFO, head), bf16)
-    ask, slot_query, plan = pl.pallas_call(
+    ask, slot_query = pl.pallas_call(
         functools.partial(ask_kernel, pool_size, block_len),
         out_shape=(
             packet,
             shape((slots, rows + 2 * FRESH, head), bf16),
-            shape((slots * blocks + slots + 2 * entries,), i32),
         ),
         in_specs=[HBM] * 6,
-        out_specs=(VMEM, VMEM, SMEM),
+        out_specs=(VMEM, VMEM),
         scratch_shapes=[
             pltpu.SMEM((slots, blocks), i32),
             pltpu.SMEM((slots,), i32),
@@ -450,17 +462,17 @@
         bytes_accessed=4 * slots * blocks * block_len * width,
         transcendentals=half * rows * blocks * block_len,
     )
-    peak_a, sum_a, acc_a, sent, place = pl.pallas_call(
-        functools.partial(first_kernel, scale, group, blocks, steps),
+    peak_a, sum_a, acc_a, sent, place, slot_of = pl.pallas_call(
+        functools.partial(first_kernel, scale, group, blocks, steps, n_inst),
         out_shape=(
             stat, stat, own,
             shape((entries, block_len, width), bf16),
-            shape((entries + arrivals + 1,), i32),
+            shape((8, head), i32),
+            shape((arrivals * rows // head, head), i32),
         ),
-        in_specs=[SMEM, VMEM, HBM],
-        out_specs=(VMEM, VMEM, VMEM, VMEM, SMEM),
+        in_specs=[VMEM, HBM],
+        out_specs=(VMEM,) * 6,
         scratch_shapes=[
-            pltpu.SMEM((n_inst,), i32),
             kv_scratch,
             pltpu.SemaphoreType.DMA((half, blocks)),
             pltpu.SemaphoreType.DMA((entries,)),
@@ -468,13 +480,13 @@
         compiler_params=params(50),
         cost_estimate=own_cost,
         name="own_first",
-    )(plan, slot_query, pool)
+    )(slot_query, pool)
 
     part_cols = columns // n_tp
     answer = pl.pallas_call(
         functools.partial(answer_kernel, scale),
         out_shape=packet,
-        in_specs=[SMEM, VMEM, VMEM],
+        in_specs=[VMEM, VMEM, VMEM],
         out_specs=VMEM,
         scratch_shapes=[
             pltpu.VMEM((arrivals, head), f32),
@@ -487,9 +499,9 @@
 
     ahead = 5 * TILE
     peak_b, sum_b, acc_b, held = pl.pallas_call(
-        functools.partial(second_kernel, scale, group, blocks, steps, half),
+        functools.partial(second_kernel, scale, group, blocks, steps, entries, half),
         out_shape=(stat, stat, own, shape((head_width, ahead), bf16)),
-        in_specs=[SMEM, VMEM, HBM, HBM, pl.BlockSpec(memory_space=pl.ANY)],
+        in_specs=[VMEM, HBM, HBM, ANY],
         out_specs=(VMEM, VMEM, VMEM, VMEM),
         scratch_shapes=[
             kv_scratch,
@@ -499,13 +511,13 @@
         compiler_params=params(50),
         cost_estimate=own_cost,
         name="own_second",
-    )(plan, slot_query, pool, out_weight, answer)
+    )(slot_query, pool, out_weight, answer)
 
     out_rows = steps * slots
     partial_out = pl.pallas_call(
-        functools.partial(project_kernel, entries),
+        project_kernel,
         out_shape=shape((n_tp, out_rows, part_cols), bf16),
-        in_specs=[SMEM] + [VMEM] * 8 + [HBM],
+        in_specs=[VMEM] * 9 + [HBM],
         out_specs=VMEM,
         scratch_shapes=[
             pltpu.VMEM((out_rows, head_width), f32),
@@ -514,7 +526,7 @@
         ],
         compiler_params=params(44),
         name="project",
-    )(place, back, peak_a, sum_a, acc_a, peak_b, sum_b, acc_b, held, out_weight)
+    )(slot_of, back, peak_a, sum_a, acc_a, peak_b, sum_b, acc_b, held, out_weight)
     shares = lax.all_to_all(partial_out, "tp", 0, 0, tiled=True)
     total = jnp.sum(shares.astype(f32), axis=0).astype(bf16)
     return total.reshape(steps, slots, columns // n_tp)

time: 54.5 us -> 53.5 us (0.982)
  Pallas kernels: 18.6 us -> 16.5 us
  waiting for transfers between devices: 10.1 us -> 11.9 us
  local copies, waits for them, and re-layouts: 2.09 us -> 1.43 us
    all_to_all x1, waiting for transfers between devices: 4.11 us -> 5.73 us  [shards(): asked = lax.all_to_all(ask, 'inst', 0, 0, tiled=True)]
    pallas_call x1, Pallas kernels: 4.33 us -> 3.37 us  [shards(): pl.pallas_call(functools.partial(first_kernel, scale, group, blocks, step...]
    unnamed x8 -> x4, local copies, waits for them, and re-layouts: 1.46 us -> 0.8 us
  transfers between devices with their start and end apart: 2 -> 2, of which waited for: 2 -> 2; matrix products, arithmetic and copies ran while one was open for 0% -> 0% of each run, Pallas kernels for 15% -> 13%
where the time goes in v5:
time: 53.5 us; the launch traced here: 52.9 us
  Pallas kernels  16.5 us (31%)
  waiting for transfers between devices  11.9 us (22%)
  starting transfers between devices  11.8 us (22%)
  blocking collectives  11.1 us (21%)
  local copies, waits for them, and re-layouts  1.43 us (3%)
    all_to_all x1, blocking collectives, shards(): shares = lax.all_to_all(partial_out, 'tp', 0, 0, tiled=True)  11.1 us
    all_to_all x1, starting transfers between devices, shards(): asked = lax.all_to_all(ask, 'inst', 0, 0, tiled=True)  8.28 us
    all_to_all x1, waiting for transfers between devices, shards(): back = lax.all_to_all(answer, 'inst', 0, 0, tiled=True)  6.16 us
    pallas_call x1, Pallas kernels, shards(): pl.pallas_call(project_kernel, out_shape=shape((n_tp, out_rows, part_cols...  6.09 us
    all_to_all x1, waiting for transfers between devices, shards(): asked = lax.all_to_all(ask, 'inst', 0, 0, tiled=True)  5.73 us
    pallas_call x1, Pallas kernels, shards(): pl.pallas_call(functools.partial(second_kernel, scale, group, blocks, ste...  3.69 us
    all_to_all x1, starting transfers between devices, shards(): back = lax.all_to_all(answer, 'inst', 0, 0, tiled=True)  3.54 us
    pallas_call x1, Pallas kernels, shards(): pl.pallas_call(functools.partial(first_kernel, scale, group, blocks, step...  3.37 us
  transfers between devices with their start and end apart: 2, of which 2 were waited for; matrix products, arithmetic and copies ran while one was open for 0% of the time, Pallas kernels for 13%

profile of v5, /device:TPU:0, one launch (start us, length us, event | category | flops | bytes accessed | tf_op | source)
XLA Modules:
  0.0 52.9 jit_solution(16759101081976628868)
XLA Ops:
  0.0 1.9 %ask.1 = (bf16[16,72,128]{2,1,0:T(8,128)(2,1)}, bf16[4,48,128]{2,1,0:T(8,128)(2,1)}) custom-call(s32[4,16]{1,0:T(4,128)} %table_hbm.1, s32[4]{0:T(128)} %len_hbm.1, s32[16]{0:T(128)} %block_hbm.1, s32[16]{0:T(128)} %dest_hbm.1, bf16[4,4,1024]{2,1,0:T(4,128)(2,1)} %q_hbm.1, bf16[4,4,256]{2,1,0:T(4,128)(2,1)} %bitcast.4), custom_call_target="tpu_custom_call" | custom-call | tf_op jit(solution)/shard_map/ask/pallas_call | solution.py:431
  2.0 0.0 copy-start.1
  2.0 8.3 %all-to-all-start = ((bf16[16,72,128]{2,1,0:T(8,128)(2,1)}), bf16[16,72,128]{2,1,0:T(8,128)(2,1)S(1)}, u32[]{:S(2)}, u32[]{:S(2)}) async-start(bf16[16,72,128]{2,1,0:T(8,128)(2,1)} %get-tuple-element.20), calls=%async_computation | async-start | bytes 589824 | tf_op jit(solution)/shard_map/all_to_all | solution.py:454
  10.2 0.0 copy-start
  10.3 0.8 %copy-done = bf16[4,48,128]{2,1,0:T(8,128)(2,1)S(1)} copy-done((bf16[4,48,128]{2,1,0:T(8,128)(2,1)S(1)}, bf16[4,48,128]{2,1,0:T(8,128)(2,1)}, u32[]{:S(2)}) %copy-start) | copy-done | bytes 49176
  11.0 3.4 %own_first.1 = (f32[2,8,128]{2,1,0:T(8,128)S(1)}, f32[2,8,128]{2,1,0:T(8,128)S(1)}, f32[2,32,128]{2,1,0:T(8,128)S(1)}, bf16[16,128,256]{2,1,0:T(8,128)(2,1)S(1)}...) custom-call(bf16[4,48,128]{2,1,0:T(8,128)(2,1)S(1)} %copy-done, bf16[96,128,256]{2,1,0:T(8,128)(2,1)} %bitcast.2), custom_call_target="tpu_custom_call" | custom-call | flops 134217728 | bytes 8388608 | tf_op jit(solution)/shard_map/own_first/pallas_call | solution.py:465
  14.4 5.7 %all-to-all-done.asked_ref = bf16[16,72,128]{2,1,0:T(8,128)(2,1)S(1)} async-done(((bf16[16,72,128]{2,1,0:T(8,128)(2,1)}), bf16[16,72,128]{2,1,0:T(8,128)(2,1)S(1)}, u32[]{:S(2)}, u32[]{:S(2)}) %all-to-all-start) | async-done | bytes 294944 | tf_op jit(solution)/shard_map/all_to_all | solution.py:454
  20.2 1.4 %answer.1.after_ref = bf16[16,72,128]{2,1,0:T(8,128)(2,1)} custom-call(s32[8,128]{1,0:T(8,128)S(1)} %get-tuple-element.19.place_ref, bf16[16,72,128]{2,1,0:T(8,128)(2,1)S(1)} %all-to-all-done.asked_ref, bf16[16,128,256]{2,1,0:T(8,128)(2,1)S(1)} %get-tuple-element.21.sent_ref), custom_call_target="tpu_custom_call" | custom-call | tf_op jit(solution)/shard_map/answer/pallas_call | solution.py:486
  21.6 3.5 %all-to-all-start.1 = ((bf16[16,72,128]{2,1,0:T(8,128)(2,1)}), bf16[16,72,128]{2,1,0:T(8,128)(2,1)S(1)}, u32[]{:S(2)}, u32[]{:S(2)}) async-start(bf16[16,72,128]{2,1,0:T(8,128)(2,1)} %answer.1.after_ref), calls=%async_computation.1 | async-start | bytes 589824 | tf_op jit(solution)/shard_map/all_to_all | solution.py:498
  25.1 0.0 copy-done.1
  25.1 3.7 %own_second.1 = (f32[2,8,128]{2,1,0:T(8,128)S(1)}, f32[2,8,128]{2,1,0:T(8,128)S(1)}, f32[2,32,128]{2,1,0:T(8,128)S(1)}, bf16[1024,1280]{1,0:T(8,128)(2,1)S(1)}) custom-call(bf16[4,48,128]{2,1,0:T(8,128)(2,1)S(1)} %copy-done.1, bf16[96,128,256]{2,1,0:T(8,128)(2,1)} %bitcast.3, bf16[1024,8192]{1,0:T(8,128)(2,1)} %weight_ref.3, ...), custom_call_target="tpu_custom_call" | custom-call | flops 134217728 | bytes 8388608 | tf_op jit(solution)/shard_map/own_second/pallas_call | solution.py:501
  28.8 6.2 %all-to-all-done.1.back_ref = bf16[16,72,128]{2,1,0:T(8,128)(2,1)S(1)} async-done(((bf16[16,72,128]{2,1,0:T(8,128)(2,1)}), bf16[16,72,128]{2,1,0:T(8,128)(2,1)S(1)}, u32[]{:S(2)}, u32[]{:S(2)}) %all-to-all-start.1) | async-done | bytes 294944 | tf_op jit(solution)/shard_map/all_to_all | solution.py:498
  35.0 6.1 %project.1 = bf16[8,16,1024]{2,1,0:T(8,128)(2,1)S(1)} custom-call(s32[8,128]{1,0:T(8,128)S(1)} %get-tuple-element.18.slot_ref, bf16[16,72,128]{2,1,0:T(8,128)(2,1)S(1)} %all-to-all-done.1.back_ref, f32[2,8,128]{2,1,0:T(8,128)S(1)} %get-tuple-element.22.peak_a, f32[2,8,128]{2,1,0:T(8,128)S(1)} %get-tuple-element.23.sum_a, ...), custom_call_target="tpu_custom_call" | custom-call | tf_op jit(solution)/shard_map/project/pallas_call | solution.py:517
  41.1 11.1 %all_to_all.15 = bf16[8,16,1024]{2,1,0:T(8,128)(2,1)S(1)} all-to-all(bf16[8,16,1024]{2,1,0:T(8,128)(2,1)S(1)} %project.1), channel_id=1, replica_groups=mesh['inst'=16,'tp'=8] {'tp'}, dimensions={0} | all-to-all | bytes 524288 | tf_op jit(solution)/shard_map/all_to_all | solution.py:530
  52.3 0.6 %reshape.11 = bf16[4,4,1024]{2,1,0:T(4,128)(2,1)} reshape(bf16[16,1024]{1,0:T(8,128)(2,1)S(1)} %reduce_sum.12) | data formatting | bytes 65536 | tf_op jit(solution)/shard_map/reshape | solution.py:532
  (1 shorter events, 0.0 us)
Async XLA Ops:
  2.0 23.2 %copy-start.1 = (bf16[4,48,128]{2,1,0:T(8,128)(2,1)S(1)}, bf16[4,48,128]{2,1,0:T(8,128)(2,1)}, u32[]{:S(2)}) copy-start(bf16[4,48,128]{2,1,0:T(8,128)(2,1)} %get-tuple-element.17.q_ref) | copy-start | bytes 147460
  2.0 18.2 %all-to-all-start = ((bf16[16,72,128]{2,1,0:T(8,128)(2,1)}), bf16[16,72,128]{2,1,0:T(8,128)(2,1)S(1)}, u32[]{:S(2)}, u32[]{:S(2)}) async-start(bf16[16,72,128]{2,1,0:T(8,128)(2,1)} %get-tuple-element.20), calls=%async_computation | async-start | bytes 589824 | tf_op jit(solution)/shard_map/all_to_all | solution.py:454
  10.2 0.8 %copy-start = (bf16[4,48,128]{2,1,0:T(8,128)(2,1)S(1)}, bf16[4,48,128]{2,1,0:T(8,128)(2,1)}, u32[]{:S(2)}) copy-start(bf16[4,48,128]{2,1,0:T(8,128)(2,1)} %get-tuple-element.17.q_ref) | copy-start | bytes 147460
  21.6 13.4 %all-to-all-start.1 = ((bf16[16,72,128]{2,1,0:T(8,128)(2,1)}), bf16[16,72,128]{2,1,0:T(8,128)(2,1)S(1)}, u32[]{:S(2)}, u32[]{:S(2)}) async-start(bf16[16,72,128]{2,1,0:T(8,128)(2,1)} %answer.1.after_ref), calls=%async_computation.1 | async-start | bytes 589824 | tf_op jit(solution)/shard_map/all_to_all | solution.py:498

commit v6 on v5

--- a/solution.py
+++ b/solution.py
@@ -11,13 +11,13 @@
 INFO = 8
 MASKED = -1e30
 TILE = 256
+AHEAD = 4
 FRESH = 8
 PLAN_ROW = 4
 LENGTH_BASE = 64
 
 VMEM = pl.BlockSpec(memory_space=pltpu.VMEM)
 HBM = pl.BlockSpec(memory_space=pltpu.HBM)
-ANY = pl.BlockSpec(memory_space=pl.ANY)
 
 nt_dims = (((1,), (1,)), ((), ()))
 
@@ -172,11 +172,11 @@
         copy.wait()
 
 
-def first_kernel(
+def bring_kernel(
     scale, head_group, blocks, steps, n_inst,
-    q_ref, pool_ref,
-    peak_ref, sum_ref, acc_ref, sent_ref, place_ref, slot_ref,
-    kv_ref, sems, sent_sems,
+    q_ref, pool_ref, weight_ref,
+    peak_ref, sum_ref, acc_ref, sent_ref, held_ref, place_ref, slot_ref,
+    kv_ref, sems, sent_sems, held_sem,
 ):
     pool_size = pool_ref.shape[0]
     slots, rows, head = q_ref.shape[0], q_ref.shape[1] - 2 * FRESH, q_ref.shape[2]
@@ -191,6 +191,11 @@
                 pltpu.make_async_copy(pool_ref.at[block_id], sent_ref.at[e], sent_sems.at[e])
             )
             copies[e].start()
+        held_copy = pltpu.make_async_copy(
+            weight_ref.at[:, pl.ds(0, held_ref.shape[1])], held_ref, held_sem
+        )
+        held_copy.start()
+        copies.append(held_copy)
         lane = lax.broadcasted_iota(jnp.int32, place_ref.shape, 1)
         places = jnp.zeros(place_ref.shape, jnp.int32)
         for e in range(entries):
@@ -210,27 +215,6 @@
 
     own_kernel(
         scale, head_group, blocks, 0, steps, plan, q_ref, pool_ref,
-        peak_ref, sum_ref, acc_ref, kv_ref, sems, bring,
-    )
-
-
-def second_kernel(
-    scale, head_group, blocks, steps, entries, first,
-    q_ref, pool_ref, weight_ref, after_ref,
-    peak_ref, sum_ref, acc_ref, held_ref,
-    kv_ref, sems, weight_sem,
-):
-    del after_ref
-
-    def bring():
-        copy = pltpu.make_async_copy(
-            weight_ref.at[:, pl.ds(0, held_ref.shape[1])], held_ref, weight_sem
-        )
-        copy.start()
-        return [copy]
-
-    own_kernel(
-        scale, head_group, blocks, first, steps, Plan(q_ref, blocks, entries), q_ref, pool_ref,
         peak_ref, sum_ref, acc_ref, kv_ref, sems, bring,
     )
 
@@ -312,26 +296,27 @@
 
 
 def project_kernel(
-    slot_ref, back_ref, peak_a, sum_a, acc_a, peak_b, sum_b, acc_b,
+    slot_ref, back_ref, peak_ref, sum_ref, acc_ref,
     held_ref, weight_ref, out_ref, att_ref, w_ref, sems,
 ):
-    half, rows, head = acc_a.shape
-    slots = half + acc_b.shape[0]
+    slots, rows, head = acc_ref.shape
     n_inst = back_ref.shape[0]
     parts, out_rows, part_cols = out_ref.shape
     held = held_ref.shape[1]
     steps = out_rows // slots
     group = rows // steps
+    columns = parts * part_cols
+    edges = list(range(held, columns - part_cols + 1, part_cols)) + [columns]
+    while edges[-1] - edges[-2] > TILE:
+        edges.insert(-1, columns - (columns - edges[-2]) // (2 * TILE) * TILE)
     copies = {}
-    for c in range(parts):
-        low, high = max(held, c * part_cols), (c + 1) * part_cols
-        if low < high:
-            copies[c] = pltpu.make_async_copy(
-                weight_ref.at[:, pl.ds(low, high - low)],
-                w_ref.at[:, pl.ds(low - held, high - low)],
-                sems.at[c],
-            )
-            copies[c].start()
+    for k, (low, high) in enumerate(zip(edges, edges[1:])):
+        copies[low] = pltpu.make_async_copy(
+            weight_ref.at[:, pl.ds(low, high - low)],
+            w_ref.at[:, pl.ds(low - held, high - low)],
+            sems.at[k],
+        )
+        copies[low].start()
     across = head // rows
     slot_of = slot_ref[...]
     lines = slot_of.shape[0]
@@ -352,13 +337,10 @@
         return total
 
     peaks, sums = together(peak_rows), together(sum_rows)
-    peak_own = [peak_a[k] for k in range(half)] + [peak_b[k] for k in range(slots - half)]
-    sum_own = [sum_a[k] for k in range(half)] + [sum_b[k] for k in range(slots - half)]
-    acc_own = [acc_a[k] for k in range(half)] + [acc_b[k] for k in range(slots - half)]
     best, best_of = [], jnp.zeros((lines, head), jnp.float32)
     for k in range(slots):
         top = jnp.max(jnp.where(slot_of == k, peaks, MASKED), axis=0, keepdims=True)
-        best.append(jnp.maximum(over_groups(jnp.maximum, top, rows), peak_own[k]))
+        best.append(jnp.maximum(over_groups(jnp.maximum, top, rows), peak_ref[k]))
         best_of = jnp.where(slot_of == k, best[k], best_of)
     gains = jnp.where(slot_of >= 0, sums * jnp.exp(peaks - best_of), 0.0)
     keeps, matrix = [], []
@@ -368,9 +350,9 @@
     first_group = lax.broadcasted_iota(jnp.int32, (rows, head), 1) < rows
     for k in range(slots):
         mine = jnp.where(slot_of == k, gains, 0.0)
-        keep = jnp.exp(peak_own[k] - best[k])
+        keep = jnp.exp(peak_ref[k] - best[k])
         total = over_groups(jnp.add, jnp.sum(mine, axis=0, keepdims=True), rows)
-        inverse = 1.0 / (total + sum_own[k] * keep)
+        inverse = 1.0 / (total + sum_ref[k] * keep)
         keep = (keep * inverse)[0:1]
         keeps.append(
             jnp.sum(jnp.where(same & first_group, keep, 0.0), axis=1, keepdims=True)
@@ -384,25 +366,24 @@
     values = back_ref[:, : CAP * rows, :].reshape(n_inst * CAP * rows, head)
     arrived = split_dot(jnp.concatenate(matrix, axis=0), values)
     for slot in range(slots):
-        done = keeps[slot] * acc_own[slot] + arrived[slot * rows : (slot + 1) * rows]
+        done = keeps[slot] * acc_ref[slot] + arrived[slot * rows : (slot + 1) * rows]
         for step in range(steps):
             for g in range(group):
                 at = step * group + g
                 to = step * slots + slot
                 att_ref[to : to + 1, g * head : (g + 1) * head] = done[at : at + 1]
     attended = att_ref[...].astype(jnp.bfloat16)
-    for c in range(parts):
-        if c in copies:
-            copies[c].wait()
-        for low in range(c * part_cols, (c + 1) * part_cols, TILE):
-            if low < held:
-                weight = held_ref[:, low : low + TILE]
-            else:
-                weight = w_ref[:, low - held : low - held + TILE]
-            at = low - c * part_cols
-            out_ref[c, :, at : at + TILE] = jnp.dot(
-                attended, weight, preferred_element_type=jnp.float32
-            ).astype(jnp.bfloat16)
+    for low in range(0, columns, TILE):
+        if low in copies:
+            copies[low].wait()
+        if low < held:
+            weight = held_ref[:, low : low + TILE]
+        else:
+            weight = w_ref[:, low - held : low - held + TILE]
+        c, at = low // part_cols, low % part_cols
+        out_ref[c, :, at : at + TILE] = jnp.dot(
+            attended, weight, preferred_element_type=jnp.float32
+        ).astype(jnp.bfloat16)
 
 
 def params(mib):
@@ -453,34 +434,34 @@
     )(block_table, cache_len, send_block, send_dest, queries, fresh)
     asked = lax.all_to_all(ask, "inst", 0, 0, tiled=True)
 
-    half = slots // 2
-    own = shape((half, rows, head), f32)
-    stat = shape((half, 8, head), f32)
-    kv_scratch = pltpu.VMEM((half, (blocks + 1) * block_len, width), bf16)
-    own_cost = pl.CostEstimate(
-        flops=2 * slots * rows * blocks * block_len * width,
-        bytes_accessed=4 * slots * blocks * block_len * width,
-        transcendentals=half * rows * blocks * block_len,
-    )
-    peak_a, sum_a, acc_a, sent, place, slot_of = pl.pallas_call(
-        functools.partial(first_kernel, scale, group, blocks, steps, n_inst),
+    ahead = AHEAD * TILE
+    own = shape((slots, rows, head), f32)
+    stat = shape((slots, 8, head), f32)
+    own_peak, own_sum, own_acc, sent, held, place, slot_of = pl.pallas_call(
+        functools.partial(bring_kernel, scale, group, blocks, steps, n_inst),
         out_shape=(
             stat, stat, own,
             shape((entries, block_len, width), bf16),
+            shape((head_width, ahead), bf16),
             shape((8, head), i32),
             shape((arrivals * rows // head, head), i32),
         ),
-        in_specs=[VMEM, HBM],
-        out_specs=(VMEM,) * 6,
+        in_specs=[VMEM, HBM, HBM],
+        out_specs=(VMEM,) * 7,
         scratch_shapes=[
-            kv_scratch,
-            pltpu.SemaphoreType.DMA((half, blocks)),
+            pltpu.VMEM((slots, (blocks + 1) * block_len, width), bf16),
+            pltpu.SemaphoreType.DMA((slots, blocks)),
             pltpu.SemaphoreType.DMA((entries,)),
+            pltpu.SemaphoreType.DMA,
         ],
         compiler_params=params(50),
-        cost_estimate=own_cost,
-        name="own_first",
-    )(slot_query, pool)
+        cost_estimate=pl.CostEstimate(
+            flops=4 * slots * rows * blocks * block_len * width,
+            bytes_accessed=8 * slots * blocks * block_len * width,
+            transcendentals=slots * rows * blocks * block_len,
+        ),
+        name="own",
+    )(slot_query, pool, out_weight)
 
     part_cols = columns // n_tp
     answer = pl.pallas_call(
@@ -497,36 +478,20 @@
     )(place, asked, sent)
     back = lax.all_to_all(answer, "inst", 0, 0, tiled=True)
 
-    ahead = 5 * TILE
-    peak_b, sum_b, acc_b, held = pl.pallas_call(
-        functools.partial(second_kernel, scale, group, blocks, steps, entries, half),
-        out_shape=(stat, stat, own, shape((head_width, ahead), bf16)),
-        in_specs=[VMEM, HBM, HBM, ANY],
-        out_specs=(VMEM, VMEM, VMEM, VMEM),
-        scratch_shapes=[
-            kv_scratch,
-            pltpu.SemaphoreType.DMA((half, blocks)),
-            pltpu.SemaphoreType.DMA,
-        ],
-        compiler_params=params(50),
-        cost_estimate=own_cost,
-        name="own_second",
-    )(slot_query, pool, out_weight, answer)
-
     out_rows = steps * slots
     partial_out = pl.pallas_call(
         project_kernel,
         out_shape=shape((n_tp, out_rows, part_cols), bf16),
-        in_specs=[VMEM] * 9 + [HBM],
+        in_specs=[VMEM] * 6 + [HBM],
         out_specs=VMEM,
         scratch_shapes=[
             pltpu.VMEM((out_rows, head_width), f32),
             pltpu.VMEM((head_width, columns - ahead), bf16),
-            pltpu.SemaphoreType.DMA((n_tp,)),
+            pltpu.SemaphoreType.DMA((2 * n_tp,)),
         ],
         compiler_params=params(44),
         name="project",
-    )(slot_of, back, peak_a, sum_a, acc_a, peak_b, sum_b, acc_b, held, out_weight)
+    )(slot_of, back, own_peak, own_sum, own_acc, held, out_weight)
     shares = lax.all_to_all(partial_out, "tp", 0, 0, tiled=True)
     total = jnp.sum(shares.astype(f32), axis=0).astype(bf16)
     return total.reshape(steps, slots, columns // n_tp)

time: 53.5 us -> 52.2 us (0.976)
  blocking collectives: 11.1 us -> 24.3 us
  waiting for transfers between devices: 11.9 us -> 4.01 us
  starting transfers between devices: 11.8 us -> 8.14 us
  Pallas kernels: 16.5 us -> 13.9 us
    all_to_all x0 -> x1, blocking collectives: none -> 13.2 us  [shards(): back = lax.all_to_all(answer, 'inst', 0, 0, tiled=True)]
    all_to_all x1 -> x0, waiting for transfers between devices: 6.16 us -> none  [shards(): back = lax.all_to_all(answer, 'inst', 0, 0, tiled=True)]
    all_to_all x1 -> x0, starting transfers between devices: 3.54 us -> none  [shards(): back = lax.all_to_all(answer, 'inst', 0, 0, tiled=True)]
    pallas_call x2 -> x1, Pallas kernels: 7.06 us -> 5.09 us  [shards(): pl.pallas_call(functools.partial(bring_kernel, scale, group, blocks, step...]
    all_to_all x1, waiting for transfers between devices: 5.73 us -> 4.01 us  [shards(): asked = lax.all_to_all(ask, 'inst', 0, 0, tiled=True)]
    pallas_call x1, Pallas kernels: 1.43 us -> 0.74 us  [shards(): pl.pallas_call(functools.partial(answer_kernel, scale), out_shape=packet,...]
  transfers between devices with their start and end apart: 2 -> 1, of which waited for: 2 -> 1; matrix products, arithmetic and copies ran while one was open for 0% -> 0% of each run, Pallas kernels for 13% -> 10%
where the time goes in v6:
time: 52.2 us; the launch traced here: 51.9 us
  blocking collectives  24.3 us (47%)
  Pallas kernels  13.9 us (27%)
  starting transfers between devices  8.14 us (16%)
  waiting for transfers between devices  4.01 us (8%)
  local copies, waits for them, and re-layouts  1.43 us (3%)
    all_to_all x1, blocking collectives, shards(): back = lax.all_to_all(answer, 'inst', 0, 0, tiled=True)  13.2 us
    all_to_all x1, blocking collectives, shards(): shares = lax.all_to_all(partial_out, 'tp', 0, 0, tiled=True)  11.1 us
    all_to_all x1, starting transfers between devices, shards(): asked = lax.all_to_all(ask, 'inst', 0, 0, tiled=True)  8.14 us
    pallas_call x1, Pallas kernels, shards(): pl.pallas_call(project_kernel, out_shape=shape((n_tp, out_rows, part_cols...  6.17 us
    pallas_call x1, Pallas kernels, shards(): pl.pallas_call(functools.partial(bring_kernel, scale, group, blocks, step...  5.09 us
    all_to_all x1, waiting for transfers between devices, shards(): asked = lax.all_to_all(ask, 'inst', 0, 0, tiled=True)  4.01 us
    pallas_call x1, Pallas kernels, shards(): pl.pallas_call(functools.partial(ask_kernel, pool_size, block_len), out_s...  1.93 us
  transfers between devices with their start and end apart: 1, of which 1 were waited for; matrix products, arithmetic and copies ran while one was open for 0% of the time, Pallas kernels for 10%

profile of v6, /device:TPU:0, one launch (start us, length us, event | category | flops | bytes accessed | tf_op | source)
XLA Modules:
  0.0 51.9 jit_solution(2019388930478877141)
XLA Ops:
  0.0 1.9 %ask.1 = (bf16[16,72,128]{2,1,0:T(8,128)(2,1)}, bf16[4,48,128]{2,1,0:T(8,128)(2,1)}) custom-call(s32[4,16]{1,0:T(4,128)} %table_hbm.1, s32[4]{0:T(128)} %len_hbm.1, s32[16]{0:T(128)} %block_hbm.1, s32[16]{0:T(128)} %dest_hbm.1, bf16[4,4,1024]{2,1,0:T(4,128)(2,1)} %q_hbm.1, bf16[4,4,256]{2,1,0:T(4,128)(2,1)} %bitcast.3), custom_call_target="tpu_custom_call" | custom-call | tf_op jit(solution)/shard_map/ask/pallas_call | solution.py:412
  1.9 8.1 %all-to-all-start = ((bf16[16,72,128]{2,1,0:T(8,128)(2,1)}), bf16[16,72,128]{2,1,0:T(8,128)(2,1)S(1)}, u32[]{:S(2)}, u32[]{:S(2)}) async-start(bf16[16,72,128]{2,1,0:T(8,128)(2,1)} %get-tuple-element.17), calls=%async_computation | async-start | bytes 589824 | tf_op jit(solution)/shard_map/all_to_all | solution.py:435
  10.1 0.0 copy-start
  10.1 0.8 %copy-done = bf16[4,48,128]{2,1,0:T(8,128)(2,1)S(1)} copy-done((bf16[4,48,128]{2,1,0:T(8,128)(2,1)S(1)}, bf16[4,48,128]{2,1,0:T(8,128)(2,1)}, u32[]{:S(2)}) %copy-start) | copy-done | bytes 49176
  10.9 5.1 %own.1 = (f32[4,8,128]{2,1,0:T(8,128)S(1)}, f32[4,8,128]{2,1,0:T(8,128)S(1)}, f32[4,32,128]{2,1,0:T(8,128)S(1)}, bf16[16,128,256]{2,1,0:T(8,128)(2,1)S(1)}, bf16...) custom-call(bf16[4,48,128]{2,1,0:T(8,128)(2,1)S(1)} %copy-done, ...), custom_call_target="tpu_custom_call" | custom-call | flops 268435456 | bytes 16777216 | tf_op jit(solution)/shard_map/own/pallas_call | solution.py:440
  16.0 4.0 %all-to-all-done.asked_ref = bf16[16,72,128]{2,1,0:T(8,128)(2,1)S(1)} async-done(((bf16[16,72,128]{2,1,0:T(8,128)(2,1)}), bf16[16,72,128]{2,1,0:T(8,128)(2,1)S(1)}, u32[]{:S(2)}, u32[]{:S(2)}) %all-to-all-start) | async-done | bytes 294944 | tf_op jit(solution)/shard_map/all_to_all | solution.py:435
  20.0 0.7 %answer.1 = bf16[16,72,128]{2,1,0:T(8,128)(2,1)S(1)} custom-call(s32[8,128]{1,0:T(8,128)S(1)} %get-tuple-element.16.place_ref, bf16[16,72,128]{2,1,0:T(8,128)(2,1)S(1)} %all-to-all-done.asked_ref, bf16[16,128,256]{2,1,0:T(8,128)(2,1)S(1)} %get-tuple-element.18.sent_ref), custom_call_target="tpu_custom_call" | custom-call | tf_op jit(solution)/shard_map/answer/pallas_call | solution.py:467
  20.7 13.2 %all_to_all.15.back_ref = bf16[16,72,128]{2,1,0:T(8,128)(2,1)S(1)} all-to-all(bf16[16,72,128]{2,1,0:T(8,128)(2,1)S(1)} %answer.1), channel_id=1, replica_groups=mesh['inst'=16,'tp'=8] {'inst'}, dimensions={0} | all-to-all | bytes 589824 | tf_op jit(solution)/shard_map/all_to_all | solution.py:479
  33.9 6.2 %project.1 = bf16[8,16,1024]{2,1,0:T(8,128)(2,1)S(1)} custom-call(s32[8,128]{1,0:T(8,128)S(1)} %get-tuple-element.15.slot_ref, bf16[16,72,128]{2,1,0:T(8,128)(2,1)S(1)} %all_to_all.15.back_ref, f32[4,8,128]{2,1,0:T(8,128)S(1)} %get-tuple-element.19.peak_ref, f32[4,8,128]{2,1,0:T(8,128)S(1)} %get-tuple-element.20.sum_ref, ...), custom_call_target="tpu_custom_call" | custom-call | tf_op jit(solution)/shard_map/project/pallas_call | solution.py:482
  40.1 11.1 %all_to_all.16 = bf16[8,16,1024]{2,1,0:T(8,128)(2,1)S(1)} all-to-all(bf16[8,16,1024]{2,1,0:T(8,128)(2,1)S(1)} %project.1), channel_id=1, replica_groups=mesh['inst'=16,'tp'=8] {'tp'}, dimensions={0} | all-to-all | bytes 524288 | tf_op jit(solution)/shard_map/all_to_all | solution.py:495
  51.3 0.6 %reshape.11 = bf16[4,4,1024]{2,1,0:T(4,128)(2,1)} reshape(bf16[16,1024]{1,0:T(8,128)(2,1)S(1)} %reduce_sum.12) | data formatting | bytes 65536 | tf_op jit(solution)/shard_map/reshape | solution.py:497
  (1 shorter events, 0.0 us)
Async XLA Ops:
  1.9 18.1 %all-to-all-start = ((bf16[16,72,128]{2,1,0:T(8,128)(2,1)}), bf16[16,72,128]{2,1,0:T(8,128)(2,1)S(1)}, u32[]{:S(2)}, u32[]{:S(2)}) async-start(bf16[16,72,128]{2,1,0:T(8,128)(2,1)} %get-tuple-element.17), calls=%async_computation | async-start | bytes 589824 | tf_op jit(solution)/shard_map/all_to_all | solution.py:435
  10.1 0.8 %copy-start = (bf16[4,48,128]{2,1,0:T(8,128)(2,1)S(1)}, bf16[4,48,128]{2,1,0:T(8,128)(2,1)}, u32[]{:S(2)}) copy-start(bf16[4,48,128]{2,1,0:T(8,128)(2,1)} %get-tuple-element.14.q_ref) | copy-start | bytes 147460

commit v7 on v6

--- a/solution.py
+++ b/solution.py
@@ -11,7 +11,7 @@
 INFO = 8
 MASKED = -1e30
 TILE = 256
-AHEAD = 4
+LATE = 1
 FRESH = 8
 PLAN_ROW = 4
 LENGTH_BASE = 64
@@ -120,12 +120,12 @@
 def own_kernel(
     scale, head_group, blocks, first,
     steps, plan, q_ref, pool_ref,
-    peak_ref, sum_ref, acc_ref, kv_ref, sems, bring,
+    stat_ref, acc_ref, kv_ref, sems, bring,
 ):
     pool_size, block_len, _ = pool_ref.shape
     slots, rows, head = q_ref.shape[0], q_ref.shape[1] - 2 * FRESH, q_ref.shape[2]
     span = blocks * block_len
-    mine = range(first, first + peak_ref.shape[0])
+    mine = range(first, first + acc_ref.shape[0])
 
     def own_copy(slot, b):
         block_id = jnp.clip(plan.table[slot][b], 0, pool_size - 1)
@@ -165,9 +165,11 @@
         total = jnp.sum(functools.reduce(jnp.add, weights), axis=1, keepdims=True)
         acc_ref[slot - first] = split_dot(jnp.concatenate(weights, axis=1), kv_ref[slot - first, :, head:])
         same = lane % rows == lax.broadcasted_iota(jnp.int32, (rows, block_len), 0)
-        for ref, column in ((peak_ref, peak), (sum_ref, total)):
-            across = jnp.sum(jnp.where(same, column, 0.0), axis=0, keepdims=True)
-            ref[slot - first] = jnp.broadcast_to(across, ref.shape[1:])
+        for row, column in ((0, peak), (stat_ref.shape[0] // 2, total)):
+            row += slot - first
+            stat_ref[row : row + 1, :] = jnp.sum(
+                jnp.where(same, column, 0.0), axis=0, keepdims=True
+            )
     for copy in brought:
         copy.wait()
 
@@ -175,7 +177,7 @@
 def bring_kernel(
     scale, head_group, blocks, steps, n_inst,
     q_ref, pool_ref, weight_ref,
-    peak_ref, sum_ref, acc_ref, sent_ref, held_ref, place_ref, slot_ref,
+    stat_ref, acc_ref, sent_ref, held_ref, place_ref, slot_ref,
     kv_ref, sems, sent_sems, held_sem,
 ):
     pool_size = pool_ref.shape[0]
@@ -215,7 +217,7 @@
 
     own_kernel(
         scale, head_group, blocks, 0, steps, plan, q_ref, pool_ref,
-        peak_ref, sum_ref, acc_ref, kv_ref, sems, bring,
+        stat_ref, acc_ref, kv_ref, sems, bring,
     )
 
 
@@ -296,27 +298,44 @@
 
 
 def project_kernel(
-    slot_ref, back_ref, peak_ref, sum_ref, acc_ref,
-    held_ref, weight_ref, out_ref, att_ref, w_ref, sems,
+    scale, head_group, blocks, steps, entries,
+    slot_ref, back_ref, q_ref, stat_ref, acc_ref,
+    held_ref, weight_ref, pool_ref, out_ref,
+    late_stat, late_acc, kv_ref, att_ref, w_ref, own_sems, sems,
 ):
-    slots, rows, head = acc_ref.shape
+    early, rows, head = acc_ref.shape
+    slots = early + late_acc.shape[0]
     n_inst = back_ref.shape[0]
     parts, out_rows, part_cols = out_ref.shape
     held = held_ref.shape[1]
-    steps = out_rows // slots
     group = rows // steps
-    columns = parts * part_cols
-    edges = list(range(held, columns - part_cols + 1, part_cols)) + [columns]
-    while edges[-1] - edges[-2] > TILE:
-        edges.insert(-1, columns - (columns - edges[-2]) // (2 * TILE) * TILE)
-    copies = {}
-    for k, (low, high) in enumerate(zip(edges, edges[1:])):
-        copies[low] = pltpu.make_async_copy(
-            weight_ref.at[:, pl.ds(low, high - low)],
-            w_ref.at[:, pl.ds(low - held, high - low)],
-            sems.at[k],
-        )
-        copies[low].start()
+    ahead = held // part_cols
+
+    def copy(c):
+        return pltpu.make_async_copy(
+            weight_ref.at[:, pl.ds(pl.multiple_of(c * part_cols, part_cols), part_cols)],
+            w_ref.at[:, pl.ds(pl.multiple_of((c - ahead) * part_cols, part_cols), part_cols)],
+            sems.at[c],
+        )
+
+    for c in range(ahead, ahead + 2):
+        copy(c).start()
+
+    def bring():
+        for c in range(ahead + 2, parts):
+            copy(c).start()
+        return []
+
+    own_kernel(
+        scale, head_group, blocks, early, steps, Plan(q_ref, blocks, entries), q_ref, pool_ref,
+        late_stat, late_acc, kv_ref, own_sems, bring,
+    )
+    owns = [(stat_ref, acc_ref, k) for k in range(early)]
+    owns += [(late_stat, late_acc, k) for k in range(slots - early)]
+    sums_at = stat_ref.shape[0] // 2
+    peak_own = [stat[k : k + 1, :] for stat, _, k in owns]
+    sum_own = [stat[sums_at + k : sums_at + k + 1, :] for stat, _, k in owns]
+    acc_own = [acc[k] for _, acc, k in owns]
     across = head // rows
     slot_of = slot_ref[...]
     lines = slot_of.shape[0]
@@ -340,7 +359,7 @@
     best, best_of = [], jnp.zeros((lines, head), jnp.float32)
     for k in range(slots):
         top = jnp.max(jnp.where(slot_of == k, peaks, MASKED), axis=0, keepdims=True)
-        best.append(jnp.maximum(over_groups(jnp.maximum, top, rows), peak_ref[k]))
+        best.append(jnp.maximum(over_groups(jnp.maximum, top, rows), peak_own[k]))
         best_of = jnp.where(slot_of == k, best[k], best_of)
     gains = jnp.where(slot_of >= 0, sums * jnp.exp(peaks - best_of), 0.0)
     keeps, matrix = [], []
@@ -350,10 +369,10 @@
     first_group = lax.broadcasted_iota(jnp.int32, (rows, head), 1) < rows
     for k in range(slots):
         mine = jnp.where(slot_of == k, gains, 0.0)
-        keep = jnp.exp(peak_ref[k] - best[k])
+        keep = jnp.exp(peak_own[k] - best[k])
         total = over_groups(jnp.add, jnp.sum(mine, axis=0, keepdims=True), rows)
-        inverse = 1.0 / (total + sum_ref[k] * keep)
-        keep = (keep * inverse)[0:1]
+        inverse = 1.0 / (total + sum_own[k] * keep)
+        keep = keep * inverse
         keeps.append(
             jnp.sum(jnp.where(same & first_group, keep, 0.0), axis=1, keepdims=True)
         )
@@ -366,24 +385,34 @@
     values = back_ref[:, : CAP * rows, :].reshape(n_inst * CAP * rows, head)
     arrived = split_dot(jnp.concatenate(matrix, axis=0), values)
     for slot in range(slots):
-        done = keeps[slot] * acc_ref[slot] + arrived[slot * rows : (slot + 1) * rows]
+        done = keeps[slot] * acc_own[slot] + arrived[slot * rows : (slot + 1) * rows]
         for step in range(steps):
             for g in range(group):
                 at = step * group + g
                 to = step * slots + slot
                 att_ref[to : to + 1, g * head : (g + 1) * head] = done[at : at + 1]
     attended = att_ref[...].astype(jnp.bfloat16)
-    for low in range(0, columns, TILE):
-        if low in copies:
-            copies[low].wait()
-        if low < held:
-            weight = held_ref[:, low : low + TILE]
-        else:
-            weight = w_ref[:, low - held : low - held + TILE]
-        c, at = low // part_cols, low % part_cols
-        out_ref[c, :, at : at + TILE] = jnp.dot(
-            attended, weight, preferred_element_type=jnp.float32
-        ).astype(jnp.bfloat16)
+
+    def multiply(c, source, start):
+        def tile(k, carry):
+            at = pl.multiple_of(k * TILE, TILE)
+            weight = source[:, pl.ds(pl.multiple_of(start + at, TILE), TILE)]
+            out_ref[c, :, pl.ds(at, TILE)] = jnp.dot(
+                attended, weight, preferred_element_type=jnp.float32
+            ).astype(jnp.bfloat16)
+            return carry
+
+        lax.fori_loop(0, part_cols // TILE, tile, 0, unroll=True)
+
+    for c in range(ahead):
+        multiply(c, held_ref, c * part_cols)
+
+    def part(c, carry):
+        copy(c).wait()
+        multiply(c, w_ref, (c - ahead) * part_cols)
+        return carry
+
+    lax.fori_loop(ahead, parts, part, 0)
 
 
 def params(mib):
@@ -434,23 +463,24 @@
     )(block_table, cache_len, send_block, send_dest, queries, fresh)
     asked = lax.all_to_all(ask, "inst", 0, 0, tiled=True)
 
-    ahead = AHEAD * TILE
-    own = shape((slots, rows, head), f32)
-    stat = shape((slots, 8, head), f32)
-    own_peak, own_sum, own_acc, sent, held, place, slot_of = pl.pallas_call(
+    ahead = columns // n_tp
+    early = slots - LATE
+    own = shape((early, rows, head), f32)
+    stat = shape((8, head), f32)
+    own_stat, own_acc, sent, held, place, slot_of = pl.pallas_call(
         functools.partial(bring_kernel, scale, group, blocks, steps, n_inst),
         out_shape=(
-            stat, stat, own,
+            stat, own,
             shape((entries, block_len, width), bf16),
             shape((head_width, ahead), bf16),
             shape((8, head), i32),
             shape((arrivals * rows // head, head), i32),
         ),
         in_specs=[VMEM, HBM, HBM],
-        out_specs=(VMEM,) * 7,
+        out_specs=(VMEM,) * 6,
         scratch_shapes=[
-            pltpu.VMEM((slots, (blocks + 1) * block_len, width), bf16),
-            pltpu.SemaphoreType.DMA((slots, blocks)),
+            pltpu.VMEM((early, (blocks + 1) * block_len, width), bf16),
+            pltpu.SemaphoreType.DMA((early, blocks)),
             pltpu.SemaphoreType.DMA((entries,)),
             pltpu.SemaphoreType.DMA,
         ],
@@ -480,18 +510,22 @@
 
     out_rows = steps * slots
     partial_out = pl.pallas_call(
-        project_kernel,
+        functools.partial(project_kernel, scale, group, blocks, steps, entries),
         out_shape=shape((n_tp, out_rows, part_cols), bf16),
-        in_specs=[VMEM] * 6 + [HBM],
+        in_specs=[VMEM] * 6 + [HBM, HBM],
         out_specs=VMEM,
         scratch_shapes=[
+            pltpu.VMEM(stat.shape, f32),
+            pltpu.VMEM((LATE, rows, head), f32),
+            pltpu.VMEM((LATE, (blocks + 1) * block_len, width), bf16),
             pltpu.VMEM((out_rows, head_width), f32),
             pltpu.VMEM((head_width, columns - ahead), bf16),
-            pltpu.SemaphoreType.DMA((2 * n_tp,)),
+            pltpu.SemaphoreType.DMA((LATE, blocks)),
+            pltpu.SemaphoreType.DMA((n_tp,)),
         ],
-        compiler_params=params(44),
+        compiler_params=params(49),
         name="project",
-    )(slot_of, back, own_peak, own_sum, own_acc, held, out_weight)
+    )(slot_of, back, slot_query, own_stat, own_acc, held, out_weight, pool)
     shares = lax.all_to_all(partial_out, "tp", 0, 0, tiled=True)
     total = jnp.sum(shares.astype(f32), axis=0).astype(bf16)
     return total.reshape(steps, slots, columns // n_tp)

time: 52.2 us -> 55.2 us (1.057)
  Pallas kernels: 13.9 us -> 17.2 us
  blocking collectives: 24.3 us -> 23.7 us
    pallas_call x1, Pallas kernels: 6.17 us -> 9.66 us  [shards(): pl.pallas_call(functools.partial(project_kernel, scale, group, blocks, st...]
    all_to_all x1, blocking collectives: 13.2 us -> 12.6 us  [shards(): back = lax.all_to_all(answer, 'inst', 0, 0, tiled=True)]
  transfers between devices with their start and end apart: 1 -> 1, of which waited for: 1 -> 1; matrix products, arithmetic and copies ran while one was open for 0% -> 0% of each run, Pallas kernels for 10% -> 9%
where the time goes in v7:
time: 55.2 us; the launch traced here: 54.8 us
  blocking collectives  23.7 us (43%)
  Pallas kernels  17.2 us (31%)
  starting transfers between devices  8.14 us (15%)
  waiting for transfers between devices  4.27 us (8%)
  local copies, waits for them, and re-layouts  1.43 us (3%)
    all_to_all x1, blocking collectives, shards(): back = lax.all_to_all(answer, 'inst', 0, 0, tiled=True)  12.6 us
    all_to_all x1, blocking collectives, shards(): shares = lax.all_to_all(partial_out, 'tp', 0, 0, tiled=True)  11.1 us
    pallas_call x1, Pallas kernels, shards(): pl.pallas_call(functools.partial(project_kernel, scale, group, blocks, st...  9.66 us
    all_to_all x1, starting transfers between devices, shards(): asked = lax.all_to_all(ask, 'inst', 0, 0, tiled=True)  8.14 us
    pallas_call x1, Pallas kernels, shards(): pl.pallas_call(functools.partial(bring_kernel, scale, group, blocks, step...  4.82 us
    all_to_all x1, waiting for transfers between devices, shards(): asked = lax.all_to_all(ask, 'inst', 0, 0, tiled=True)  4.27 us
    pallas_call x1, Pallas kernels, shards(): pl.pallas_call(functools.partial(ask_kernel, pool_size, block_len), out_s...  1.94 us
  transfers between devices with their start and end apart: 1, of which 1 were waited for; matrix products, arithmetic and copies ran while one was open for 0% of the time, Pallas kernels for 9%

profile of v7, /device:TPU:0, one launch (start us, length us, event | category | flops | bytes accessed | tf_op | source)
XLA Modules:
  0.0 54.8 jit_solution(17333914848908104438)
XLA Ops:
  0.0 1.9 %ask.1 = (bf16[16,72,128]{2,1,0:T(8,128)(2,1)}, bf16[4,48,128]{2,1,0:T(8,128)(2,1)}) custom-call(s32[4,16]{1,0:T(4,128)} %table_hbm.1, s32[4]{0:T(128)} %len_hbm.1, s32[16]{0:T(128)} %block_hbm.1, s32[16]{0:T(128)} %dest_hbm.1, bf16[4,4,1024]{2,1,0:T(4,128)(2,1)} %q_hbm.1, bf16[4,4,256]{2,1,0:T(4,128)(2,1)} %bitcast.4), custom_call_target="tpu_custom_call" | custom-call | tf_op jit(solution)/shard_map/ask/pallas_call | solution.py:441
  1.9 8.1 %all-to-all-start = ((bf16[16,72,128]{2,1,0:T(8,128)(2,1)}), bf16[16,72,128]{2,1,0:T(8,128)(2,1)S(1)}, u32[]{:S(2)}, u32[]{:S(2)}) async-start(bf16[16,72,128]{2,1,0:T(8,128)(2,1)} %get-tuple-element.16), calls=%async_computation | async-start | bytes 589824 | tf_op jit(solution)/shard_map/all_to_all | solution.py:464
  10.1 0.0 copy-start
  10.1 0.8 %copy-done = bf16[4,48,128]{2,1,0:T(8,128)(2,1)S(1)} copy-done((bf16[4,48,128]{2,1,0:T(8,128)(2,1)S(1)}, bf16[4,48,128]{2,1,0:T(8,128)(2,1)}, u32[]{:S(2)}) %copy-start) | copy-done | bytes 49176
  10.9 0.0 copy-start.1
  10.9 4.8 %own.1 = (f32[8,128]{1,0:T(8,128)S(1)}, f32[3,32,128]{2,1,0:T(8,128)S(1)}, bf16[16,128,256]{2,1,0:T(8,128)(2,1)S(1)}, bf16[1024,1024]{1,0:T(8,128)(2,1)S(1)}, s3...) custom-call(bf16[4,48,128]{2,1,0:T(8,128)(2,1)S(1)} %copy-done, bf16[96,128,256]{2,1,0:T(8,128)(2,1)} %bitcast.2, ...), custom_call_target="tpu_custom_call" | custom-call | flops 268435456 | bytes 16777216 | tf_op jit(solution)/shard_map/own/pallas_call | solution.py:470
  15.7 4.3 %all-to-all-done.asked_ref = bf16[16,72,128]{2,1,0:T(8,128)(2,1)S(1)} async-done(((bf16[16,72,128]{2,1,0:T(8,128)(2,1)}), bf16[16,72,128]{2,1,0:T(8,128)(2,1)S(1)}, u32[]{:S(2)}, u32[]{:S(2)}) %all-to-all-start) | async-done | bytes 294944 | tf_op jit(solution)/shard_map/all_to_all | solution.py:464
  20.0 0.7 %answer.1 = bf16[16,72,128]{2,1,0:T(8,128)(2,1)S(1)} custom-call(s32[8,128]{1,0:T(8,128)S(1)} %get-tuple-element.15.place_ref, bf16[16,72,128]{2,1,0:T(8,128)(2,1)S(1)} %all-to-all-done.asked_ref, bf16[16,128,256]{2,1,0:T(8,128)(2,1)S(1)} %get-tuple-element.17.sent_ref), custom_call_target="tpu_custom_call" | custom-call | tf_op jit(solution)/shard_map/answer/pallas_call | solution.py:497
  20.7 12.6 %all_to_all.15.back_ref = bf16[16,72,128]{2,1,0:T(8,128)(2,1)S(1)} all-to-all(bf16[16,72,128]{2,1,0:T(8,128)(2,1)S(1)} %answer.1), channel_id=1, replica_groups=mesh['inst'=16,'tp'=8] {'inst'}, dimensions={0} | all-to-all | bytes 589824 | tf_op jit(solution)/shard_map/all_to_all | solution.py:509
  33.3 0.0 copy-done.1
  33.3 9.7 %project.1 = bf16[8,16,1024]{2,1,0:T(8,128)(2,1)S(1)} custom-call(s32[8,128]{1,0:T(8,128)S(1)} %get-tuple-element.14.slot_ref, bf16[16,72,128]{2,1,0:T(8,128)(2,1)S(1)} %all_to_all.15.back_ref, bf16[4,48,128]{2,1,0:T(8,128)(2,1)S(1)} %copy-done.1, f32[8,128]{1,0:T(8,128)S(1)} %get-tuple-element.18.stat_ref, f32[3,32,128]{2,1,0:T(8,128)S(1)} %get-tuple-element.19.acc_ref, ...), custom_call_target="tpu_custom_call" | custom-call | tf_op jit(solution)/shard_map/project/pallas_call | solution.py:512
  43.0 11.1 %all_to_all.16 = bf16[8,16,1024]{2,1,0:T(8,128)(2,1)S(1)} all-to-all(bf16[8,16,1024]{2,1,0:T(8,128)(2,1)S(1)} %project.1), channel_id=1, replica_groups=mesh['inst'=16,'tp'=8] {'tp'}, dimensions={0} | all-to-all | bytes 524288 | tf_op jit(solution)/shard_map/all_to_all | solution.py:529
  54.2 0.6 %reshape.11 = bf16[4,4,1024]{2,1,0:T(4,128)(2,1)} reshape(bf16[16,1024]{1,0:T(8,128)(2,1)S(1)} %reduce_sum.12) | data formatting | bytes 65536 | tf_op jit(solution)/shard_map/reshape | solution.py:531
  (1 shorter events, 0.0 us)
Async XLA Ops:
  1.9 18.1 %all-to-all-start = ((bf16[16,72,128]{2,1,0:T(8,128)(2,1)}), bf16[16,72,128]{2,1,0:T(8,128)(2,1)S(1)}, u32[]{:S(2)}, u32[]{:S(2)}) async-start(bf16[16,72,128]{2,1,0:T(8,128)(2,1)} %get-tuple-element.16), calls=%async_computation | async-start | bytes 589824 | tf_op jit(solution)/shard_map/all_to_all | solution.py:464
  10.1 0.8 %copy-start = (bf16[4,48,128]{2,1,0:T(8,128)(2,1)S(1)}, bf16[4,48,128]{2,1,0:T(8,128)(2,1)}, u32[]{:S(2)}) copy-start(bf16[4,48,128]{2,1,0:T(8,128)(2,1)} %get-tuple-element.13.q_ref) | copy-start | bytes 147460
  10.9 22.4 %copy-start.1 = (bf16[4,48,128]{2,1,0:T(8,128)(2,1)S(1)}, bf16[4,48,128]{2,1,0:T(8,128)(2,1)}, u32[]{:S(2)}) copy-start(bf16[4,48,128]{2,1,0:T(8,128)(2,1)} %get-tuple-element.13.q_ref) | copy-start | bytes 147460

commit v8 on v6

--- a/solution.py
+++ b/solution.py
@@ -11,7 +11,6 @@
 INFO = 8
 MASKED = -1e30
 TILE = 256
-AHEAD = 4
 FRESH = 8
 PLAN_ROW = 4
 LENGTH_BASE = 64
@@ -147,12 +146,14 @@
         for k in range(2):
             part = jnp.concatenate([fresh[k * FRESH : (k + 1) * FRESH], rest], axis=0)
             kv_ref[slot - first, span:, k * head : (k + 1) * head] = part.astype(jnp.bfloat16)
-    for slot in mine:
+    def score(slot):
         for b in range(blocks):
             own_copy(slot, b).wait()
-        scores = lax.dot_general(
+        return lax.dot_general(
             q_ref[slot, :rows, :], kv_ref[slot - first, :, :head], nt_dims, preferred_element_type=jnp.float32
         ) * scale
+
+    def attend(slot, scores):
         parts_s = []
         for b in range(blocks):
             live = jnp.clip(plan.length[slot] - b * block_len, 0, block_len)
@@ -168,6 +169,12 @@
         for ref, column in ((peak_ref, peak), (sum_ref, total)):
             across = jnp.sum(jnp.where(same, column, 0.0), axis=0, keepdims=True)
             ref[slot - first] = jnp.broadcast_to(across, ref.shape[1:])
+
+    scores = score(first)
+    for slot in mine:
+        later = score(slot + 1) if slot + 1 in mine else None
+        attend(slot, scores)
+        scores = later
     for copy in brought:
         copy.wait()
 
@@ -305,18 +312,17 @@
     held = held_ref.shape[1]
     steps = out_rows // slots
     group = rows // steps
-    columns = parts * part_cols
-    edges = list(range(held, columns - part_cols + 1, part_cols)) + [columns]
-    while edges[-1] - edges[-2] > TILE:
-        edges.insert(-1, columns - (columns - edges[-2]) // (2 * TILE) * TILE)
-    copies = {}
-    for k, (low, high) in enumerate(zip(edges, edges[1:])):
-        copies[low] = pltpu.make_async_copy(
-            weight_ref.at[:, pl.ds(low, high - low)],
-            w_ref.at[:, pl.ds(low - held, high - low)],
-            sems.at[k],
-        )
-        copies[low].start()
+    ahead = held // part_cols
+
+    def copy(c):
+        return pltpu.make_async_copy(
+            weight_ref.at[:, pl.ds(pl.multiple_of(c * part_cols, part_cols), part_cols)],
+            w_ref.at[:, pl.ds(pl.multiple_of((c - ahead) * part_cols, part_cols), part_cols)],
+            sems.at[c],
+        )
+
+    for c in range(ahead, parts):
+        copy(c).start()
     across = head // rows
     slot_of = slot_ref[...]
     lines = slot_of.shape[0]
@@ -373,17 +379,27 @@
                 to = step * slots + slot
                 att_ref[to : to + 1, g * head : (g + 1) * head] = done[at : at + 1]
     attended = att_ref[...].astype(jnp.bfloat16)
-    for low in range(0, columns, TILE):
-        if low in copies:
-            copies[low].wait()
-        if low < held:
-            weight = held_ref[:, low : low + TILE]
-        else:
-            weight = w_ref[:, low - held : low - held + TILE]
-        c, at = low // part_cols, low % part_cols
-        out_ref[c, :, at : at + TILE] = jnp.dot(
-            attended, weight, preferred_element_type=jnp.float32
-        ).astype(jnp.bfloat16)
+
+    def multiply(c, source, start):
+        def tile(k, carry):
+            at = pl.multiple_of(k * TILE, TILE)
+            weight = source[:, pl.ds(pl.multiple_of(start + at, TILE), TILE)]
+            out_ref[c, :, pl.ds(at, TILE)] = jnp.dot(
+                attended, weight, preferred_element_type=jnp.float32
+            ).astype(jnp.bfloat16)
+            return carry
+
+        lax.fori_loop(0, part_cols // TILE, tile, 0, unroll=True)
+
+    for c in range(ahead):
+        multiply(c, held_ref, c * part_cols)
+
+    def part(c, carry):
+        copy(c).wait()
+        multiply(c, w_ref, (c - ahead) * part_cols)
+        return carry
+
+    lax.fori_loop(ahead, parts, part, 0)
 
 
 def params(mib):
@@ -434,7 +450,7 @@
     )(block_table, cache_len, send_block, send_dest, queries, fresh)
     asked = lax.all_to_all(ask, "inst", 0, 0, tiled=True)
 
-    ahead = AHEAD * TILE
+    ahead = columns // n_tp
     own = shape((slots, rows, head), f32)
     stat = shape((slots, 8, head), f32)
     own_peak, own_sum, own_acc, sent, held, place, slot_of = pl.pallas_call(
@@ -487,7 +503,7 @@
         scratch_shapes=[
             pltpu.VMEM((out_rows, head_width), f32),
             pltpu.VMEM((head_width, columns - ahead), bf16),
-            pltpu.SemaphoreType.DMA((2 * n_tp,)),
+            pltpu.SemaphoreType.DMA((n_tp,)),
         ],
         compiler_params=params(44),
         name="project",

time: 52.2 us -> 51.6 us (0.989)
  blocking collectives: 24.3 us -> 23.7 us
    all_to_all x1, blocking collectives: 13.2 us -> 12.6 us  [shards(): back = lax.all_to_all(answer, 'inst', 0, 0, tiled=True)]
  transfers between devices with their start and end apart: 1 -> 1, of which waited for: 1 -> 1; matrix products, arithmetic and copies ran while one was open for 0% -> 0% of each run, Pallas kernels for 10% -> 9%
where the time goes in v8:
time: 51.6 us; the launch traced here: 51.1 us
  blocking collectives  23.7 us (46%)
  Pallas kernels  13.4 us (26%)
  starting transfers between devices  8.14 us (16%)
  waiting for transfers between devices  4.31 us (8%)
  local copies, waits for them, and re-layouts  1.43 us (3%)
    all_to_all x1, blocking collectives, shards(): back = lax.all_to_all(answer, 'inst', 0, 0, tiled=True)  12.6 us
    all_to_all x1, blocking collectives, shards(): shares = lax.all_to_all(partial_out, 'tp', 0, 0, tiled=True)  11.1 us
    all_to_all x1, starting transfers between devices, shards(): asked = lax.all_to_all(ask, 'inst', 0, 0, tiled=True)  8.14 us
    pallas_call x1, Pallas kernels, shards(): pl.pallas_call(project_kernel, out_shape=shape((n_tp, out_rows, part_cols...  5.93 us
    pallas_call x1, Pallas kernels, shards(): pl.pallas_call(functools.partial(bring_kernel, scale, group, blocks, step...  4.79 us
    all_to_all x1, waiting for transfers between devices, shards(): asked = lax.all_to_all(ask, 'inst', 0, 0, tiled=True)  4.31 us
    pallas_call x1, Pallas kernels, shards(): pl.pallas_call(functools.partial(ask_kernel, pool_size, block_len), out_s...  1.93 us
  transfers between devices with their start and end apart: 1, of which 1 were waited for; matrix products, arithmetic and copies ran while one was open for 0% of the time, Pallas kernels for 9%

profile of v8, /device:TPU:0, one launch (start us, length us, event | category | flops | bytes accessed | tf_op | source)
XLA Modules:
  0.0 51.1 jit_solution(7488145981423404417)
XLA Ops:
  0.0 1.9 %ask.1 = (bf16[16,72,128]{2,1,0:T(8,128)(2,1)}, bf16[4,48,128]{2,1,0:T(8,128)(2,1)}) custom-call(s32[4,16]{1,0:T(4,128)} %table_hbm.1, s32[4]{0:T(128)} %len_hbm.1, s32[16]{0:T(128)} %block_hbm.1, s32[16]{0:T(128)} %dest_hbm.1, bf16[4,4,1024]{2,1,0:T(4,128)(2,1)} %q_hbm.1, bf16[4,4,256]{2,1,0:T(4,128)(2,1)} %bitcast.3), custom_call_target="tpu_custom_call" | custom-call | tf_op jit(solution)/shard_map/ask/pallas_call | solution.py:428
  1.9 8.1 %all-to-all-start = ((bf16[16,72,128]{2,1,0:T(8,128)(2,1)}), bf16[16,72,128]{2,1,0:T(8,128)(2,1)S(1)}, u32[]{:S(2)}, u32[]{:S(2)}) async-start(bf16[16,72,128]{2,1,0:T(8,128)(2,1)} %get-tuple-element.17), calls=%async_computation | async-start | bytes 589824 | tf_op jit(solution)/shard_map/all_to_all | solution.py:451
  10.1 0.0 copy-start
  10.1 0.8 %copy-done = bf16[4,48,128]{2,1,0:T(8,128)(2,1)S(1)} copy-done((bf16[4,48,128]{2,1,0:T(8,128)(2,1)S(1)}, bf16[4,48,128]{2,1,0:T(8,128)(2,1)}, u32[]{:S(2)}) %copy-start) | copy-done | bytes 49176
  10.9 4.8 %own.1 = (f32[4,8,128]{2,1,0:T(8,128)S(1)}, f32[4,8,128]{2,1,0:T(8,128)S(1)}, f32[4,32,128]{2,1,0:T(8,128)S(1)}, bf16[16,128,256]{2,1,0:T(8,128)(2,1)S(1)}, bf16...) custom-call(bf16[4,48,128]{2,1,0:T(8,128)(2,1)S(1)} %copy-done, ...), custom_call_target="tpu_custom_call" | custom-call | flops 268435456 | bytes 16777216 | tf_op jit(solution)/shard_map/own/pallas_call | solution.py:456
  15.7 4.3 %all-to-all-done.asked_ref = bf16[16,72,128]{2,1,0:T(8,128)(2,1)S(1)} async-done(((bf16[16,72,128]{2,1,0:T(8,128)(2,1)}), bf16[16,72,128]{2,1,0:T(8,128)(2,1)S(1)}, u32[]{:S(2)}, u32[]{:S(2)}) %all-to-all-start) | async-done | bytes 294944 | tf_op jit(solution)/shard_map/all_to_all | solution.py:451
  20.0 0.7 %answer.1 = bf16[16,72,128]{2,1,0:T(8,128)(2,1)S(1)} custom-call(s32[8,128]{1,0:T(8,128)S(1)} %get-tuple-element.16.place_ref, bf16[16,72,128]{2,1,0:T(8,128)(2,1)S(1)} %all-to-all-done.asked_ref, bf16[16,128,256]{2,1,0:T(8,128)(2,1)S(1)} %get-tuple-element.18.sent_ref), custom_call_target="tpu_custom_call" | custom-call | tf_op jit(solution)/shard_map/answer/pallas_call | solution.py:483
  20.7 12.6 %all_to_all.15.back_ref = bf16[16,72,128]{2,1,0:T(8,128)(2,1)S(1)} all-to-all(bf16[16,72,128]{2,1,0:T(8,128)(2,1)S(1)} %answer.1), channel_id=1, replica_groups=mesh['inst'=16,'tp'=8] {'inst'}, dimensions={0} | all-to-all | bytes 589824 | tf_op jit(solution)/shard_map/all_to_all | solution.py:495
  33.3 5.9 %project.1 = bf16[8,16,1024]{2,1,0:T(8,128)(2,1)S(1)} custom-call(s32[8,128]{1,0:T(8,128)S(1)} %get-tuple-element.15.slot_ref, bf16[16,72,128]{2,1,0:T(8,128)(2,1)S(1)} %all_to_all.15.back_ref, f32[4,8,128]{2,1,0:T(8,128)S(1)} %get-tuple-element.19.peak_ref, f32[4,8,128]{2,1,0:T(8,128)S(1)} %get-tuple-element.20.sum_ref, ...), custom_call_target="tpu_custom_call" | custom-call | tf_op jit(solution)/shard_map/project/pallas_call | solution.py:498
  39.2 11.1 %all_to_all.16 = bf16[8,16,1024]{2,1,0:T(8,128)(2,1)S(1)} all-to-all(bf16[8,16,1024]{2,1,0:T(8,128)(2,1)S(1)} %project.1), channel_id=1, replica_groups=mesh['inst'=16,'tp'=8] {'tp'}, dimensions={0} | all-to-all | bytes 524288 | tf_op jit(solution)/shard_map/all_to_all | solution.py:511
  50.4 0.6 %reshape.11 = bf16[4,4,1024]{2,1,0:T(4,128)(2,1)} reshape(bf16[16,1024]{1,0:T(8,128)(2,1)S(1)} %reduce_sum.12) | data formatting | bytes 65536 | tf_op jit(solution)/shard_map/reshape | solution.py:513
  (1 shorter events, 0.0 us)
Async XLA Ops:
  1.9 18.1 %all-to-all-start = ((bf16[16,72,128]{2,1,0:T(8,128)(2,1)}), bf16[16,72,128]{2,1,0:T(8,128)(2,1)S(1)}, u32[]{:S(2)}, u32[]{:S(2)}) async-start(bf16[16,72,128]{2,1,0:T(8,128)(2,1)} %get-tuple-element.17), calls=%async_computation | async-start | bytes 589824 | tf_op jit(solution)/shard_map/all_to_all | solution.py:451
  10.1 0.8 %copy-start = (bf16[4,48,128]{2,1,0:T(8,128)(2,1)S(1)}, bf16[4,48,128]{2,1,0:T(8,128)(2,1)}, u32[]{:S(2)}) copy-start(bf16[4,48,128]{2,1,0:T(8,128)(2,1)} %get-tuple-element.14.q_ref) | copy-start | bytes 147460

commit v9 on v8

--- a/solution.py
+++ b/solution.py
@@ -134,9 +134,15 @@
             sems.at[slot - first, b],
         )
 
+    def live_tokens(slot, b):
+        live = jnp.clip(plan.length[slot] - b * block_len, 0, block_len)
+        return jnp.where(plan.table[slot][b] < pool_size, live, 0)
+
+    lives = {(slot, b): live_tokens(slot, b) for slot in mine for b in range(blocks)}
+    kv_ref[:, :, head:] = jnp.zeros((kv_ref.shape[0], kv_ref.shape[1], head), kv_ref.dtype)
     for slot in mine:
         for b in range(blocks):
-            own_copy(slot, b).start()
+            pl.when(lives[slot, b] > 0)(own_copy(slot, b).start)
     brought = bring()
     lane = lax.broadcasted_iota(jnp.int32, (rows, block_len), 1)
     step = lax.broadcasted_iota(jnp.int32, (rows, block_len), 0) // head_group
@@ -148,7 +154,7 @@
             kv_ref[slot - first, span:, k * head : (k + 1) * head] = part.astype(jnp.bfloat16)
     def score(slot):
         for b in range(blocks):
-            own_copy(slot, b).wait()
+            pl.when(lives[slot, b] > 0)(own_copy(slot, b).wait)
         return lax.dot_general(
             q_ref[slot, :rows, :], kv_ref[slot - first, :, :head], nt_dims, preferred_element_type=jnp.float32
         ) * scale
@@ -156,10 +162,8 @@
     def attend(slot, scores):
         parts_s = []
         for b in range(blocks):
-            live = jnp.clip(plan.length[slot] - b * block_len, 0, block_len)
-            live = jnp.where(plan.table[slot][b] < pool_size, live, 0)
             part = scores[:, b * block_len : (b + 1) * block_len]
-            parts_s.append(jnp.where(lane < live, part, MASKED))
+            parts_s.append(jnp.where(lane < lives[slot, b], part, MASKED))
         parts_s.append(jnp.where((lane <= step) & (lane < steps), scores[:, span:], MASKED))
         peak = jnp.max(functools.reduce(jnp.maximum, parts_s), axis=1, keepdims=True)
         weights = [jnp.exp(part - peak) for part in parts_s]

time: 51.6 us -> 51.4 us (level)
  Pallas kernels: 13.4 us -> 12.7 us
  waiting for transfers between devices: 4.31 us -> 5 us
    pallas_call x1, Pallas kernels: 4.79 us -> 4.09 us  [shards(): pl.pallas_call(functools.partial(bring_kernel, scale, group, blocks, step...]
    all_to_all x1, waiting for transfers between devices: 4.31 us -> 5 us  [shards(): asked = lax.all_to_all(ask, 'inst', 0, 0, tiled=True)]
  transfers between devices with their start and end apart: 1 -> 1, of which waited for: 1 -> 1; matrix products, arithmetic and copies ran while one was open for 0% -> 0% of each run, Pallas kernels for 9% -> 8%
where the time goes in v9:
time: 51.4 us; the launch traced here: 51 us
  blocking collectives  23.6 us (46%)
  Pallas kernels  12.7 us (25%)
  starting transfers between devices  8.14 us (16%)
  waiting for transfers between devices  5 us (10%)
  local copies, waits for them, and re-layouts  1.43 us (3%)
    all_to_all x1, blocking collectives, shards(): back = lax.all_to_all(answer, 'inst', 0, 0, tiled=True)  12.5 us
    all_to_all x1, blocking collectives, shards(): shares = lax.all_to_all(partial_out, 'tp', 0, 0, tiled=True)  11.1 us
    all_to_all x1, starting transfers between devices, shards(): asked = lax.all_to_all(ask, 'inst', 0, 0, tiled=True)  8.14 us
    pallas_call x1, Pallas kernels, shards(): pl.pallas_call(project_kernel, out_shape=shape((n_tp, out_rows, part_cols...  5.93 us
    all_to_all x1, waiting for transfers between devices, shards(): asked = lax.all_to_all(ask, 'inst', 0, 0, tiled=True)  5 us
    pallas_call x1, Pallas kernels, shards(): pl.pallas_call(functools.partial(bring_kernel, scale, group, blocks, step...  4.09 us
    pallas_call x1, Pallas kernels, shards(): pl.pallas_call(functools.partial(ask_kernel, pool_size, block_len), out_s...  1.93 us
  transfers between devices with their start and end apart: 1, of which 1 were waited for; matrix products, arithmetic and copies ran while one was open for 0% of the time, Pallas kernels for 8%

profile of v9, /device:TPU:0, one launch (start us, length us, event | category | flops | bytes accessed | tf_op | source)
XLA Modules:
  0.0 51.0 jit_solution(9119989224242093434)
XLA Ops:
  0.0 1.9 %ask.1 = (bf16[16,72,128]{2,1,0:T(8,128)(2,1)}, bf16[4,48,128]{2,1,0:T(8,128)(2,1)}) custom-call(s32[4,16]{1,0:T(4,128)} %table_hbm.1, s32[4]{0:T(128)} %len_hbm.1, s32[16]{0:T(128)} %block_hbm.1, s32[16]{0:T(128)} %dest_hbm.1, bf16[4,4,1024]{2,1,0:T(4,128)(2,1)} %q_hbm.1, bf16[4,4,256]{2,1,0:T(4,128)(2,1)} %bitcast.3), custom_call_target="tpu_custom_call" | custom-call | tf_op jit(solution)/shard_map/ask/pallas_call | solution.py:432
  1.9 8.1 %all-to-all-start = ((bf16[16,72,128]{2,1,0:T(8,128)(2,1)}), bf16[16,72,128]{2,1,0:T(8,128)(2,1)S(1)}, u32[]{:S(2)}, u32[]{:S(2)}) async-start(bf16[16,72,128]{2,1,0:T(8,128)(2,1)} %get-tuple-element.17), calls=%async_computation | async-start | bytes 589824 | tf_op jit(solution)/shard_map/all_to_all | solution.py:455
  10.1 0.0 copy-start
  10.1 0.8 %copy-done = bf16[4,48,128]{2,1,0:T(8,128)(2,1)S(1)} copy-done((bf16[4,48,128]{2,1,0:T(8,128)(2,1)S(1)}, bf16[4,48,128]{2,1,0:T(8,128)(2,1)}, u32[]{:S(2)}) %copy-start) | copy-done | bytes 49176
  10.9 4.1 %own.1 = (f32[4,8,128]{2,1,0:T(8,128)S(1)}, f32[4,8,128]{2,1,0:T(8,128)S(1)}, f32[4,32,128]{2,1,0:T(8,128)S(1)}, bf16[16,128,256]{2,1,0:T(8,128)(2,1)S(1)}, bf16...) custom-call(bf16[4,48,128]{2,1,0:T(8,128)(2,1)S(1)} %copy-done, ...), custom_call_target="tpu_custom_call" | custom-call | flops 268435456 | bytes 16777216 | tf_op jit(solution)/shard_map/own/pallas_call | solution.py:460
  15.0 5.0 %all-to-all-done.asked_ref = bf16[16,72,128]{2,1,0:T(8,128)(2,1)S(1)} async-done(((bf16[16,72,128]{2,1,0:T(8,128)(2,1)}), bf16[16,72,128]{2,1,0:T(8,128)(2,1)S(1)}, u32[]{:S(2)}, u32[]{:S(2)}) %all-to-all-start) | async-done | bytes 294944 | tf_op jit(solution)/shard_map/all_to_all | solution.py:455
  20.0 0.7 %answer.1 = bf16[16,72,128]{2,1,0:T(8,128)(2,1)S(1)} custom-call(s32[8,128]{1,0:T(8,128)S(1)} %get-tuple-element.16.place_ref, bf16[16,72,128]{2,1,0:T(8,128)(2,1)S(1)} %all-to-all-done.asked_ref, bf16[16,128,256]{2,1,0:T(8,128)(2,1)S(1)} %get-tuple-element.18.sent_ref), custom_call_target="tpu_custom_call" | custom-call | tf_op jit(solution)/shard_map/answer/pallas_call | solution.py:487
  20.7 12.5 %all_to_all.15.back_ref = bf16[16,72,128]{2,1,0:T(8,128)(2,1)S(1)} all-to-all(bf16[16,72,128]{2,1,0:T(8,128)(2,1)S(1)} %answer.1), channel_id=1, replica_groups=mesh['inst'=16,'tp'=8] {'inst'}, dimensions={0} | all-to-all | bytes 589824 | tf_op jit(solution)/shard_map/all_to_all | solution.py:499
  33.2 5.9 %project.1 = bf16[8,16,1024]{2,1,0:T(8,128)(2,1)S(1)} custom-call(s32[8,128]{1,0:T(8,128)S(1)} %get-tuple-element.15.slot_ref, bf16[16,72,128]{2,1,0:T(8,128)(2,1)S(1)} %all_to_all.15.back_ref, f32[4,8,128]{2,1,0:T(8,128)S(1)} %get-tuple-element.19.peak_ref, f32[4,8,128]{2,1,0:T(8,128)S(1)} %get-tuple-element.20.sum_ref, ...), custom_call_target="tpu_custom_call" | custom-call | tf_op jit(solution)/shard_map/project/pallas_call | solution.py:502
  39.2 11.1 %all_to_all.16 = bf16[8,16,1024]{2,1,0:T(8,128)(2,1)S(1)} all-to-all(bf16[8,16,1024]{2,1,0:T(8,128)(2,1)S(1)} %project.1), channel_id=1, replica_groups=mesh['inst'=16,'tp'=8] {'tp'}, dimensions={0} | all-to-all | bytes 524288 | tf_op jit(solution)/shard_map/all_to_all | solution.py:515
  50.4 0.6 %reshape.11 = bf16[4,4,1024]{2,1,0:T(4,128)(2,1)} reshape(bf16[16,1024]{1,0:T(8,128)(2,1)S(1)} %reduce_sum.12) | data formatting | bytes 65536 | tf_op jit(solution)/shard_map/reshape | solution.py:517
  (1 shorter events, 0.0 us)
Async XLA Ops:
  1.9 18.1 %all-to-all-start = ((bf16[16,72,128]{2,1,0:T(8,128)(2,1)}), bf16[16,72,128]{2,1,0:T(8,128)(2,1)S(1)}, u32[]{:S(2)}, u32[]{:S(2)}) async-start(bf16[16,72,128]{2,1,0:T(8,128)(2,1)} %get-tuple-element.17), calls=%async_computation | async-start | bytes 589824 | tf_op jit(solution)/shard_map/all_to_all | solution.py:455
  10.1 0.8 %copy-start = (bf16[4,48,128]{2,1,0:T(8,128)(2,1)S(1)}, bf16[4,48,128]{2,1,0:T(8,128)(2,1)}, u32[]{:S(2)}) copy-start(bf16[4,48,128]{2,1,0:T(8,128)(2,1)} %get-tuple-element.14.q_ref) | copy-start | bytes 147460

commit v10 on v9

--- a/solution.py
+++ b/solution.py
@@ -13,6 +13,7 @@
 TILE = 256
 FRESH = 8
 PLAN_ROW = 4
+PACK = 4
 LENGTH_BASE = 64
 
 VMEM = pl.BlockSpec(memory_space=pltpu.VMEM)
@@ -208,13 +209,16 @@
         held_copy.start()
         copies.append(held_copy)
         lane = lax.broadcasted_iota(jnp.int32, place_ref.shape, 1)
-        places = jnp.zeros(place_ref.shape, jnp.int32)
+        places = [0] * (entries // PACK)
         for e in range(entries):
             dest = jnp.clip(plan.dest[e], 0, n_inst - 1)
             rank = sum((plan.dest[f] == plan.dest[e]).astype(jnp.int32) for f in range(e))
             place = jnp.minimum(rank, CAP - 1) * n_inst + dest
-            places = jnp.where(lane == e, place, places)
-        place_ref[...] = places
+            places[e // PACK] += place << (8 * (e % PACK))
+        packed = jnp.zeros(place_ref.shape, jnp.int32)
+        for k, number in enumerate(places):
+            packed = jnp.where(lane == k, number, packed)
+        place_ref[...] = packed
         line = lax.broadcasted_iota(jnp.int32, slot_ref.shape, 0)
         arrival = line * (head // rows) + lax.broadcasted_iota(jnp.int32, slot_ref.shape, 1) // rows
         slot_of = jnp.full(slot_ref.shape, -1, jnp.int32)
@@ -252,8 +256,9 @@
     key = lane.astype(jnp.float32)
     places, starts, masks, scores = [], [], [], []
     across = place_ref[...]
+    packed = [across[0, k] for k in range(entries // PACK)]
     for e in range(entries):
-        place = across[0, e]
+        place = (packed[e // PACK] >> (8 * (e % PACK))) & 127
         dest = lax.rem(place, n_inst)
         rank = lax.div(place, n_inst)
         start = pl.multiple_of(rank * rows, rows)

time: 51.4 us -> 51.4 us (level)
  no operation moved by 1% of the time
where the time goes in v10:
time: 51.4 us; the launch traced here: 51 us
  blocking collectives  23.6 us (46%)
  Pallas kernels  12.8 us (25%)
  starting transfers between devices  8.14 us (16%)
  waiting for transfers between devices  4.87 us (9%)
  local copies, waits for them, and re-layouts  1.43 us (3%)
    all_to_all x1, blocking collectives, shards(): back = lax.all_to_all(answer, 'inst', 0, 0, tiled=True)  12.5 us
    all_to_all x1, blocking collectives, shards(): shares = lax.all_to_all(partial_out, 'tp', 0, 0, tiled=True)  11.1 us
    all_to_all x1, starting transfers between devices, shards(): asked = lax.all_to_all(ask, 'inst', 0, 0, tiled=True)  8.14 us
    pallas_call x1, Pallas kernels, shards(): pl.pallas_call(project_kernel, out_shape=shape((n_tp, out_rows, part_cols...  5.93 us
    all_to_all x1, waiting for transfers between devices, shards(): asked = lax.all_to_all(ask, 'inst', 0, 0, tiled=True)  4.87 us
    pallas_call x1, Pallas kernels, shards(): pl.pallas_call(functools.partial(bring_kernel, scale, group, blocks, step...  4.23 us
    pallas_call x1, Pallas kernels, shards(): pl.pallas_call(functools.partial(ask_kernel, pool_size, block_len), out_s...  1.93 us
  transfers between devices with their start and end apart: 1, of which 1 were waited for; matrix products, arithmetic and copies ran while one was open for 0% of the time, Pallas kernels for 8%

profile of v10, /device:TPU:0, one launch (start us, length us, event | category | flops | bytes accessed | tf_op | source)
XLA Modules:
  0.0 51.0 jit_solution(16276234700982835292)
XLA Ops:
  0.0 1.9 %ask.1 = (bf16[16,72,128]{2,1,0:T(8,128)(2,1)}, bf16[4,48,128]{2,1,0:T(8,128)(2,1)}) custom-call(s32[4,16]{1,0:T(4,128)} %table_hbm.1, s32[4]{0:T(128)} %len_hbm.1, s32[16]{0:T(128)} %block_hbm.1, s32[16]{0:T(128)} %dest_hbm.1, bf16[4,4,1024]{2,1,0:T(4,128)(2,1)} %q_hbm.1, bf16[4,4,256]{2,1,0:T(4,128)(2,1)} %bitcast.3), custom_call_target="tpu_custom_call" | custom-call | tf_op jit(solution)/shard_map/ask/pallas_call | solution.py:437
  1.9 8.1 %all-to-all-start = ((bf16[16,72,128]{2,1,0:T(8,128)(2,1)}), bf16[16,72,128]{2,1,0:T(8,128)(2,1)S(1)}, u32[]{:S(2)}, u32[]{:S(2)}) async-start(bf16[16,72,128]{2,1,0:T(8,128)(2,1)} %get-tuple-element.17), calls=%async_computation | async-start | bytes 589824 | tf_op jit(solution)/shard_map/all_to_all | solution.py:460
  10.1 0.0 copy-start
  10.1 0.8 %copy-done = bf16[4,48,128]{2,1,0:T(8,128)(2,1)S(1)} copy-done((bf16[4,48,128]{2,1,0:T(8,128)(2,1)S(1)}, bf16[4,48,128]{2,1,0:T(8,128)(2,1)}, u32[]{:S(2)}) %copy-start) | copy-done | bytes 49176
  10.9 4.2 %own.1 = (f32[4,8,128]{2,1,0:T(8,128)S(1)}, f32[4,8,128]{2,1,0:T(8,128)S(1)}, f32[4,32,128]{2,1,0:T(8,128)S(1)}, bf16[16,128,256]{2,1,0:T(8,128)(2,1)S(1)}, bf16...) custom-call(bf16[4,48,128]{2,1,0:T(8,128)(2,1)S(1)} %copy-done, ...), custom_call_target="tpu_custom_call" | custom-call | flops 268435456 | bytes 16777216 | tf_op jit(solution)/shard_map/own/pallas_call | solution.py:465
  15.1 4.9 %all-to-all-done.asked_ref = bf16[16,72,128]{2,1,0:T(8,128)(2,1)S(1)} async-done(((bf16[16,72,128]{2,1,0:T(8,128)(2,1)}), bf16[16,72,128]{2,1,0:T(8,128)(2,1)S(1)}, u32[]{:S(2)}, u32[]{:S(2)}) %all-to-all-start) | async-done | bytes 294944 | tf_op jit(solution)/shard_map/all_to_all | solution.py:460
  20.0 0.7 %answer.1 = bf16[16,72,128]{2,1,0:T(8,128)(2,1)S(1)} custom-call(s32[8,128]{1,0:T(8,128)S(1)} %get-tuple-element.16.place_ref, bf16[16,72,128]{2,1,0:T(8,128)(2,1)S(1)} %all-to-all-done.asked_ref, bf16[16,128,256]{2,1,0:T(8,128)(2,1)S(1)} %get-tuple-element.18.sent_ref), custom_call_target="tpu_custom_call" | custom-call | tf_op jit(solution)/shard_map/answer/pallas_call | solution.py:492
  20.7 12.5 %all_to_all.15.back_ref = bf16[16,72,128]{2,1,0:T(8,128)(2,1)S(1)} all-to-all(bf16[16,72,128]{2,1,0:T(8,128)(2,1)S(1)} %answer.1), channel_id=1, replica_groups=mesh['inst'=16,'tp'=8] {'inst'}, dimensions={0} | all-to-all | bytes 589824 | tf_op jit(solution)/shard_map/all_to_all | solution.py:504
  33.2 5.9 %project.1 = bf16[8,16,1024]{2,1,0:T(8,128)(2,1)S(1)} custom-call(s32[8,128]{1,0:T(8,128)S(1)} %get-tuple-element.15.slot_ref, bf16[16,72,128]{2,1,0:T(8,128)(2,1)S(1)} %all_to_all.15.back_ref, f32[4,8,128]{2,1,0:T(8,128)S(1)} %get-tuple-element.19.peak_ref, f32[4,8,128]{2,1,0:T(8,128)S(1)} %get-tuple-element.20.sum_ref, ...), custom_call_target="tpu_custom_call" | custom-call | tf_op jit(solution)/shard_map/project/pallas_call | solution.py:507
  39.1 11.1 %all_to_all.16 = bf16[8,16,1024]{2,1,0:T(8,128)(2,1)S(1)} all-to-all(bf16[8,16,1024]{2,1,0:T(8,128)(2,1)S(1)} %project.1), channel_id=1, replica_groups=mesh['inst'=16,'tp'=8] {'tp'}, dimensions={0} | all-to-all | bytes 524288 | tf_op jit(solution)/shard_map/all_to_all | solution.py:520
  50.3 0.6 %reshape.11 = bf16[4,4,1024]{2,1,0:T(4,128)(2,1)} reshape(bf16[16,1024]{1,0:T(8,128)(2,1)S(1)} %reduce_sum.12) | data formatting | bytes 65536 | tf_op jit(solution)/shard_map/reshape | solution.py:522
  (1 shorter events, 0.0 us)
Async XLA Ops:
  1.9 18.1 %all-to-all-start = ((bf16[16,72,128]{2,1,0:T(8,128)(2,1)}), bf16[16,72,128]{2,1,0:T(8,128)(2,1)S(1)}, u32[]{:S(2)}, u32[]{:S(2)}) async-start(bf16[16,72,128]{2,1,0:T(8,128)(2,1)} %get-tuple-element.17), calls=%async_computation | async-start | bytes 589824 | tf_op jit(solution)/shard_map/all_to_all | solution.py:460
  10.1 0.8 %copy-start = (bf16[4,48,128]{2,1,0:T(8,128)(2,1)S(1)}, bf16[4,48,128]{2,1,0:T(8,128)(2,1)}, u32[]{:S(2)}) copy-start(bf16[4,48,128]{2,1,0:T(8,128)(2,1)} %get-tuple-element.14.q_ref) | copy-start | bytes 147460

commit v11 on v10

--- a/solution.py
+++ b/solution.py
@@ -14,6 +14,7 @@
 FRESH = 8
 PLAN_ROW = 4
 PACK = 4
+CHUNKS = 2
 LENGTH_BASE = 64
 
 VMEM = pl.BlockSpec(memory_space=pltpu.VMEM)
@@ -321,16 +322,17 @@
     held = held_ref.shape[1]
     steps = out_rows // slots
     group = rows // steps
-    ahead = held // part_cols
+    chunk = part_cols // CHUNKS
+    ahead = held // chunk
 
     def copy(c):
         return pltpu.make_async_copy(
-            weight_ref.at[:, pl.ds(pl.multiple_of(c * part_cols, part_cols), part_cols)],
-            w_ref.at[:, pl.ds(pl.multiple_of((c - ahead) * part_cols, part_cols), part_cols)],
+            weight_ref.at[:, pl.ds(pl.multiple_of(c * chunk, chunk), chunk)],
+            w_ref.at[:, pl.ds(pl.multiple_of((c - ahead) * chunk, chunk), chunk)],
             sems.at[c],
         )
 
-    for c in range(ahead, parts):
+    for c in range(ahead, parts * CHUNKS):
         copy(c).start()
     across = head // rows
     slot_of = slot_ref[...]
@@ -389,26 +391,24 @@
                 att_ref[to : to + 1, g * head : (g + 1) * head] = done[at : at + 1]
     attended = att_ref[...].astype(jnp.bfloat16)
 
-    def multiply(c, source, start):
-        def tile(k, carry):
-            at = pl.multiple_of(k * TILE, TILE)
-            weight = source[:, pl.ds(pl.multiple_of(start + at, TILE), TILE)]
-            out_ref[c, :, pl.ds(at, TILE)] = jnp.dot(
+    def multiply(part, at, source, start):
+        for low in range(0, chunk, TILE):
+            weight = source[:, pl.ds(pl.multiple_of(start + low, TILE), TILE)]
+            out_ref[part, :, pl.ds(pl.multiple_of(at + low, TILE), TILE)] = jnp.dot(
                 attended, weight, preferred_element_type=jnp.float32
             ).astype(jnp.bfloat16)
-            return carry
-
-        lax.fori_loop(0, part_cols // TILE, tile, 0, unroll=True)
 
     for c in range(ahead):
-        multiply(c, held_ref, c * part_cols)
-
-    def part(c, carry):
-        copy(c).wait()
-        multiply(c, w_ref, (c - ahead) * part_cols)
+        multiply(c // CHUNKS, c % CHUNKS * chunk, held_ref, c * chunk)
+
+    def part(p, carry):
+        for k in range(CHUNKS):
+            c = p * CHUNKS + k
+            copy(c).wait()
+            multiply(p, k * chunk, w_ref, (c - ahead) * chunk)
         return carry
 
-    lax.fori_loop(ahead, parts, part, 0)
+    lax.fori_loop(held // part_cols, parts, part, 0)
 
 
 def params(mib):
@@ -512,7 +512,7 @@
         scratch_shapes=[
             pltpu.VMEM((out_rows, head_width), f32),
             pltpu.VMEM((head_width, columns - ahead), bf16),
-            pltpu.SemaphoreType.DMA((n_tp,)),
+            pltpu.SemaphoreType.DMA((n_tp * CHUNKS,)),
         ],
         compiler_params=params(44),
         name="project",

time: 51.4 us -> 51.8 us (level)
  no operation moved by 1% of the time
where the time goes in v11:
time: 51.8 us; the launch traced here: 51.4 us
  blocking collectives  23.6 us (46%)
  Pallas kernels  13.3 us (26%)
  starting transfers between devices  8.14 us (16%)
  waiting for transfers between devices  4.81 us (9%)
  local copies, waits for them, and re-layouts  1.43 us (3%)
    all_to_all x1, blocking collectives, shards(): back = lax.all_to_all(answer, 'inst', 0, 0, tiled=True)  12.5 us
    all_to_all x1, blocking collectives, shards(): shares = lax.all_to_all(partial_out, 'tp', 0, 0, tiled=True)  11.1 us
    all_to_all x1, starting transfers between devices, shards(): asked = lax.all_to_all(ask, 'inst', 0, 0, tiled=True)  8.14 us
    pallas_call x1, Pallas kernels, shards(): pl.pallas_call(project_kernel, out_shape=shape((n_tp, out_rows, part_cols...  6.4 us
    all_to_all x1, waiting for transfers between devices, shards(): asked = lax.all_to_all(ask, 'inst', 0, 0, tiled=True)  4.81 us
    pallas_call x1, Pallas kernels, shards(): pl.pallas_call(functools.partial(bring_kernel, scale, group, blocks, step...  4.29 us
    pallas_call x1, Pallas kernels, shards(): pl.pallas_call(functools.partial(ask_kernel, pool_size, block_len), out_s...  1.93 us
  transfers between devices with their start and end apart: 1, of which 1 were waited for; matrix products, arithmetic and copies ran while one was open for 0% of the time, Pallas kernels for 8%

profile of v11, /device:TPU:0, one launch (start us, length us, event | category | flops | bytes accessed | tf_op | source)
XLA Modules:
  0.0 51.4 jit_solution(14726078189434905759)
XLA Ops:
  0.0 1.9 %ask.1 = (bf16[16,72,128]{2,1,0:T(8,128)(2,1)}, bf16[4,48,128]{2,1,0:T(8,128)(2,1)}) custom-call(s32[4,16]{1,0:T(4,128)} %table_hbm.1, s32[4]{0:T(128)} %len_hbm.1, s32[16]{0:T(128)} %block_hbm.1, s32[16]{0:T(128)} %dest_hbm.1, bf16[4,4,1024]{2,1,0:T(4,128)(2,1)} %q_hbm.1, bf16[4,4,256]{2,1,0:T(4,128)(2,1)} %bitcast.3), custom_call_target="tpu_custom_call" | custom-call | tf_op jit(solution)/shard_map/ask/pallas_call | solution.py:437
  1.9 8.1 %all-to-all-start = ((bf16[16,72,128]{2,1,0:T(8,128)(2,1)}), bf16[16,72,128]{2,1,0:T(8,128)(2,1)S(1)}, u32[]{:S(2)}, u32[]{:S(2)}) async-start(bf16[16,72,128]{2,1,0:T(8,128)(2,1)} %get-tuple-element.17), calls=%async_computation | async-start | bytes 589824 | tf_op jit(solution)/shard_map/all_to_all | solution.py:460
  10.1 0.0 copy-start
  10.1 0.8 %copy-done = bf16[4,48,128]{2,1,0:T(8,128)(2,1)S(1)} copy-done((bf16[4,48,128]{2,1,0:T(8,128)(2,1)S(1)}, bf16[4,48,128]{2,1,0:T(8,128)(2,1)}, u32[]{:S(2)}) %copy-start) | copy-done | bytes 49176
  10.9 4.3 %own.1 = (f32[4,8,128]{2,1,0:T(8,128)S(1)}, f32[4,8,128]{2,1,0:T(8,128)S(1)}, f32[4,32,128]{2,1,0:T(8,128)S(1)}, bf16[16,128,256]{2,1,0:T(8,128)(2,1)S(1)}, bf16...) custom-call(bf16[4,48,128]{2,1,0:T(8,128)(2,1)S(1)} %copy-done, ...), custom_call_target="tpu_custom_call" | custom-call | flops 268435456 | bytes 16777216 | tf_op jit(solution)/shard_map/own/pallas_call | solution.py:465
  15.2 4.8 %all-to-all-done.asked_ref = bf16[16,72,128]{2,1,0:T(8,128)(2,1)S(1)} async-done(((bf16[16,72,128]{2,1,0:T(8,128)(2,1)}), bf16[16,72,128]{2,1,0:T(8,128)(2,1)S(1)}, u32[]{:S(2)}, u32[]{:S(2)}) %all-to-all-start) | async-done | bytes 294944 | tf_op jit(solution)/shard_map/all_to_all | solution.py:460
  20.0 0.7 %answer.1 = bf16[16,72,128]{2,1,0:T(8,128)(2,1)S(1)} custom-call(s32[8,128]{1,0:T(8,128)S(1)} %get-tuple-element.16.place_ref, bf16[16,72,128]{2,1,0:T(8,128)(2,1)S(1)} %all-to-all-done.asked_ref, bf16[16,128,256]{2,1,0:T(8,128)(2,1)S(1)} %get-tuple-element.18.sent_ref), custom_call_target="tpu_custom_call" | custom-call | tf_op jit(solution)/shard_map/answer/pallas_call | solution.py:492
  20.7 12.5 %all_to_all.15.back_ref = bf16[16,72,128]{2,1,0:T(8,128)(2,1)S(1)} all-to-all(bf16[16,72,128]{2,1,0:T(8,128)(2,1)S(1)} %answer.1), channel_id=1, replica_groups=mesh['inst'=16,'tp'=8] {'inst'}, dimensions={0} | all-to-all | bytes 589824 | tf_op jit(solution)/shard_map/all_to_all | solution.py:504
  33.2 6.4 %project.1 = bf16[8,16,1024]{2,1,0:T(8,128)(2,1)S(1)} custom-call(s32[8,128]{1,0:T(8,128)S(1)} %get-tuple-element.15.slot_ref, bf16[16,72,128]{2,1,0:T(8,128)(2,1)S(1)} %all_to_all.15.back_ref, f32[4,8,128]{2,1,0:T(8,128)S(1)} %get-tuple-element.19.peak_ref, f32[4,8,128]{2,1,0:T(8,128)S(1)} %get-tuple-element.20.sum_ref, ...), custom_call_target="tpu_custom_call" | custom-call | tf_op jit(solution)/shard_map/project/pallas_call | solution.py:507
  39.6 11.1 %all_to_all.16 = bf16[8,16,1024]{2,1,0:T(8,128)(2,1)S(1)} all-to-all(bf16[8,16,1024]{2,1,0:T(8,128)(2,1)S(1)} %project.1), channel_id=1, replica_groups=mesh['inst'=16,'tp'=8] {'tp'}, dimensions={0} | all-to-all | bytes 524288 | tf_op jit(solution)/shard_map/all_to_all | solution.py:520
  50.8 0.6 %reshape.11 = bf16[4,4,1024]{2,1,0:T(4,128)(2,1)} reshape(bf16[16,1024]{1,0:T(8,128)(2,1)S(1)} %reduce_sum.12) | data formatting | bytes 65536 | tf_op jit(solution)/shard_map/reshape | solution.py:522
  (1 shorter events, 0.0 us)
Async XLA Ops:
  1.9 18.1 %all-to-all-start = ((bf16[16,72,128]{2,1,0:T(8,128)(2,1)}), bf16[16,72,128]{2,1,0:T(8,128)(2,1)S(1)}, u32[]{:S(2)}, u32[]{:S(2)}) async-start(bf16[16,72,128]{2,1,0:T(8,128)(2,1)} %get-tuple-element.17), calls=%async_computation | async-start | bytes 589824 | tf_op jit(solution)/shard_map/all_to_all | solution.py:460
  10.1 0.8 %copy-start = (bf16[4,48,128]{2,1,0:T(8,128)(2,1)S(1)}, bf16[4,48,128]{2,1,0:T(8,128)(2,1)}, u32[]{:S(2)}) copy-start(bf16[4,48,128]{2,1,0:T(8,128)(2,1)} %get-tuple-element.14.q_ref) | copy-start | bytes 147460

commit v12 on v10

--- a/solution.py
+++ b/solution.py
@@ -10,7 +10,7 @@
 CAP = 2
 INFO = 8
 MASKED = -1e30
-TILE = 256
+TILE = 1024
 FRESH = 8
 PLAN_ROW = 4
 PACK = 4

time: 51.4 us -> 51.4 us (level)
  no operation moved by 1% of the time
where the time goes in v12:
time: 51.4 us; the launch traced here: 51 us
  blocking collectives  23.6 us (46%)
  Pallas kernels  12.8 us (25%)
  starting transfers between devices  8.14 us (16%)
  waiting for transfers between devices  4.84 us (9%)
  local copies, waits for them, and re-layouts  1.43 us (3%)
    all_to_all x1, blocking collectives, shards(): back = lax.all_to_all(answer, 'inst', 0, 0, tiled=True)  12.5 us
    all_to_all x1, blocking collectives, shards(): shares = lax.all_to_all(partial_out, 'tp', 0, 0, tiled=True)  11.1 us
    all_to_all x1, starting transfers between devices, shards(): asked = lax.all_to_all(ask, 'inst', 0, 0, tiled=True)  8.14 us
    pallas_call x1, Pallas kernels, shards(): pl.pallas_call(project_kernel, out_shape=shape((n_tp, out_rows, part_cols...  5.92 us
    all_to_all x1, waiting for transfers between devices, shards(): asked = lax.all_to_all(ask, 'inst', 0, 0, tiled=True)  4.84 us
    pallas_call x1, Pallas kernels, shards(): pl.pallas_call(functools.partial(bring_kernel, scale, group, blocks, step...  4.26 us
    pallas_call x1, Pallas kernels, shards(): pl.pallas_call(functools.partial(ask_kernel, pool_size, block_len), out_s...  1.93 us
  transfers between devices with their start and end apart: 1, of which 1 were waited for; matrix products, arithmetic and copies ran while one was open for 0% of the time, Pallas kernels for 8%

profile of v12, /device:TPU:0, one launch (start us, length us, event | category | flops | bytes accessed | tf_op | source)
XLA Modules:
  0.0 51.0 jit_solution(1305996393095625330)
XLA Ops:
  0.0 1.9 %ask.1 = (bf16[16,72,128]{2,1,0:T(8,128)(2,1)}, bf16[4,48,128]{2,1,0:T(8,128)(2,1)}) custom-call(s32[4,16]{1,0:T(4,128)} %table_hbm.1, s32[4]{0:T(128)} %len_hbm.1, s32[16]{0:T(128)} %block_hbm.1, s32[16]{0:T(128)} %dest_hbm.1, bf16[4,4,1024]{2,1,0:T(4,128)(2,1)} %q_hbm.1, bf16[4,4,256]{2,1,0:T(4,128)(2,1)} %bitcast.3), custom_call_target="tpu_custom_call" | custom-call | tf_op jit(solution)/shard_map/ask/pallas_call | solution.py:437
  1.9 8.1 %all-to-all-start = ((bf16[16,72,128]{2,1,0:T(8,128)(2,1)}), bf16[16,72,128]{2,1,0:T(8,128)(2,1)S(1)}, u32[]{:S(2)}, u32[]{:S(2)}) async-start(bf16[16,72,128]{2,1,0:T(8,128)(2,1)} %get-tuple-element.17), calls=%async_computation | async-start | bytes 589824 | tf_op jit(solution)/shard_map/all_to_all | solution.py:460
  10.1 0.0 copy-start
  10.1 0.8 %copy-done = bf16[4,48,128]{2,1,0:T(8,128)(2,1)S(1)} copy-done((bf16[4,48,128]{2,1,0:T(8,128)(2,1)S(1)}, bf16[4,48,128]{2,1,0:T(8,128)(2,1)}, u32[]{:S(2)}) %copy-start) | copy-done | bytes 49176
  10.9 4.3 %own.1 = (f32[4,8,128]{2,1,0:T(8,128)S(1)}, f32[4,8,128]{2,1,0:T(8,128)S(1)}, f32[4,32,128]{2,1,0:T(8,128)S(1)}, bf16[16,128,256]{2,1,0:T(8,128)(2,1)S(1)}, bf16...) custom-call(bf16[4,48,128]{2,1,0:T(8,128)(2,1)S(1)} %copy-done, ...), custom_call_target="tpu_custom_call" | custom-call | flops 268435456 | bytes 16777216 | tf_op jit(solution)/shard_map/own/pallas_call | solution.py:465
  15.2 4.8 %all-to-all-done.asked_ref = bf16[16,72,128]{2,1,0:T(8,128)(2,1)S(1)} async-done(((bf16[16,72,128]{2,1,0:T(8,128)(2,1)}), bf16[16,72,128]{2,1,0:T(8,128)(2,1)S(1)}, u32[]{:S(2)}, u32[]{:S(2)}) %all-to-all-start) | async-done | bytes 294944 | tf_op jit(solution)/shard_map/all_to_all | solution.py:460
  20.0 0.7 %answer.1 = bf16[16,72,128]{2,1,0:T(8,128)(2,1)S(1)} custom-call(s32[8,128]{1,0:T(8,128)S(1)} %get-tuple-element.16.place_ref, bf16[16,72,128]{2,1,0:T(8,128)(2,1)S(1)} %all-to-all-done.asked_ref, bf16[16,128,256]{2,1,0:T(8,128)(2,1)S(1)} %get-tuple-element.18.sent_ref), custom_call_target="tpu_custom_call" | custom-call | tf_op jit(solution)/shard_map/answer/pallas_call | solution.py:492
  20.7 12.5 %all_to_all.15.back_ref = bf16[16,72,128]{2,1,0:T(8,128)(2,1)S(1)} all-to-all(bf16[16,72,128]{2,1,0:T(8,128)(2,1)S(1)} %answer.1), channel_id=1, replica_groups=mesh['inst'=16,'tp'=8] {'inst'}, dimensions={0} | all-to-all | bytes 589824 | tf_op jit(solution)/shard_map/all_to_all | solution.py:504
  33.2 5.9 %project.1 = bf16[8,16,1024]{2,1,0:T(8,128)(2,1)S(1)} custom-call(s32[8,128]{1,0:T(8,128)S(1)} %get-tuple-element.15.slot_ref, bf16[16,72,128]{2,1,0:T(8,128)(2,1)S(1)} %all_to_all.15.back_ref, f32[4,8,128]{2,1,0:T(8,128)S(1)} %get-tuple-element.19.peak_ref, f32[4,8,128]{2,1,0:T(8,128)S(1)} %get-tuple-element.20.sum_ref, ...), custom_call_target="tpu_custom_call" | custom-call | tf_op jit(solution)/shard_map/project/pallas_call | solution.py:507
  39.1 11.1 %all_to_all.16 = bf16[8,16,1024]{2,1,0:T(8,128)(2,1)S(1)} all-to-all(bf16[8,16,1024]{2,1,0:T(8,128)(2,1)S(1)} %project.1), channel_id=1, replica_groups=mesh['inst'=16,'tp'=8] {'tp'}, dimensions={0} | all-to-all | bytes 524288 | tf_op jit(solution)/shard_map/all_to_all | solution.py:520
  50.3 0.6 %reshape.11 = bf16[4,4,1024]{2,1,0:T(4,128)(2,1)} reshape(bf16[16,1024]{1,0:T(8,128)(2,1)S(1)} %reduce_sum.12) | data formatting | bytes 65536 | tf_op jit(solution)/shard_map/reshape | solution.py:522
  (1 shorter events, 0.0 us)
Async XLA Ops:
  1.9 18.1 %all-to-all-start = ((bf16[16,72,128]{2,1,0:T(8,128)(2,1)}), bf16[16,72,128]{2,1,0:T(8,128)(2,1)S(1)}, u32[]{:S(2)}, u32[]{:S(2)}) async-start(bf16[16,72,128]{2,1,0:T(8,128)(2,1)} %get-tuple-element.17), calls=%async_computation | async-start | bytes 589824 | tf_op jit(solution)/shard_map/all_to_all | solution.py:460
  10.1 0.8 %copy-start = (bf16[4,48,128]{2,1,0:T(8,128)(2,1)S(1)}, bf16[4,48,128]{2,1,0:T(8,128)(2,1)}, u32[]{:S(2)}) copy-start(bf16[4,48,128]{2,1,0:T(8,128)(2,1)} %get-tuple-element.14.q_ref) | copy-start | bytes 147460
